TPU v7x, 32 devices: a whole 2x2x4 slice. The times are simulated.
32 devices in a mesh: dp: 8 (over y, x, core), tensor: 4 (over z).
Axes of the slice: x: 2, y: 2, z: 4, core: 2. Of those that a mesh axis runs over, the one named last changes fastest.
Arguments:
- layer_in: bfloat16 [8192, 2304], P(('dp', 'tensor')), may hold values from -6 to 6
- out_grad: bfloat16 [8192, 2304], P(('dp', 'tensor')), may hold values from -6 to 6
- piece_starts: int32 [8, 2], P('dp'), may hold values from 0 to 768, as said below
- attn_gain: bfloat16 [2304], P('dp'), may hold values from -0.3984375 to 0.3984375
- attn_out_gain: bfloat16 [2304], P('dp'), may hold values from -0.3984375 to 0.3984375
- feed_gain: bfloat16 [2304], P('dp'), may hold values from -0.3984375 to 0.3984375
- feed_out_gain: bfloat16 [2304], P('dp'), may hold values from -0.3984375 to 0.3984375
- query_weight: bfloat16 [2304, 2048], P('dp', 'tensor'), may hold values from -2 to 2
- key_weight: bfloat16 [2304, 1024], P('dp'), may hold values from -2 to 2
- value_weight: bfloat16 [2304, 1024], P('dp'), may hold values from -0.125 to 0.125
- out_weight: bfloat16 [2048, 2304], P('tensor', 'dp'), may hold values from -0.75 to 0.75
- gate_weight: bfloat16 [2304, 9216], P('dp', 'tensor'), may hold values from -0.125 to 0.125
- up_weight: bfloat16 [2304, 9216], P('dp', 'tensor'), may hold values from -0.125 to 0.125
- down_weight: bfloat16 [9216, 2304], P('tensor', 'dp'), may hold values from -0.0625 to 0.0625
Outputs:
- layer_out: bfloat16 [8192, 2304], P(('dp', 'tensor'))
- in_grad: bfloat16 [8192, 2304], P(('dp', 'tensor'))
- grad_query_weight: float32 [2304, 2048], P('dp', 'tensor')
- grad_key_weight: float32 [2304, 1024], P('dp')
- grad_value_weight: float32 [2304, 1024], P('dp')
- grad_out_weight: float32 [2048, 2304], P('tensor', 'dp')
- grad_gate_weight: float32 [2304, 9216], P('dp', 'tensor')
- grad_up_weight: float32 [2304, 9216], P('dp', 'tensor')
- grad_down_weight: float32 [9216, 2304], P('tensor', 'dp')
- grad_attn_gain: float32 [2304], P('dp')
- grad_attn_out_gain: float32 [2304], P('dp')
- grad_feed_gain: float32 [2304], P('dp')
- grad_feed_out_gain: float32 [2304], P('dp')
Inputs may be any that keep to these rules, and one draw needn't show every extreme that they name: `piece_starts`: each sequence has 2 picture pieces of 256 tokens: the first starts in the sequence's first half and the second in its second half, so they never intersect and each lies inside the sequence.
All inputs are finite; a program needn't handle non-finite values.
Results may differ from a plain program's by a relative error of at most 0.024.
Values may be sent and summed in bfloat16 or wider, within the bound.
A program may use at most 256 MiB of HBM per device.

v0:
```python
from functools import partial

import jax
import jax.numpy as jnp
from jax import lax
from jax.sharding import PartitionSpec as P

H = 8
KV = 4
HD = 256
L = 1024
PIECE = 256


norm_epsilon = 1e-06
logit_cap = 50.0


def rms_scale(values, gain):
    inverse = lax.rsqrt(jnp.mean(values * values, axis=-1, keepdims=True) + norm_epsilon)
    return values * inverse * (1.0 + gain)


def rotate(values, cosine_table, sine_table):
    half_size = values.shape[-1] // 2
    turned = jnp.concatenate([-values[..., half_size:], values[..., :half_size]], axis=-1)
    return values * cosine_table + turned * sine_table


def rope_tables(token_count, seq_len, head_size):
    positions = (jnp.arange(token_count, dtype=jnp.int32) % jnp.int32(seq_len)).astype(jnp.float32)
    exponent = jnp.arange(head_size // 2, dtype=jnp.int32).astype(jnp.float32) * (-2.0 / head_size)
    frequency = jnp.exp(exponent * jnp.log(jnp.float32(10000.0)))
    angles = positions[:, None] * frequency[None, :]
    angles = jnp.concatenate([angles, angles], axis=-1)[:, None, :]
    return (jnp.cos(angles), jnp.sin(angles))


def visible_block(starts, block_start, block_rows, seq_len):
    query_pos = jnp.int32(block_start) + jnp.arange(block_rows, dtype=jnp.int32)
    key_pos = jnp.arange(seq_len, dtype=jnp.int32)
    allowed = key_pos[None, :] <= query_pos[:, None]
    for piece_index in range(starts.shape[0]):
        begin = starts[piece_index]
        finish = begin + jnp.int32(PIECE)
        inside_query = (query_pos >= begin) & (query_pos < finish)
        inside_key = (key_pos >= begin) & (key_pos < finish)
        allowed = allowed | inside_query[:, None] & inside_key[None, :]
    return allowed


def capped_scores(query_block, key_seq, starts, block_start):
    scores = jnp.einsum("qhd,khd->hqk", query_block, key_seq, preferred_element_type=jnp.float32)
    tangent = jnp.tanh(scores / logit_cap)
    allowed = visible_block(starts, block_start, query_block.shape[0], key_seq.shape[0])
    capped_all = logit_cap * tangent
    capped = jnp.where(allowed[None], capped_all, jnp.full_like(capped_all, -1e30))
    return (capped, tangent)


def attend_forward(seq_items):
    query_seq, key_seq, value_seq, starts = seq_items
    seq_len = query_seq.shape[0]
    block_rows = min(512, seq_len)
    outputs = []
    totals = []
    for block_start in range(0, seq_len, block_rows):
        query_block = query_seq[block_start : block_start + block_rows]
        capped, tangent = capped_scores(query_block, key_seq, starts, block_start)
        largest = jnp.max(capped, axis=-1, keepdims=True)
        weights = jnp.exp(capped - largest)
        denominator = jnp.sum(weights, axis=-1, keepdims=True)
        softmax_low = (weights / denominator).astype(jnp.bfloat16)
        block_out = jnp.einsum(
            "hqk,khd->qhd", softmax_low, value_seq, preferred_element_type=jnp.float32
        )
        outputs.append(block_out.astype(jnp.bfloat16))
        totals.append((largest + jnp.log(denominator))[..., 0])
    return (jnp.concatenate(outputs, axis=0), jnp.concatenate(totals, axis=1))


def attend_backward(seq_items):
    query_seq, key_seq, value_seq, starts, totals, grad_seq = seq_items
    seq_len = query_seq.shape[0]
    block_rows = min(512, seq_len)
    grad_queries = []
    grad_keys = jnp.zeros(key_seq.shape, jnp.float32)
    grad_values = jnp.zeros(value_seq.shape, jnp.float32)
    for block_start in range(0, seq_len, block_rows):
        query_block = query_seq[block_start : block_start + block_rows]
        grad_block = grad_seq[block_start : block_start + block_rows]
        capped, tangent = capped_scores(query_block, key_seq, starts, block_start)
        softmax_full = jnp.exp(capped - totals[:, block_start : block_start + block_rows, None])
        softmax_low = softmax_full.astype(jnp.bfloat16)
        grad_probs = jnp.einsum(
            "qhd,khd->hqk", grad_block, value_seq, preferred_element_type=jnp.float32
        )
        inner_sum = jnp.sum(softmax_full * grad_probs, axis=-1, keepdims=True)
        grad_scores = (softmax_full * (grad_probs - inner_sum) * (1.0 - tangent * tangent)).astype(
            jnp.bfloat16
        )
        grad_queries.append(
            jnp.einsum("hqk,khd->qhd", grad_scores, key_seq, preferred_element_type=jnp.float32)
        )
        grad_keys = grad_keys + jnp.einsum(
            "hqk,qhd->khd", grad_scores, query_block, preferred_element_type=jnp.float32
        )
        grad_values = grad_values + jnp.einsum(
            "hqk,qhd->khd", softmax_low, grad_block, preferred_element_type=jnp.float32
        )
    return (jnp.concatenate(grad_queries, axis=0), grad_keys, grad_values)


def contract_rows(left_side, right_side):
    return lax.dot_general(
        left_side, right_side, (((0,), (0,)), ((), ())), preferred_element_type=jnp.float32
    )


def contract_cols(left_side, right_side):
    return lax.dot_general(
        left_side, right_side, (((1,), (1,)), ((), ())), preferred_element_type=jnp.float32
    )


def body(
    layer_in,
    out_grad,
    piece_starts,
    attn_gain,
    attn_out_gain,
    feed_gain,
    feed_out_gain,
    query_weight,
    key_weight,
    value_weight,
    out_weight,
    gate_weight,
    up_weight,
    down_weight,
):
    head_size = HD
    heads_here = query_weight.shape[1] // head_size
    per_group = H // KV
    kv_here = max(1, heads_here // per_group)
    fan_heads = heads_here // kv_here
    tensor_rank = lax.axis_index("tensor")
    kv_first = tensor_rank * heads_here // per_group
    (
        query_full,
        key_full,
        value_full,
        output_full,
        gate_full,
        up_full,
        down_full,
        gain_one,
        gain_two,
        gain_three,
        gain_four,
    ) = (
        lax.all_gather(query_weight, "dp", axis=0, tiled=True),
        lax.all_gather(key_weight, "dp", axis=0, tiled=True),
        lax.all_gather(value_weight, "dp", axis=0, tiled=True),
        lax.all_gather(out_weight, "dp", axis=1, tiled=True),
        lax.all_gather(gate_weight, "dp", axis=0, tiled=True),
        lax.all_gather(up_weight, "dp", axis=0, tiled=True),
        lax.all_gather(down_weight, "dp", axis=1, tiled=True),
        lax.all_gather(attn_gain, "dp", axis=0, tiled=True),
        lax.all_gather(attn_out_gain, "dp", axis=0, tiled=True),
        lax.all_gather(feed_gain, "dp", axis=0, tiled=True),
        lax.all_gather(feed_out_gain, "dp", axis=0, tiled=True),
    )
    gain_one = gain_one.astype(jnp.float32)
    gain_two = gain_two.astype(jnp.float32)
    gain_three = gain_three.astype(jnp.float32)
    gain_four = gain_four.astype(jnp.float32)
    key_cols = lax.dynamic_slice_in_dim(key_full, kv_first * head_size, kv_here * head_size, 1)
    value_cols = lax.dynamic_slice_in_dim(value_full, kv_first * head_size, kv_here * head_size, 1)
    width = key_cols.shape[0]
    inputs = layer_in.astype(jnp.float32)
    hidden_one = lax.all_gather(
        rms_scale(inputs, gain_one).astype(jnp.bfloat16), "tensor", axis=0, tiled=True
    )
    token_count = hidden_one.shape[0]
    seq_count = token_count // L
    cosine_table, sine_table = rope_tables(token_count, L, head_size)
    query_scale = head_size ** (-0.5)
    query_pre = jnp.dot(hidden_one, query_full, preferred_element_type=jnp.float32)
    key_pre = jnp.dot(hidden_one, key_cols, preferred_element_type=jnp.float32)
    value_heads = jnp.dot(hidden_one, value_cols, preferred_element_type=jnp.float32).astype(
        jnp.bfloat16
    )
    queries = (
        rotate(query_pre.reshape(token_count, heads_here, head_size), cosine_table, sine_table)
        * query_scale
    ).astype(jnp.bfloat16)
    key_heads = rotate(
        key_pre.reshape(token_count, kv_here, head_size), cosine_table, sine_table
    ).astype(jnp.bfloat16)
    value_heads = value_heads.reshape(token_count, kv_here, head_size)
    keys_wide = jnp.repeat(key_heads, fan_heads, axis=1)
    values_wide = jnp.repeat(value_heads, fan_heads, axis=1)
    seq_shape = (seq_count, L, heads_here, head_size)
    query_seqs = queries.reshape(seq_shape)
    key_seqs = keys_wide.reshape(seq_shape)
    value_seqs = values_wide.reshape(seq_shape)
    mixed_heads, totals = lax.map(attend_forward, (query_seqs, key_seqs, value_seqs, piece_starts))
    mixed_heads = mixed_heads.reshape(token_count, heads_here * head_size)
    attn_part = jnp.dot(mixed_heads, output_full, preferred_element_type=jnp.float32)
    attn_rows = lax.psum_scatter(attn_part, "tensor", scatter_dimension=0, tiled=True)
    resid = inputs + rms_scale(attn_rows, gain_two)
    hidden_three = lax.all_gather(
        rms_scale(resid, gain_three).astype(jnp.bfloat16), "tensor", axis=0, tiled=True
    )
    gate_value = jnp.dot(hidden_three, gate_full, preferred_element_type=jnp.float32)
    upward = jnp.dot(hidden_three, up_full, preferred_element_type=jnp.float32)
    activated = jax.nn.gelu(gate_value, approximate=True)
    product = (activated * upward).astype(jnp.bfloat16)
    feed_part = jnp.dot(product, down_full, preferred_element_type=jnp.float32)
    feed_rows = lax.psum_scatter(feed_part, "tensor", scatter_dimension=0, tiled=True)
    layer_out = (resid + rms_scale(feed_rows, gain_four)).astype(jnp.bfloat16)
    out_cot = out_grad.astype(jnp.float32)
    pull_four = jax.vjp(rms_scale, feed_rows, gain_four)[1]
    grad_feed_rows, grad_gain_four = pull_four(out_cot)
    grad_feed = lax.all_gather(grad_feed_rows.astype(jnp.bfloat16), "tensor", axis=0, tiled=True)
    grad_down = contract_rows(product, grad_feed)
    grad_product = contract_cols(grad_feed, down_full)
    gelu_pull = jax.vjp(partial(jax.nn.gelu, approximate=True), gate_value)[1]
    grad_gate = gelu_pull(grad_product * upward)[0].astype(jnp.bfloat16)
    grad_upward = (grad_product * activated).astype(jnp.bfloat16)
    grad_gate_w = contract_rows(hidden_three, grad_gate)
    grad_up_w = contract_rows(hidden_three, grad_upward)
    grad_mid = contract_cols(grad_gate, gate_full) + contract_cols(grad_upward, up_full)
    grad_mid_rows = lax.psum_scatter(grad_mid, "tensor", scatter_dimension=0, tiled=True)
    pull_three = jax.vjp(rms_scale, resid, gain_three)[1]
    grad_resid_add, grad_gain_three = pull_three(grad_mid_rows)
    grad_resid = out_cot + grad_resid_add
    pull_two = jax.vjp(rms_scale, attn_rows, gain_two)[1]
    grad_attn_rows, grad_gain_two = pull_two(grad_resid)
    grad_attn = lax.all_gather(grad_attn_rows.astype(jnp.bfloat16), "tensor", axis=0, tiled=True)
    grad_output_w = contract_rows(mixed_heads, grad_attn)
    grad_mixed = contract_cols(grad_attn, output_full).astype(jnp.bfloat16)
    grad_q, grad_k, grad_v = lax.map(
        attend_backward,
        (query_seqs, key_seqs, value_seqs, piece_starts, totals, grad_mixed.reshape(seq_shape)),
    )
    grad_q = grad_q.reshape(token_count, heads_here, head_size)
    grad_query_pre = (rotate(grad_q, cosine_table, -sine_table) * query_scale).astype(jnp.bfloat16)
    grad_query_pre = grad_query_pre.reshape(token_count, heads_here * head_size)
    grad_key_pre = (
        rotate(grad_k.reshape(token_count, heads_here, head_size), cosine_table, -sine_table)
        .astype(jnp.bfloat16)
        .reshape(token_count, heads_here * head_size)
    )
    grad_value_pre = grad_v.astype(jnp.bfloat16).reshape(token_count, heads_here * head_size)
    grad_query_w = contract_rows(hidden_one, grad_query_pre)
    grad_key_cols = (
        contract_rows(hidden_one, grad_key_pre)
        .reshape(width, kv_here, fan_heads, head_size)
        .sum(axis=2)
        .reshape(width, kv_here * head_size)
    )
    grad_value_cols = (
        contract_rows(hidden_one, grad_value_pre)
        .reshape(width, kv_here, fan_heads, head_size)
        .sum(axis=2)
        .reshape(width, kv_here * head_size)
    )
    key_spread = jnp.broadcast_to(
        key_cols.reshape(width, kv_here, 1, head_size), (width, kv_here, fan_heads, head_size)
    ).reshape(width, heads_here * head_size)
    value_spread = jnp.broadcast_to(
        value_cols.reshape(width, kv_here, 1, head_size), (width, kv_here, fan_heads, head_size)
    ).reshape(width, heads_here * head_size)
    grad_first = (
        contract_cols(grad_query_pre, query_full)
        + contract_cols(grad_key_pre, key_spread)
        + contract_cols(grad_value_pre, value_spread)
    )
    grad_first_rows = lax.psum_scatter(
        grad_first.astype(jnp.bfloat16), "tensor", scatter_dimension=0, tiled=True
    ).astype(jnp.float32)
    pull_one = jax.vjp(rms_scale, inputs, gain_one)[1]
    grad_in_add, grad_gain_one = pull_one(grad_first_rows)
    in_grad = (grad_resid + grad_in_add).astype(jnp.bfloat16)
    gain_grads = jnp.stack([grad_gain_one, grad_gain_two, grad_gain_three, grad_gain_four])
    (
        shard_query,
        shard_key,
        shard_value,
        shard_output,
        shard_gate,
        shard_up,
        shard_down,
        shard_gains,
    ) = (
        lax.psum_scatter(
            grad_query_w.astype(jnp.bfloat16), "dp", scatter_dimension=0, tiled=True
        ).astype(jnp.float32),
        lax.psum_scatter(
            grad_key_cols.astype(jnp.bfloat16), "dp", scatter_dimension=0, tiled=True
        ).astype(jnp.float32),
        lax.psum_scatter(
            grad_value_cols.astype(jnp.bfloat16), "dp", scatter_dimension=0, tiled=True
        ).astype(jnp.float32),
        lax.psum_scatter(
            grad_output_w.astype(jnp.bfloat16), "dp", scatter_dimension=1, tiled=True
        ).astype(jnp.float32),
        lax.psum_scatter(
            grad_gate_w.astype(jnp.bfloat16), "dp", scatter_dimension=0, tiled=True
        ).astype(jnp.float32),
        lax.psum_scatter(
            grad_up_w.astype(jnp.bfloat16), "dp", scatter_dimension=0, tiled=True
        ).astype(jnp.float32),
        lax.psum_scatter(
            grad_down.astype(jnp.bfloat16), "dp", scatter_dimension=1, tiled=True
        ).astype(jnp.float32),
        lax.psum_scatter(
            gain_grads.astype(jnp.bfloat16), "dp", scatter_dimension=1, tiled=True
        ).astype(jnp.float32),
    )
    rows_here = shard_key.shape[0]
    key_place = lax.dynamic_update_slice_in_dim(
        jnp.zeros((rows_here, KV * head_size), jnp.float32), shard_key, kv_first * head_size, 1
    )
    value_place = lax.dynamic_update_slice_in_dim(
        jnp.zeros((rows_here, KV * head_size), jnp.float32), shard_value, kv_first * head_size, 1
    )
    key_total, value_total, gain_total = (
        lax.psum(key_place.astype(jnp.bfloat16), "tensor").astype(jnp.float32),
        lax.psum(value_place.astype(jnp.bfloat16), "tensor").astype(jnp.float32),
        lax.psum(shard_gains.astype(jnp.bfloat16), "tensor").astype(jnp.float32),
    )
    return (
        layer_out,
        in_grad,
        shard_query,
        key_total,
        value_total,
        shard_output,
        shard_gate,
        shard_up,
        shard_down,
        gain_total[0],
        gain_total[1],
        gain_total[2],
        gain_total[3],
    )


def solution(mesh):
    in_specs = (
        P(("dp", "tensor"), None),
        P(("dp", "tensor"), None),
        P("dp", None),
        P("dp"),
        P("dp"),
        P("dp"),
        P("dp"),
        P("dp", "tensor"),
        P("dp", None),
        P("dp", None),
        P("tensor", "dp"),
        P("dp", "tensor"),
        P("dp", "tensor"),
        P("tensor", "dp"),
    )
    out_specs = (
        P(("dp", "tensor"), None),
        P(("dp", "tensor"), None),
        P("dp", "tensor"),
        P("dp", None),
        P("dp", None),
        P("tensor", "dp"),
        P("dp", "tensor"),
        P("dp", "tensor"),
        P("tensor", "dp"),
        P("dp"),
        P("dp"),
        P("dp"),
        P("dp"),
    )
    return jax.shard_map(body, mesh=mesh, in_specs=in_specs, out_specs=out_specs, check_vma=False)
```

profile of v0, /device:TPU:0, one launch (start us, length us, event | category | flops | bytes accessed | tf_op | source)
XLA Modules:
  0.0 2014.9 jit_solution(14185302190047932422)
XLA Ops:
  13.4 26.5 %all-reduce.4 = (bf16[2304]{0:T(1024)(128)(2,1)S(1)}, bf16[2304]{0:T(1024)(128)(2,1)}, bf16[2304]{0:T(1024)(128)(2,1)}, bf16[2304]{0:T(1024)(128)(2,1)}) all-reduce(bf16[2304]{0:T(1024)(128)(2,1)S(1)} %dynamic-update-slice, bf16[2304]{0:T(1024)(128)(2,1)S(1)} %dynamic-update-slice.1, ...), channel_id=1, replica_groups=mesh['dp'=8,'tensor'=4] {'dp'}, use_global_device_ids=true, to_apply=%add | all-reduce | flops 9216 | bytes 36864
  55.5 79.4 %all-gather.12.cloned.1.call-done = bf16[1024,2304]{1,0:T(8,128)(2,1)} async-done(((bf16[256,2304]{1,0:T(8,128)(2,1)}), bf16[1024,2304]{1,0:T(8,128)(2,1)}) %all-gather.12.cloned.1.call-update) | async-done | bytes 4718608 | tf_op jit(solution)/shard_map/all_gather | solution.py:182
  145.4 28.7 %all-gather.18.cloned.1.call-done = bf16[2304,1024]{1,0:T(8,128)(2,1)} async-done(((bf16[288,1024]{1,0:T(8,128)(2,1)}), bf16[2304,1024]{1,0:T(8,128)(2,1)}) %all-gather.18.cloned.1.call-update) | async-done | bytes 4718608 | tf_op jit(solution)/shard_map/all_gather | solution.py:163
  187.7 27.1 %all-gather.14.cloned.1.call-done = bf16[2304,1024]{1,0:T(8,128)(2,1)} async-done(((bf16[288,1024]{1,0:T(8,128)(2,1)}), bf16[2304,1024]{1,0:T(8,128)(2,1)}) %all-gather.14.cloned.1.call-update) | async-done | bytes 4718608 | tf_op jit(solution)/shard_map/all_gather | solution.py:164
  254.0 159.8 %reduce-scatter.15.cloned.1.call-done = f32[256,2304]{1,0:T(8,128)} async-done(((f32[1024,2304]{1,0:T(8,128)}), f32[256,2304]{1,0:T(8,128)}) %reduce-scatter.15.cloned.1.call-update) | async-done | bytes 2359312 | tf_op jit(solution)/shard_map/reduce_scatter | solution.py:211
  421.8 58.5 %all-gather.24.cloned.1.call-done = bf16[2304,2304]{1,0:T(8,128)(2,1)} async-done(((bf16[288,2304]{1,0:T(8,128)(2,1)}), bf16[2304,2304]{1,0:T(8,128)(2,1)}) %all-gather.24.cloned.1.call-update) | async-done | bytes 10616848 | tf_op jit(solution)/shard_map/all_gather | solution.py:166
  480.3 91.6 %all-gather.22.cloned.1.call-done = bf16[1024,2304]{1,0:T(8,128)(2,1)} async-done(((bf16[256,2304]{1,0:T(8,128)(2,1)}), bf16[1024,2304]{1,0:T(8,128)(2,1)}) %all-gather.22.cloned.1.call-update) | async-done | bytes 4718608 | tf_op jit(solution)/shard_map/all_gather | solution.py:213
  588.5 47.6 %all-gather.26.cloned.1.call-done = bf16[2304,2304]{1,0:T(8,128)(2,1)} async-done(((bf16[288,2304]{1,0:T(8,128)(2,1)}), bf16[2304,2304]{1,0:T(8,128)(2,1)}) %all-gather.26.cloned.1.call-update) | async-done | bytes 10616848 | tf_op jit(solution)/shard_map/all_gather | solution.py:167
  636.1 21.1 %multiply_convert_fusion.1 = (bf16[1024,2304]{1,0:T(8,128)(2,1)}, f32[1024,2304]{1,0:T(8,128)}) fusion(f32[1024,2304]{1,0:T(8,128)} %fusion.192, bf16[1024,2304]{1,0:T(8,128)(2,1)} %all-gather.22.cloned.1.call-done, bf16[2304,2304]{1,0:T(8,128)(2,1)} %all-gather.26.cloned.1.call-done), kind=kOutput, calls=%fused_computation.18 | convolution fusion | flops 10895228928 | bytes 38928384 | tf_op jit(solution)/shard_map/dot_general | solution.py:217
  657.2 44.5 %all-gather.28.cloned.1.call-done = bf16[2304,2304]{0,1:T(8,128)(2,1)} async-done(((bf16[2304,288]{0,1:T(8,128)(2,1)}), bf16[2304,2304]{0,1:T(8,128)(2,1)}) %all-gather.28.cloned.1.call-update) | async-done | bytes 10616848 | tf_op jit(solution)/shard_map/all_gather | solution.py:168
  720.1 159.7 %reduce-scatter.17.cloned.1.call-done = f32[256,2304]{1,0:T(8,128)} async-done(((f32[1024,2304]{1,0:T(8,128)}), f32[256,2304]{1,0:T(8,128)}) %reduce-scatter.17.cloned.1.call-update) | async-done | bytes 2359312 | tf_op jit(solution)/shard_map/reduce_scatter | solution.py:221
  888.3 90.3 %all-gather.30.cloned.1.call-done = bf16[1024,2304]{1,0:T(8,128)(2,1)} async-done(((bf16[256,2304]{1,0:T(8,128)(2,1)}), bf16[1024,2304]{1,0:T(8,128)(2,1)}) %all-gather.30.cloned.1.call-update) | async-done | bytes 4718608 | tf_op jit(solution)/shard_map/all_gather | solution.py:226
  978.6 27.8 %multiply_convert_fusion = (bf16[1024,2304]{1,0:T(8,128)(2,1)}, bf16[1024,2304]{1,0:T(8,128)(2,1)}) fusion(f32[1024,2304]{1,0:T(8,128)} %fusion.192, f32[1024,2304]{1,0:T(8,128)} %get-tuple-element.112, bf16[1024,2304]{1,0:T(8,128)(2,1)} %all-gather.30.cloned.1.call-done, bf16[2304,2304]{0,1:T(8,128)(2,1)} %all-gather.28.cloned.1.call-done), kind=kOutput, calls=%fused_computation.17 | convolution fusion | flops 10928259072 | bytes 43646976 | tf_op jit(solution)/shard_map/dot_general | solution.py:121
  1023.1 19.8 convolution_add_fusion
  1043.0 159.8 %reduce-scatter.19.cloned.1.call-done = f32[256,2304]{1,0:T(8,128)} async-done(((f32[1024,2304]{1,0:T(8,128)}), f32[256,2304]{1,0:T(8,128)}) %reduce-scatter.19.cloned.1.call-update) | async-done | bytes 2359312 | tf_op jit(solution)/shard_map/reduce_scatter | solution.py:235
  1213.8 89.0 %all-gather.32.cloned.1.call-done = bf16[1024,2304]{1,0:T(8,128)(2,1)} async-done(((bf16[256,2304]{1,0:T(8,128)(2,1)}), bf16[1024,2304]{1,0:T(8,128)(2,1)}) %all-gather.32.cloned.1.call-update) | async-done | bytes 4718608 | tf_op jit(solution)/shard_map/all_gather | solution.py:241
  1498.1 44.5 %reduce-scatter.31.cloned.1.call-done = bf16[288,2304]{1,0:T(8,128)(2,1)} async-done(((bf16[2304,2304]{1,0:T(8,128)(2,1)}), bf16[288,2304]{1,0:T(8,128)(2,1)}) %reduce-scatter.31.cloned.1.call-update) | async-done | bytes 1327120 | tf_op jit(solution)/shard_map/reduce_scatter | solution.py:310
  1545.6 82.6 %reduce-scatter.33.cloned.1.call-done = bf16[288,2304]{1,0:T(8,128)(2,1)} async-done(((bf16[2304,2304]{1,0:T(8,128)(2,1)}), bf16[288,2304]{1,0:T(8,128)(2,1)}) %reduce-scatter.33.cloned.1.call-update) | async-done | bytes 1327120 | tf_op jit(solution)/shard_map/reduce_scatter | solution.py:313
  1631.2 82.8 %reduce-scatter.35.cloned.1.call-done = bf16[2304,288]{0,1:T(8,128)(2,1)} async-done(((bf16[2304,2304]{0,1:T(8,128)(2,1)}), bf16[2304,288]{0,1:T(8,128)(2,1)}) %reduce-scatter.35.cloned.1.call-update) | async-done | bytes 1327120 | tf_op jit(solution)/shard_map/reduce_scatter | solution.py:316
  1718.1 54.9 %all-reduce.8.cloned.1.call-done = (bf16[288,1024]{1,0:T(8,128)(2,1)}, bf16[288,1024]{1,0:T(8,128)(2,1)}) async-done(((bf16[288,1024]{1,0:T(8,128)(2,1)}, bf16[288,1024]{1,0:T(8,128)(2,1)}), (bf16[288,1024]{1,0:T(8,128)(2,1)}, bf16[288,1024]{1,0:T(8,128)(2,1)})) %all-reduce.8.cloned.1.call-update) | async-done | bytes 1179664 | tf_op jit(solution)/shard_map/psum | solution.py:331
  1777.6 40.8 %reduce-scatter.23.cloned.1.call-done = bf16[288,512]{1,0:T(8,128)(2,1)} async-done(((bf16[2304,512]{1,0:T(8,128)(2,1)}), bf16[288,512]{1,0:T(8,128)(2,1)}) %reduce-scatter.23.cloned.1.call-update) | async-done | bytes 294928 | tf_op jit(solution)/shard_map/reduce_scatter | solution.py:298
  1820.3 44.4 %reduce-scatter.29.cloned.1.call-done = bf16[512,288]{0,1:T(8,128)(2,1)} async-done(((bf16[512,2304]{0,1:T(8,128)(2,1)}), bf16[512,288]{0,1:T(8,128)(2,1)}) %reduce-scatter.29.cloned.1.call-update) | async-done | bytes 294928 | tf_op jit(solution)/shard_map/reduce_scatter | solution.py:307
  1866.5 85.7 %reduce-scatter.21.cloned.1.call-done = bf16[256,2304]{1,0:T(8,128)(2,1)} async-done(((bf16[1024,2304]{1,0:T(8,128)(2,1)}), bf16[256,2304]{1,0:T(8,128)(2,1)}) %reduce-scatter.21.cloned.1.call-update) | async-done | bytes 1179664 | tf_op jit(solution)/shard_map/reduce_scatter | solution.py:281
  1962.3 32.0 %reduce-scatter.37.cloned.1.call-done = bf16[288,4]{1,0:T(8,128)(2,1)} async-done(((bf16[2304,4]{1,0:T(8,128)(2,1)}), bf16[288,4]{1,0:T(8,128)(2,1)}) %reduce-scatter.37.cloned.1.call-update) | async-done | bytes 2320
  (320 shorter events, 398.1 us)
Async XLA Ops:
  7.2 48.3 %all-gather.16.cloned.1.call-start = ((), (), s32[]{:S(2)}) async-start(), calls=%async_computation.14 | async-start | bytes 2654208 | tf_op jit(solution)/shard_map/all_gather | solution.py:162
  7.9 126.9 %all-gather.12.cloned.1.call-start = ((), (), s32[]{:S(2)}) async-start(), calls=%async_computation.12 | async-start | bytes 5898240 | tf_op jit(solution)/shard_map/all_gather | solution.py:182
  45.8 128.3 %all-gather.18.cloned.1.call-start = ((), (), s32[]{:S(2)}) async-start(), calls=%async_computation.15 | async-start | bytes 5308416 | tf_op jit(solution)/shard_map/all_gather | solution.py:163
  46.6 168.3 %all-gather.14.cloned.1.call-start = ((), (), s32[]{:S(2)}) async-start(), calls=%async_computation.13 | async-start | bytes 5308416 | tf_op jit(solution)/shard_map/all_gather | solution.py:164
  47.1 198.5 %all-gather.20.cloned.1.call-start = ((), (), s32[]{:S(2)}) async-start(), calls=%async_computation.16 | async-start | bytes 2654208 | tf_op jit(solution)/shard_map/all_gather | solution.py:165
  47.7 366.0 %reduce-scatter.15.cloned.1.call-start = ((), (), s32[]{:S(2)}) async-start(), calls=%async_computation.17 | async-start | bytes 11796480 | tf_op jit(solution)/shard_map/reduce_scatter | solution.py:211
  252.3 228.0 %all-gather.24.cloned.1.call-start = ((), (), s32[]{:S(2)}) async-start(), calls=%async_computation.19 | async-start | bytes 11943936 | tf_op jit(solution)/shard_map/all_gather | solution.py:166
  253.1 318.8 %all-gather.22.cloned.1.call-start = ((), (), s32[]{:S(2)}) async-start(), calls=%async_computation.18 | async-start | bytes 5898240 | tf_op jit(solution)/shard_map/all_gather | solution.py:213
  420.4 215.7 %all-gather.26.cloned.1.call-start = ((), (), s32[]{:S(2)}) async-start(), calls=%async_computation.20 | async-start | bytes 11943936 | tf_op jit(solution)/shard_map/all_gather | solution.py:167
  421.1 280.5 %all-gather.28.cloned.1.call-start = ((), (), s32[]{:S(2)}) async-start(), calls=%async_computation.21 | async-start | bytes 11943936 | tf_op jit(solution)/shard_map/all_gather | solution.py:168
  421.7 458.1 %reduce-scatter.17.cloned.1.call-start = ((), (), s32[]{:S(2)}) async-start(), calls=%async_computation.22 | async-start | bytes 11796480 | tf_op jit(solution)/shard_map/reduce_scatter | solution.py:221
  718.4 260.2 %all-gather.30.cloned.1.call-start = ((), (), s32[]{:S(2)}) async-start(), calls=%async_computation.23 | async-start | bytes 5898240 | tf_op jit(solution)/shard_map/all_gather | solution.py:226
  888.2 314.7 %reduce-scatter.19.cloned.1.call-start = ((), (), s32[]{:S(2)}) async-start(), calls=%async_computation.24 | async-start | bytes 11796480 | tf_op jit(solution)/shard_map/reduce_scatter | solution.py:235
  1043.0 259.8 %all-gather.32.cloned.1.call-start = ((), (), s32[]{:S(2)}) async-start(), calls=%async_computation.25 | async-start | bytes 5898240 | tf_op jit(solution)/shard_map/all_gather | solution.py:241
  1212.4 231.9 %reduce-scatter.25.cloned.1.call-start = ((), (), s32[]{:S(2)}) async-start(), calls=%async_computation.28 | async-start | bytes 1327104 | tf_op jit(solution)/shard_map/reduce_scatter | solution.py:301
  1380.8 76.2 %reduce-scatter.27.cloned.1.call-start = ((), (), s32[]{:S(2)}) async-start(), calls=%async_computation.29 | async-start | bytes 1327104 | tf_op jit(solution)/shard_map/reduce_scatter | solution.py:304
  1392.6 150.0 %reduce-scatter.31.cloned.1.call-start = ((), (), s32[]{:S(2)}) async-start(), calls=%async_computation.31 | async-start | bytes 11943936 | tf_op jit(solution)/shard_map/reduce_scatter | solution.py:310
  1409.8 218.4 %reduce-scatter.33.cloned.1.call-start = ((), (), s32[]{:S(2)}) async-start(), calls=%async_computation.32 | async-start | bytes 11943936 | tf_op jit(solution)/shard_map/reduce_scatter | solution.py:313
  1426.8 287.1 %reduce-scatter.35.cloned.1.call-start = ((), (), s32[]{:S(2)}) async-start(), calls=%async_computation.33 | async-start | bytes 11943936 | tf_op jit(solution)/shard_map/reduce_scatter | solution.py:316
  1444.2 328.9 %all-reduce.8.cloned.1.call-start = ((), (), s32[]{:S(2)}) async-start(), calls=%async_computation.35 | async-start | bytes 2359296 | tf_op jit(solution)/shard_map/psum | solution.py:331
  1458.8 359.6 %reduce-scatter.23.cloned.1.call-start = ((), (), s32[]{:S(2)}) async-start(), calls=%async_computation.27 | async-start | bytes 2654208 | tf_op jit(solution)/shard_map/reduce_scatter | solution.py:298
  1473.4 391.3 %reduce-scatter.29.cloned.1.call-start = ((), (), s32[]{:S(2)}) async-start(), calls=%async_computation.30 | async-start | bytes 2654208 | tf_op jit(solution)/shard_map/reduce_scatter | solution.py:307
  1482.0 470.3 %reduce-scatter.21.cloned.1.call-start = ((), (), s32[]{:S(2)}) async-start(), calls=%async_computation.26 | async-start | bytes 5898240 | tf_op jit(solution)/shard_map/reduce_scatter | solution.py:281
  1496.8 497.5 %reduce-scatter.37.cloned.1.call-start = ((), (), s32[]{:S(2)}) async-start(), calls=%async_computation.34 | async-start | bytes 663552
  (74 other events, 2444.7 us)
Sparse Core Ops, SparseCore 0:
  9.9 31.9 all-gather.15
  46.0 88.8 all-gather.11
  136.7 37.3 all-gather.17
  175.9 38.9 all-gather.13
  216.6 29.0 all-gather.19
  252.4 161.2 reduce-scatter.14
  415.6 64.6 all-gather.23
  482.5 89.4 all-gather.21
  573.8 62.2 all-gather.25
  637.8 63.8 all-gather.27
  718.5 161.2 reduce-scatter.16
  888.3 90.2 all-gather.29
  1043.1 159.7 reduce-scatter.18
  1212.5 90.2 all-gather.31
  1380.9 35.2 reduce-scatter.24
  1420.2 36.7 reduce-scatter.26
  1460.3 82.1 reduce-scatter.30
  1545.9 82.1 reduce-scatter.32
  1631.7 82.1 reduce-scatter.34
  1716.8 56.2 all-reduce.7
  1776.4 42.0 reduce-scatter.22
  1822.2 42.4 reduce-scatter.28
  1867.0 85.2 reduce-scatter.20
  1959.4 34.8 reduce-scatter.36
where the time goes:
time: 2020 us; the launch traced here: 2010 us
  waiting for transfers between devices  1530 us (76%)
  matrix products  308 us (15%)
  other arithmetic  78.9 us (4%)
  blocking collectives  38.2 us (2%)
  local copies, waits for them, and re-layouts  36.4 us (2%)
    reduce_scatter x1, waiting for transfers between devices, body(): lax.psum_scatter(grad_mid, 'tensor', scatter_dimension=0, tiled=True)  160 us
    reduce_scatter x1, waiting for transfers between devices, body(): lax.psum_scatter(attn_part, 'tensor', scatter_dimension=0, tiled=True)  160 us
    reduce_scatter x1, waiting for transfers between devices, body(): lax.psum_scatter(feed_part, 'tensor', scatter_dimension=0, tiled=True)  160 us
    all_gather x1, waiting for transfers between devices, body(): lax.all_gather(rms_scale(resid, gain_three).astype(jnp.bfloat16), 'tensor...  91.6 us
    all_gather x1, waiting for transfers between devices, body(): lax.all_gather(grad_feed_rows.astype(jnp.bfloat16), 'tensor', axis=0, til...  90.3 us
    all_gather x1, waiting for transfers between devices, body(): lax.all_gather(grad_attn_rows.astype(jnp.bfloat16), 'tensor', axis=0, til...  89 us
    reduce_scatter x1, waiting for transfers between devices, body(): lax.psum_scatter(grad_first.astype(jnp.bfloat16), 'tensor', scatter_dimen...  85.7 us
    dot_general x7, matrix products, contract_cols(): lax.dot_general(left_side, right_side, (((1,), (1,)), ((), ())), preferre...  84.5 us
  transfers between devices with their start and end apart: 24, of which 22 were waited for; matrix products, arithmetic and copies ran while one was open for 11% of the time, Pallas kernels for 0%

commit v1 on v0

v1 whole, which is shorter than its diff:
```python
import functools

import jax
import jax.numpy as jnp
from jax import lax
from jax.experimental import pallas as pl
from jax.experimental.pallas import tpu as pltpu
from jax.sharding import PartitionSpec as P

H = 8
KV = 4
HD = 256
L = 1024
PIECE = 256

EPS = 1e-06
CAP = 50.0
F32 = jnp.float32
BF16 = jnp.bfloat16
MESH = pl.DeviceIdType.MESH
ANY = pl.BlockSpec(memory_space=pl.ANY)
VM = pl.BlockSpec(memory_space=pltpu.VMEM)
SM = pl.BlockSpec(memory_space=pltpu.SMEM)
ROWS = 16
TILE = 256


def dot_nn(a, b):
    return lax.dot_general(a, b, (((1,), (0,)), ((), ())), preferred_element_type=F32)


def dot_nt(a, b):
    return lax.dot_general(a, b, (((1,), (1,)), ((), ())), preferred_element_type=F32)


def dot_tn(a, b):
    return lax.dot_general(a, b, (((0,), (0,)), ((), ())), preferred_element_type=F32)


def tile_of(width):
    return next(t for t in (256, 384, 128) if width % t == 0)


def loop(count, body):
    lax.fori_loop(0, count, lambda t, c: (body(t), c)[1], 0)


def block_at(i, n, s):
    m = jnp.minimum(i, n - 1 - i)
    near = i + jnp.where(s % 2 == 1, -((s + 1) // 2), s // 2)
    far = jnp.where(i * 2 < n, i + (s - m), i - (s - m))
    return jnp.where(s <= 2 * m, near, far)


def line_barrier(i, n):
    barrier = pltpu.get_barrier_semaphore()

    @pl.when(i > 0)
    def _():
        pl.semaphore_signal(barrier, 1, device_id={"tensor": i - 1}, device_id_type=MESH)

    @pl.when(i < n - 1)
    def _():
        pl.semaphore_signal(barrier, 1, device_id={"tensor": i + 1}, device_id_type=MESH)

    pl.semaphore_wait(barrier, jnp.minimum(i, 1) + jnp.minimum(n - 1 - i, 1))


def gather_line(i, n, held, send, recv, compute):
    def copy(block, way, s, to):
        return pltpu.make_async_remote_copy(
            held.at[block],
            held.at[block],
            send.at[way, s],
            recv.at[block],
            device_id={"tensor": to},
            device_id_type=MESH,
        )

    up, down = jnp.minimum(i + 1, n - 1), jnp.maximum(i - 1, 0)

    def step(s):
        low, high = i - s, i + s

        @pl.when((s > 0) & (low >= 0))
        def _():
            copy(low, 0, s, up).wait_recv()

        @pl.when((low >= 0) & (i < n - 1))
        def _():
            copy(low, 0, s, up).start()

        @pl.when((s > 0) & (high < n))
        def _():
            copy(high, 1, s, down).wait_recv()

        @pl.when((high < n) & (i > 0))
        def _():
            copy(high, 1, s, down).start()

        compute(s, block_at(i, n, s))

    loop(n, step)

    def finish(s):
        low, high = i - s, i + s

        @pl.when((low >= 0) & (i < n - 1))
        def _():
            copy(low, 0, s, up).wait_send()

        @pl.when((high < n) & (i > 0))
        def _():
            copy(high, 1, s, down).wait_send()

    loop(n, finish)


def scatter_line(i, n, part, landed, send, recv, compute, own):
    rows = part.shape[1]

    def copy(block, way, t, to):
        slot = jnp.where(block == to, n, block) if way else block
        return pltpu.make_async_remote_copy(
            part.at[block],
            landed.at[slot],
            send.at[way, t],
            recv.at[slot],
            device_id={"tensor": to},
            device_id_type=MESH,
        )

    def arrived(slot):
        pltpu.make_async_remote_copy(
            landed.at[slot],
            landed.at[slot],
            send.at[0, 0],
            recv.at[slot],
            device_id={"tensor": i},
            device_id_type=MESH,
        ).wait_recv()

    def add(block):
        def chunk(c):
            r = pl.ds(c * ROWS, ROWS)
            total = part[block, r, :].astype(F32) + landed[block, r, :].astype(F32)
            part[block, r, :] = total.astype(BF16)

        loop(rows // ROWS, chunk)

    up, down = jnp.minimum(i + 1, n - 1), jnp.maximum(i - 1, 0)

    def step(k):
        t = k + 1
        compute(k, block_at(i, n, n - t))
        above, below = i + n - t, i - n + t

        @pl.when((above < n) & (i > 0))
        def _():
            arrived(above)
            add(above)

        @pl.when(above < n)
        def _():
            copy(above, 0, t, up).start()

        @pl.when((below >= 0) & (i < n - 1))
        def _():
            arrived(below)
            add(below)

        @pl.when(below >= 0)
        def _():
            copy(below, 1, t, down).start()

    loop(n - 1, step)
    own(n - 1)

    @pl.when(i > 0)
    def _():
        arrived(i)

    @pl.when(i < n - 1)
    def _():
        arrived(jnp.int32(n))

    def finish(k):
        t = k + 1

        @pl.when(i + n - t < n)
        def _():
            copy(i + n - t, 0, t, up).wait_send()

        @pl.when(i - n + t >= 0)
        def _():
            copy(i - n + t, 1, t, down).wait_send()

    return functools.partial(loop, n - 1, finish)


def summed_rows(i, n, mine, landed, r):
    zero = jnp.zeros((), F32)
    low = jnp.where(i > 0, landed[i, r, :].astype(F32), zero)
    high = jnp.where(i < n - 1, landed[n, r, :].astype(F32), zero)
    return mine[r, :] + low + high


def inverse_rms(v):
    return lax.rsqrt(jnp.mean(v * v, axis=-1, keepdims=True) + EPS)


def norm_back(e, v, r):
    unit = v * r
    return r * (e - unit * jnp.mean(e * unit, axis=-1, keepdims=True))


def fold_rows(v):
    return v.reshape(-1, 8, v.shape[-1]).sum(axis=0)


class Feed:
    def __init__(self, sources, slots, sems, which):
        self.sources, self.slots, self.sems, self.which = sources, slots, sems, which

    def copies(self, s):
        return [
            pltpu.make_async_copy(src.at[self.which(s)], slot.at[s % 2], self.sems.at[k, s % 2])
            for k, (src, slot) in enumerate(zip(self.sources, self.slots))
        ]

    def start(self, s):
        for c in self.copies(s):
            c.start()

    def wait(self, s):
        for c in self.copies(s):
            c.wait()

    def advance(self, s, count):
        self.wait(s)

        @pl.when(s + 1 < count)
        def _():
            self.start(s + 1)


class Drain:
    def __init__(self, targets, slots, sems, which):
        self.targets, self.slots, self.sems, self.which = targets, slots, sems, which

    def copies(self, s):
        return [
            pltpu.make_async_copy(slot.at[s % 2], dst.at[self.which(s)], self.sems.at[k, s % 2])
            for k, (dst, slot) in enumerate(zip(self.targets, self.slots))
        ]

    def free(self, s):
        @pl.when(s >= 2)
        def _():
            for c in self.copies(s - 2):
                c.wait()

    def start(self, s):
        for c in self.copies(s):
            c.start()

    def finish(self, count):
        for s in range(max(0, count - 2), count):
            for c in self.copies(jnp.int32(s)):
                c.wait()


def line_scratch(n):
    return [pltpu.SemaphoreType.DMA((2, n)), pltpu.SemaphoreType.DMA((n + 1,))]


def params(cid, mib):
    return pltpu.CompilerParams(
        collective_id=cid, has_side_effects=True, vmem_limit_bytes=mib << 20
    )


def cost(flops, moved):
    return pl.CostEstimate(flops=flops, bytes_accessed=moved, transcendentals=0)


def gains_kernel(m, mine, out, send, recv):
    me = lax.axis_index("dp")
    barrier = pltpu.get_barrier_semaphore()
    for k in range(1, m):
        pl.semaphore_signal(
            barrier, 1, device_id={"dp": lax.rem(me + k, m)}, device_id_type=MESH
        )
    pl.semaphore_wait(barrier, m - 1)

    def copy(owner, k):
        return pltpu.make_async_remote_copy(
            mine,
            out.at[owner],
            send.at[k],
            recv.at[k],
            device_id={"dp": lax.rem(me + k, m)},
            device_id_type=MESH,
        )

    for k in range(1, m):
        copy(me, k).start()
    out[me] = mine[...]
    for k in range(1, m):
        copy(lax.rem(me + m - k, m), k).wait_recv()
    for k in range(1, m):
        copy(me, k).wait_send()


def gather_gains(m, mine):
    return pl.pallas_call(
        functools.partial(gains_kernel, m),
        out_shape=jax.ShapeDtypeStruct((m,) + mine.shape, mine.dtype),
        in_specs=[VM],
        out_specs=VM,
        scratch_shapes=[pltpu.SemaphoreType.DMA((m,)), pltpu.SemaphoreType.DMA((m,))],
        compiler_params=params(0, 16),
        name="gains",
    )(mine)


def sum_gains_kernel(n, m, mine, out, landed, total, across, send, recv, send_two, recv_two):
    me, i = lax.axis_index("dp"), lax.axis_index("tensor")
    barrier = pltpu.get_barrier_semaphore()
    dp_peer = lambda k: {"dp": lax.rem(me + k, m)}
    line_peer = lambda k: {"tensor": lax.rem(i + k, n)}
    for k in range(1, m):
        pl.semaphore_signal(barrier, 1, device_id=dp_peer(k), device_id_type=MESH)
    for k in range(1, n):
        pl.semaphore_signal(barrier, 1, device_id=line_peer(k), device_id_type=MESH)
    pl.semaphore_wait(barrier, m + n - 2)

    def to_owner(k):
        return pltpu.make_async_remote_copy(
            mine.at[lax.rem(me + k, m)], landed.at[k], send.at[k], recv.at[k],
            device_id=dp_peer(k), device_id_type=MESH,
        )

    def along(k):
        return pltpu.make_async_remote_copy(
            total, across.at[k], send_two.at[k], recv_two.at[k],
            device_id=line_peer(k), device_id_type=MESH,
        )

    for k in range(1, m):
        to_owner(k).start()
    here = mine[me]
    for k in range(1, m):
        to_owner(k).wait_recv()
        here = here + landed[k]
    total[...] = here
    for k in range(1, n):
        along(k).start()
    for k in range(1, n):
        along(k).wait_recv()
        here = here + across[k]
    out[...] = here
    for k in range(1, m):
        to_owner(k).wait_send()
    for k in range(1, n):
        along(k).wait_send()


def sum_gains(n, m, mine):
    shape = mine.shape[1:]
    return pl.pallas_call(
        functools.partial(sum_gains_kernel, n, m),
        out_shape=jax.ShapeDtypeStruct(shape, F32),
        in_specs=[VM],
        out_specs=VM,
        scratch_shapes=[
            pltpu.VMEM((m,) + shape, F32),
            pltpu.VMEM(shape, F32),
            pltpu.VMEM((n,) + shape, F32),
        ]
        + [pltpu.SemaphoreType.DMA((m,))] * 2
        + [pltpu.SemaphoreType.DMA((n,))] * 2,
        compiler_params=params(6, 16),
        name="sum_gains",
    )(mine)


def first_kernel(n, x, gains, full, held, send, recv, out_sem):
    i = lax.axis_index("tensor")
    rows = x.shape[0]
    line_barrier(i, n)
    scale = 1.0 + gains[0:1, :]

    def chunk(c):
        r = pl.ds(c * ROWS, ROWS)
        v = x[r, :].astype(F32)
        held[i, r, :] = (v * inverse_rms(v) * scale).astype(BF16)

    loop(rows // ROWS, chunk)

    def keep(s, block):
        pltpu.make_async_copy(held.at[block], full.at[block], out_sem.at[s]).start()

    gather_line(i, n, held, send, recv, keep)

    def finish(s):
        block = block_at(i, n, s)
        pltpu.make_async_copy(held.at[block], full.at[block], out_sem.at[s]).wait()

    loop(n, finish)


def first(n, x, gains):
    rows, width = x.shape
    return pl.pallas_call(
        functools.partial(first_kernel, n),
        out_shape=jax.ShapeDtypeStruct((n, rows, width), BF16),
        in_specs=[VM, VM],
        out_specs=ANY,
        scratch_shapes=[pltpu.VMEM((n, rows, width), BF16)]
        + line_scratch(n)
        + [pltpu.SemaphoreType.DMA((n,))],
        compiler_params=params(1, 32),
        cost_estimate=cost(0, 300 << 20),
        name="first",
    )(x, gains)


def turn(u, cos, sin):
    half = HD // 2
    a, b = u[:, :half], u[:, half:]
    return jnp.concatenate([a * cos - b * sin, b * cos + a * sin], axis=-1)


def row_limit(starts, seq, first_row, rows):
    pos = first_row + lax.broadcasted_iota(jnp.int32, (rows, 1), 0)
    limit = pos + 1
    for piece in range(2):
        begin = starts[seq, piece]
        inside = (pos >= begin) & (pos < begin + PIECE)
        limit = jnp.maximum(limit, jnp.where(inside, begin + PIECE, 0))
    return limit


def key_span(first_row, rows):
    return min(L, first_row + rows + PIECE)


def weights_of(q, k, limit):
    bent = jnp.tanh(dot_nt(q, k) * (1.0 / CAP))
    seen = lax.broadcasted_iota(jnp.int32, (1, k.shape[0]), 1) < limit
    w = jnp.where(seen, jnp.exp(CAP * bent), 0.0)
    return w * pl.reciprocal(jnp.sum(w, axis=-1, keepdims=True)), bent


def attend_kernel(heads, kvs, starts, h1, w, cos, sin, q_out, k_out, v_out, o_out):
    tokens = h1.shape[0]
    fan = heads // kvs
    block = 256

    def project(b):
        r = pl.ds(pl.multiple_of(b * block, block), block)
        at = pl.ds(pl.multiple_of(lax.rem(b * block, L), block), block)
        c, s = cos[at, :], sin[at, :]
        x = h1[r, :]
        for h in range(heads):
            u = dot_nn(x, w[:, h * HD : (h + 1) * HD])
            q_out[h, r, :] = (turn(u, c, s) * (HD**-0.5)).astype(BF16)
        for g in range(kvs):
            u = dot_nn(x, w[:, (heads + g) * HD : (heads + g + 1) * HD])
            k_out[g, r, :] = turn(u, c, s).astype(BF16)
            u = dot_nn(x, w[:, (heads + kvs + g) * HD : (heads + kvs + g + 1) * HD])
            v_out[g, r, :] = u.astype(BF16)

    loop(tokens // block, project)
    for seq in range(tokens // L):
        base = seq * L
        for row in range(0, L, block):
            span = key_span(row, block)
            limit = row_limit(starts, seq, row, block)
            for h in range(heads):
                q = q_out[h, base + row : base + row + block, :]
                p, _ = weights_of(q, k_out[h // fan, base : base + span, :], limit)
                o = dot_nn(p.astype(BF16), v_out[h // fan, base : base + span, :])
                o_out[base + row : base + row + block, h * HD : (h + 1) * HD] = o.astype(BF16)


def attend(heads, kvs, starts, h1, w, cos, sin):
    tokens = h1.shape[0]
    return pl.pallas_call(
        functools.partial(attend_kernel, heads, kvs),
        out_shape=[
            jax.ShapeDtypeStruct((heads, tokens, HD), BF16),
            jax.ShapeDtypeStruct((kvs, tokens, HD), BF16),
            jax.ShapeDtypeStruct((kvs, tokens, HD), BF16),
            jax.ShapeDtypeStruct((tokens, heads * HD), BF16),
        ],
        in_specs=[SM, VM, VM, VM, VM],
        out_specs=[VM, VM, VM, VM],
        compiler_params=pltpu.CompilerParams(vmem_limit_bytes=48 << 20),
        cost_estimate=cost(20 << 30, 20 << 20),
        name="attend",
    )(starts, h1, w, cos, sin)


def attend_back_kernel(heads, kvs, starts, q_in, k_in, v_in, do_in, cos, sin, out, dk, dv):
    tokens = q_in.shape[1]
    fan = heads // kvs
    block = 256
    for seq in range(tokens // L):
        base = seq * L
        for g in range(kvs):
            dk[...] = jnp.zeros_like(dk)
            dv[...] = jnp.zeros_like(dv)
            for row in range(0, L, block):
                span = key_span(row, block)
                limit = row_limit(starts, seq, row, block)
                k = k_in[g, base : base + span, :]
                v = v_in[g, base : base + span, :]
                at = slice(base + row, base + row + block)
                for h in range(g * fan, (g + 1) * fan):
                    q = q_in[h, at, :]
                    do = do_in[at, h * HD : (h + 1) * HD]
                    p, bent = weights_of(q, k, limit)
                    dp = dot_nt(do, v)
                    delta = jnp.sum(p * dp, axis=-1, keepdims=True)
                    ds = (p * (dp - delta) * (1.0 - bent * bent)).astype(BF16)
                    dq = dot_nn(ds, k)
                    c, s = cos[row : row + block, :], sin[row : row + block, :]
                    out[at, h * HD : (h + 1) * HD] = (turn(dq, c, -s) * (HD**-0.5)).astype(BF16)
                    dk[:span, :] += dot_tn(ds, q)
                    dv[:span, :] += dot_tn(p.astype(BF16), do)

            def close(b, g=g, base=base):
                r = pl.ds(pl.multiple_of(b * block, block), block)
                to = pl.ds(pl.multiple_of(base + b * block, block), block)
                back = turn(dk[r, :], cos[r, :], -sin[r, :])
                out[to, (heads + g) * HD : (heads + g + 1) * HD] = back.astype(BF16)
                left = (heads + kvs + g) * HD
                out[to, left : left + HD] = dv[r, :].astype(BF16)

            loop(L // block, close)


def attend_back(heads, kvs, starts, q, k, v, do, cos, sin):
    tokens = q.shape[1]
    return pl.pallas_call(
        functools.partial(attend_back_kernel, heads, kvs),
        out_shape=jax.ShapeDtypeStruct((tokens, (heads + 2 * kvs) * HD), BF16),
        in_specs=[SM, VM, VM, VM, VM, VM, VM],
        out_specs=VM,
        scratch_shapes=[pltpu.VMEM((L, HD), F32), pltpu.VMEM((L, HD), F32)],
        compiler_params=pltpu.CompilerParams(vmem_limit_bytes=48 << 20),
        cost_estimate=cost(30 << 30, 20 << 20),
        name="attend_back",
    )(starts, q, k, v, do, cos, sin)


def into_feed_kernel(
    n, x, gains, o_hbm, wo_hbm, wg_hbm, wu_hbm,
    attn_out, y_out, h3_full, hid_out, up_out, ge_out,
    o, wo, wg, wu, part, landed, mine, held, hid_s, up_s, ge_s,
    load, rs_send, rs_recv, ag_send, ag_recv, keep_sem, out_sem,
):
    i = lax.axis_index("tensor")
    rows, width = x.shape
    loads = [
        pltpu.make_async_copy(src, dst, load.at[k])
        for k, (src, dst) in enumerate(((o_hbm, o), (wo_hbm, wo), (wg_hbm, wg), (wu_hbm, wu)))
    ]
    for c in loads:
        c.start()
    line_barrier(i, n)
    loads[0].wait()
    loads[1].wait()

    def compute(t, block):
        def tile(k):
            at = pl.ds(pl.multiple_of(k * TILE, TILE), TILE)
            part[block, :, at] = dot_nt(o[block], wo[at, :]).astype(BF16)

        loop(width // TILE, tile)

    def own(t):
        def tile(k):
            at = pl.ds(pl.multiple_of(k * TILE, TILE), TILE)
            mine[:, at] = dot_nt(o[i], wo[at, :])

        loop(width // TILE, tile)

    done = scatter_line(i, n, part, landed, rs_send, rs_recv, compute, own)
    scale_two, scale_three = 1.0 + gains[1:2, :], 1.0 + gains[2:3, :]

    def chunk(c):
        r = pl.ds(c * ROWS, ROWS)
        attn = summed_rows(i, n, mine, landed, r)
        attn_out[r, :] = attn
        y = x[r, :].astype(F32) + attn * inverse_rms(attn) * scale_two
        y_out[r, :] = y
        held[i, r, :] = (y * inverse_rms(y) * scale_three).astype(BF16)

    loop(rows // ROWS, chunk)
    done()
    loads[2].wait()
    loads[3].wait()
    drain = Drain(
        (hid_out, up_out, ge_out), (hid_s, up_s, ge_s), out_sem, lambda s: block_at(i, n, s)
    )

    def forward(s, block):
        pltpu.make_async_copy(held.at[block], h3_full.at[block], keep_sem.at[s]).start()
        drain.free(s)
        slot = s % 2
        span = tile_of(wg.shape[1])

        def tile(k):
            at = pl.ds(pl.multiple_of(k * span, span), span)
            u = dot_nn(held[block], wg[:, at])
            up = dot_nn(held[block], wu[:, at])
            c = 0.7978845608028654
            th = jnp.tanh(c * (u + 0.044715 * (u * u * u)))
            half = 0.5 * (1.0 + th)
            gelu = u * half
            slope = half + 0.5 * u * (1.0 - th * th) * (c * (1.0 + 0.134145 * (u * u)))
            hid_s[slot, :, at] = (gelu * up).astype(BF16)
            up_s[slot, :, at] = (up * slope).astype(BF16)
            ge_s[slot, :, at] = gelu.astype(BF16)

        loop(wg.shape[1] // span, tile)
        drain.start(s)

    gather_line(i, n, held, ag_send, ag_recv, forward)
    drain.finish(n)

    def finish(s):
        block = block_at(i, n, s)
        pltpu.make_async_copy(held.at[block], h3_full.at[block], keep_sem.at[s]).wait()

    loop(n, finish)


def into_feed(n, x, gains, o, wo, wg, wu):
    rows, width = x.shape
    wide = wg.shape[1]
    blocks = lambda w: jax.ShapeDtypeStruct((n, rows, w), BF16)
    mine = jax.ShapeDtypeStruct((rows, width), F32)
    return pl.pallas_call(
        functools.partial(into_feed_kernel, n),
        out_shape=[mine, mine, blocks(width), blocks(wide), blocks(wide), blocks(wide)],
        in_specs=[VM, VM, ANY, ANY, ANY, ANY],
        out_specs=[VM, VM, ANY, ANY, ANY, ANY],
        scratch_shapes=[
            pltpu.VMEM(o.shape, BF16),
            pltpu.VMEM(wo.shape, BF16),
            pltpu.VMEM(wg.shape, BF16),
            pltpu.VMEM(wu.shape, BF16),
            pltpu.VMEM((n, rows, width), BF16),
            pltpu.VMEM((n + 1, rows, width), BF16),
            pltpu.VMEM((rows, width), F32),
            pltpu.VMEM((n, rows, width), BF16),
        ]
        + [pltpu.VMEM((2, rows, wide), BF16)] * 3
        + [pltpu.SemaphoreType.DMA((4,))]
        + line_scratch(n) * 2
        + [pltpu.SemaphoreType.DMA((n,)), pltpu.SemaphoreType.DMA((3, 2))],
        compiler_params=params(2, 62),
        cost_estimate=cost(0, 600 << 20),
        name="into_feed",
    )(x, gains, o, wo, wg, wu)


def turn_feed_kernel(
    n, y, dout, gains, hid_hbm, wd_hbm, up_hbm, ge_hbm,
    layer_out, gain_out, df_full, dgate_out, dup_out,
    wd, hid_s, part, landed, mine, held, up_s, ge_s, dg_s, du_s, fold,
    load, feed_sem, rs_send, rs_recv, ag_send, ag_recv, keep_sem, back_sem, out_sem,
):
    i = lax.axis_index("tensor")
    rows, width = y.shape
    whole = pltpu.make_async_copy(wd_hbm, wd, load.at[0])
    whole.start()
    feed = Feed((hid_hbm,), (hid_s,), feed_sem, lambda s: block_at(i, n, n - 1 - s))
    feed.start(jnp.int32(0))
    line_barrier(i, n)
    whole.wait()

    def compute(t, block):
        feed.advance(t, n)
        slot = t % 2

        def tile(k):
            at = pl.ds(pl.multiple_of(k * TILE, TILE), TILE)
            part[block, :, at] = dot_nt(hid_s[slot], wd[at, :]).astype(BF16)

        loop(width // TILE, tile)

    def own(t):
        t = jnp.int32(t)
        feed.advance(t, n)
        slot = t % 2

        def tile(k):
            at = pl.ds(pl.multiple_of(k * TILE, TILE), TILE)
            mine[:, at] = dot_nt(hid_s[slot], wd[at, :])

        loop(width // TILE, tile)

    done = scatter_line(i, n, part, landed, rs_send, rs_recv, compute, own)
    scale = 1.0 + gains[3:4, :]
    fold[...] = jnp.zeros_like(fold)

    def chunk(c):
        r = pl.ds(c * ROWS, ROWS)
        f = summed_rows(i, n, mine, landed, r)
        g = dout[r, :].astype(F32)
        inv = inverse_rms(f)
        layer_out[r, :] = (y[r, :] + f * inv * scale).astype(BF16)
        held[i, r, :] = norm_back(g * scale, f, inv).astype(BF16)
        fold[...] += fold_rows(g * (f * inv))

    loop(rows // ROWS, chunk)
    gain_out[...] = jnp.sum(fold[...], axis=0, keepdims=True)
    done()
    sides = Feed((up_hbm, ge_hbm), (up_s, ge_s), back_sem, lambda s: block_at(i, n, s))
    drain = Drain((dgate_out, dup_out), (dg_s, du_s), out_sem, lambda s: block_at(i, n, s))
    sides.start(jnp.int32(0))

    def backward(s, block):
        pltpu.make_async_copy(held.at[block], df_full.at[block], keep_sem.at[s]).start()
        sides.advance(s, n)
        drain.free(s)
        slot = s % 2
        span = tile_of(wd.shape[1])

        def tile(k):
            at = pl.ds(pl.multiple_of(k * span, span), span)
            dhid = dot_nn(held[block], wd[:, at])
            dg_s[slot, :, at] = (dhid * up_s[slot, :, at].astype(F32)).astype(BF16)
            du_s[slot, :, at] = (dhid * ge_s[slot, :, at].astype(F32)).astype(BF16)

        loop(wd.shape[1] // span, tile)
        drain.start(s)

    gather_line(i, n, held, ag_send, ag_recv, backward)
    drain.finish(n)

    def finish(s):
        block = block_at(i, n, s)
        pltpu.make_async_copy(held.at[block], df_full.at[block], keep_sem.at[s]).wait()

    loop(n, finish)


def turn_feed(n, y, dout, gains, hid, wd, up, ge):
    rows, width = y.shape
    wide = wd.shape[1]
    blocks = lambda w: jax.ShapeDtypeStruct((n, rows, w), BF16)
    return pl.pallas_call(
        functools.partial(turn_feed_kernel, n),
        out_shape=[
            jax.ShapeDtypeStruct((rows, width), BF16),
            jax.ShapeDtypeStruct((1, width), F32),
            blocks(width),
            blocks(wide),
            blocks(wide),
        ],
        in_specs=[VM, VM, VM, ANY, ANY, ANY, ANY],
        out_specs=[VM, VM, ANY, ANY, ANY],
        scratch_shapes=[
            pltpu.VMEM(wd.shape, BF16),
            pltpu.VMEM((2, rows, wide), BF16),
            pltpu.VMEM((n, rows, width), BF16),
            pltpu.VMEM((n + 1, rows, width), BF16),
            pltpu.VMEM((rows, width), F32),
            pltpu.VMEM((n, rows, width), BF16),
        ]
        + [pltpu.VMEM((2, rows, wide), BF16)] * 4
        + [pltpu.VMEM((8, width), F32)]
        + [pltpu.SemaphoreType.DMA((1,)), pltpu.SemaphoreType.DMA((1, 2))]
        + line_scratch(n) * 2
        + [
            pltpu.SemaphoreType.DMA((n,)),
            pltpu.SemaphoreType.DMA((2, 2)),
            pltpu.SemaphoreType.DMA((2, 2)),
        ],
        compiler_params=params(3, 62),
        cost_estimate=cost(0, 600 << 20),
        name="turn_feed",
    )(y, dout, gains, hid, wd, up, ge)


def out_of_feed_kernel(
    n, y, attn, dout, gains, dgate_hbm, dup_hbm, wg_hbm, wu_hbm, wo_hbm,
    dy_out, gain_out, dattn_full, do_out,
    wg, wu, wo, dg_s, du_s, part, landed, mine, held, do_s, fold,
    load, feed_sem, rs_send, rs_recv, ag_send, ag_recv, keep_sem, out_sem,
):
    i = lax.axis_index("tensor")
    rows, width = y.shape
    loads = [
        pltpu.make_async_copy(src, dst, load.at[k])
        for k, (src, dst) in enumerate(((wg_hbm, wg), (wu_hbm, wu), (wo_hbm, wo)))
    ]
    for c in loads:
        c.start()
    feed = Feed((dgate_hbm, dup_hbm), (dg_s, du_s), feed_sem, lambda s: block_at(i, n, n - 1 - s))
    feed.start(jnp.int32(0))
    line_barrier(i, n)
    loads[0].wait()
    loads[1].wait()

    def product(slot, at):
        return dot_nt(dg_s[slot], wg[at, :]) + dot_nt(du_s[slot], wu[at, :])

    def compute(t, block):
        feed.advance(t, n)
        slot = t % 2

        def tile(k):
            at = pl.ds(pl.multiple_of(k * TILE, TILE), TILE)
            part[block, :, at] = product(slot, at).astype(BF16)

        loop(width // TILE, tile)

    def own(t):
        t = jnp.int32(t)
        feed.advance(t, n)
        slot = t % 2

        def tile(k):
            at = pl.ds(pl.multiple_of(k * TILE, TILE), TILE)
            mine[:, at] = product(slot, at)

        loop(width // TILE, tile)

    done = scatter_line(i, n, part, landed, rs_send, rs_recv, compute, own)
    scale_two, scale_three = 1.0 + gains[1:2, :], 1.0 + gains[2:3, :]
    fold[...] = jnp.zeros_like(fold)

    def chunk(c):
        r = pl.ds(c * ROWS, ROWS)
        dh3 = summed_rows(i, n, mine, landed, r)
        v = y[r, :]
        inv = inverse_rms(v)
        dy = dout[r, :].astype(F32) + norm_back(dh3 * scale_three, v, inv)
        dy_out[r, :] = dy
        fold[1] += fold_rows(dh3 * (v * inv))
        a = attn[r, :]
        inv = inverse_rms(a)
        held[i, r, :] = norm_back(dy * scale_two, a, inv).astype(BF16)
        fold[0] += fold_rows(dy * (a * inv))

    loop(rows // ROWS, chunk)
    gain_out[0:1, :] = jnp.sum(fold[0], axis=0, keepdims=True)
    gain_out[1:2, :] = jnp.sum(fold[1], axis=0, keepdims=True)
    done()
    loads[2].wait()
    drain = Drain((do_out,), (do_s,), out_sem, lambda s: block_at(i, n, s))

    def backward(s, block):
        pltpu.make_async_copy(held.at[block], dattn_full.at[block], keep_sem.at[s]).start()
        drain.free(s)
        do_s[s % 2] = dot_nn(held[block], wo[...]).astype(BF16)
        drain.start(s)

    gather_line(i, n, held, ag_send, ag_recv, backward)
    drain.finish(n)

    def finish(s):
        block = block_at(i, n, s)
        pltpu.make_async_copy(held.at[block], dattn_full.at[block], keep_sem.at[s]).wait()

    loop(n, finish)


def out_of_feed(n, y, attn, dout, gains, dgate, dup, wg, wu, wo):
    rows, width = y.shape
    wide = wg.shape[1]
    narrow = wo.shape[1]
    return pl.pallas_call(
        functools.partial(out_of_feed_kernel, n),
        out_shape=[
            jax.ShapeDtypeStruct((rows, width), F32),
            jax.ShapeDtypeStruct((2, width), F32),
            jax.ShapeDtypeStruct((n, rows, width), BF16),
            jax.ShapeDtypeStruct((n, rows, narrow), BF16),
        ],
        in_specs=[VM, VM, VM, VM, ANY, ANY, ANY, ANY, ANY],
        out_specs=[VM, VM, ANY, ANY],
        scratch_shapes=[
            pltpu.VMEM(wg.shape, BF16),
            pltpu.VMEM(wu.shape, BF16),
            pltpu.VMEM(wo.shape, BF16),
            pltpu.VMEM((2, rows, wide), BF16),
            pltpu.VMEM((2, rows, wide), BF16),
            pltpu.VMEM((n, rows, width), BF16),
            pltpu.VMEM((n + 1, rows, width), BF16),
            pltpu.VMEM((rows, width), F32),
            pltpu.VMEM((n, rows, width), BF16),
            pltpu.VMEM((2, rows, narrow), BF16),
            pltpu.VMEM((2, 8, width), F32),
        ]
        + [pltpu.SemaphoreType.DMA((3,)), pltpu.SemaphoreType.DMA((2, 2))]
        + line_scratch(n) * 2
        + [pltpu.SemaphoreType.DMA((n,)), pltpu.SemaphoreType.DMA((1, 2))],
        compiler_params=params(4, 62),
        cost_estimate=cost(0, 600 << 20),
        name="out_of_feed",
    )(y, attn, dout, gains, dgate, dup, wg, wu, wo)


def last_kernel(
    n, x, dy, gains, d_hbm, w_hbm, in_grad, gain_out,
    d, w, part, landed, mine, fold, load, rs_send, rs_recv,
):
    i = lax.axis_index("tensor")
    rows, width = x.shape
    loads = [
        pltpu.make_async_copy(src, dst, load.at[k])
        for k, (src, dst) in enumerate(((d_hbm, d), (w_hbm, w)))
    ]
    for c in loads:
        c.start()
    line_barrier(i, n)
    for c in loads:
        c.wait()

    def compute(t, block):
        def tile(k):
            at = pl.ds(pl.multiple_of(k * TILE, TILE), TILE)
            part[block, :, at] = dot_nt(d[block], w[at, :]).astype(BF16)

        loop(width // TILE, tile)

    def own(t):
        def tile(k):
            at = pl.ds(pl.multiple_of(k * TILE, TILE), TILE)
            mine[:, at] = dot_nt(d[i], w[at, :])

        loop(width // TILE, tile)

    done = scatter_line(i, n, part, landed, rs_send, rs_recv, compute, own)
    scale = 1.0 + gains[0:1, :]
    fold[...] = jnp.zeros_like(fold)

    def chunk(c):
        r = pl.ds(c * ROWS, ROWS)
        dh1 = summed_rows(i, n, mine, landed, r)
        v = x[r, :].astype(F32)
        inv = inverse_rms(v)
        in_grad[r, :] = (dy[r, :] + norm_back(dh1 * scale, v, inv)).astype(BF16)
        fold[...] += fold_rows(dh1 * (v * inv))

    loop(rows // ROWS, chunk)
    gain_out[...] = jnp.sum(fold[...], axis=0, keepdims=True)
    done()


def last(n, x, dy, gains, d, w):
    rows, width = x.shape
    return pl.pallas_call(
        functools.partial(last_kernel, n),
        out_shape=[
            jax.ShapeDtypeStruct((rows, width), BF16),
            jax.ShapeDtypeStruct((1, width), F32),
        ],
        in_specs=[VM, VM, VM, ANY, ANY],
        out_specs=[VM, VM],
        scratch_shapes=[
            pltpu.VMEM(d.shape, BF16),
            pltpu.VMEM(w.shape, BF16),
            pltpu.VMEM((n, rows, width), BF16),
            pltpu.VMEM((n + 1, rows, width), BF16),
            pltpu.VMEM((rows, width), F32),
            pltpu.VMEM((8, width), F32),
            pltpu.SemaphoreType.DMA((2,)),
        ]
        + line_scratch(n),
        compiler_params=params(5, 48),
        cost_estimate=cost(0, 300 << 20),
        name="last",
    )(x, dy, gains, d, w)


def rope_tables():
    positions = jnp.arange(L, dtype=jnp.int32).astype(F32)
    exponent = jnp.arange(HD // 2, dtype=jnp.int32).astype(F32) * (-2.0 / HD)
    angles = positions[:, None] * jnp.exp(exponent * jnp.log(F32(10000.0)))[None, :]
    return jnp.cos(angles), jnp.sin(angles)


def weight_grad(left, right):
    return dot_tn(left, right).astype(BF16)


def scatter_rows(grad):
    return lax.psum_scatter(grad, "dp", scatter_dimension=0, tiled=True)


def body(
    n,
    m,
    layer_in,
    out_grad,
    piece_starts,
    attn_gain,
    attn_out_gain,
    feed_gain,
    feed_out_gain,
    query_weight,
    key_weight,
    value_weight,
    out_weight,
    gate_weight,
    up_weight,
    down_weight,
):
    heads = query_weight.shape[1] // HD
    fan = H // KV
    kvs = max(1, heads // fan)
    rank = lax.axis_index("tensor")
    kv_at = (rank * heads // fan) * HD
    rows, width = layer_in.shape
    tokens = n * rows

    gathered = gather_gains(m, jnp.stack([attn_gain, attn_out_gain, feed_gain, feed_out_gain]))
    gains = gathered.transpose(1, 0, 2).reshape(4, width).astype(F32)

    def collect(shard):
        return lax.all_gather(shard, "dp", axis=0, tiled=True)

    wqkv = collect(
        jnp.concatenate(
            [
                query_weight,
                lax.dynamic_slice_in_dim(key_weight, kv_at, kvs * HD, 1),
                lax.dynamic_slice_in_dim(value_weight, kv_at, kvs * HD, 1),
            ],
            axis=1,
        )
    )
    wo = collect(out_weight.T)
    wg = collect(gate_weight)
    wu = collect(up_weight)
    wd = collect(down_weight.T)
    cos, sin = rope_tables()

    h1 = first(n, layer_in, gains)
    h1_flat = h1.reshape(tokens, width)
    q, k, v, o = attend(heads, kvs, piece_starts, h1_flat, wqkv, cos, sin)
    attn, y, h3, hid, up, ge = into_feed(
        n, layer_in, gains, o.reshape(n, rows, heads * HD), wo, wg, wu
    )
    layer_out, gain_four, df, dgate, dup = turn_feed(n, y, out_grad, gains, hid, wd, up, ge)
    flat = lambda a: a.reshape(tokens, a.shape[-1])
    tie = lax.optimization_barrier
    down_part = weight_grad(flat(df), flat(hid))
    gate_part = weight_grad(flat(h3), flat(dgate))
    up_part = weight_grad(flat(h3), flat(dup))
    dgate, dup, down_part, gate_part, up_part = tie((dgate, dup, down_part, gate_part, up_part))
    down_sum, gate_sum, up_sum = map(scatter_rows, (down_part, gate_part, up_part))
    dy, gain_mid, dattn, do = out_of_feed(n, y, attn, out_grad, gains, dgate, dup, wg, wu, wo)
    do, dattn, down_sum, gate_sum = tie((do, dattn, down_sum, gate_sum))
    out_part = weight_grad(flat(dattn), o)
    do, out_part = tie((do, out_part))
    d = attend_back(heads, kvs, piece_starts, q, k, v, flat(do), cos, sin)
    qkv_part = weight_grad(h1_flat, d)
    d, qkv_part, up_sum = tie((d, qkv_part, up_sum))
    out_sum, qkv_sum = scatter_rows(out_part), scatter_rows(qkv_part)
    in_grad, gain_one = last(n, layer_in, dy, gains, d.reshape(n, rows, -1), wqkv)

    own_rows = qkv_sum.shape[0]
    split = heads * HD
    kv = qkv_sum[:, split:].reshape(own_rows, 2, kvs * HD).transpose(1, 0, 2)
    if n * kvs == KV:
        kv = lax.all_gather(kv, "tensor", axis=2, tiled=True)
    else:
        kv = lax.dynamic_update_slice_in_dim(jnp.zeros((2, own_rows, KV * HD), BF16), kv, kv_at, 2)
        kv = lax.psum(kv, "tensor")
    kv = kv.astype(F32)

    gain_grads = jnp.concatenate([gain_one, gain_mid, gain_four], axis=0)
    gain_grads = sum_gains(n, m, gain_grads.reshape(4, m, width // m).transpose(1, 0, 2))
    return (
        layer_out,
        in_grad,
        qkv_sum[:, :split].astype(F32),
        kv[0],
        kv[1],
        out_sum.astype(F32).T,
        gate_sum.astype(F32),
        up_sum.astype(F32),
        down_sum.astype(F32).T,
        gain_grads[0],
        gain_grads[1],
        gain_grads[2],
        gain_grads[3],
    )


def solution(mesh):
    in_specs = (
        P(("dp", "tensor"), None),
        P(("dp", "tensor"), None),
        P("dp", None),
        P("dp"),
        P("dp"),
        P("dp"),
        P("dp"),
        P("dp", "tensor"),
        P("dp", None),
        P("dp", None),
        P("tensor", "dp"),
        P("dp", "tensor"),
        P("dp", "tensor"),
        P("tensor", "dp"),
    )
    out_specs = (
        P(("dp", "tensor"), None),
        P(("dp", "tensor"), None),
        P("dp", "tensor"),
        P("dp", None),
        P("dp", None),
        P("tensor", "dp"),
        P("dp", "tensor"),
        P("dp", "tensor"),
        P("tensor", "dp"),
        P("dp"),
        P("dp"),
        P("dp"),
        P("dp"),
    )
    program = functools.partial(body, mesh.shape["tensor"], mesh.shape["dp"])
    return jax.shard_map(program, mesh=mesh, in_specs=in_specs, out_specs=out_specs, check_vma=False)
```

time: 2020 us -> 1080 us (0.53)
  waiting for transfers between devices: 1530 us -> 190 us
  Pallas kernels: 0 us -> 766 us
  matrix products: 308 us -> 67 us
  other arithmetic: 78.9 us -> 15.7 us
  blocking collectives: 38.2 us -> 0 us
    reduce_scatter x11 -> x5, waiting for transfers between devices: 872 us -> 95.2 us  [scatter_rows(): return lax.psum_scatter(grad, 'dp', scatter_dimension=0, tiled=True)]
    pallas_call x0 -> x9, Pallas kernels: none -> 766 us  [the longest x1 180 us: out_of_feed(): pl.pallas_call(functools.partial(out_of_feed_kernel, n), out_shape=[jax.S...]
    all_gather x11 -> x6, waiting for transfers between devices: 571 us -> 90.2 us  [the longest x5 90.2 us: collect(): return lax.all_gather(shard, 'dp', axis=0, tiled=True)]
    dot_general x33 -> x5, matrix products: 308 us -> 67 us  [dot_tn(): lax.dot_general(a, b, (((0,), (0,)), ((), ())), preferred_element_type=F32)]
    psum x1 -> x0, waiting for transfers between devices: 54.9 us -> none  [body(): lax.psum(key_place.astype(jnp.bfloat16), 'tensor').astype(jnp.float32)]
    unnamed x25 -> x11, waiting for transfers between devices: 36.6 us -> 4.42 us
    convert_element_type x17 -> x5, other arithmetic: 35.4 us -> 6.33 us  [the longest x1 3 us: body(): up_sum.astype(F32)]
    unnamed x1 -> x0, blocking collectives: 26.5 us -> none
  transfers between devices with their start and end apart: 24 -> 11, of which waited for: 22 -> 4; matrix products, arithmetic and copies ran while one was open for 11% -> 3% of each run, Pallas kernels for 0% -> 55%
where the time goes in v1:
time: 1080 us; the launch traced here: 1070 us
  Pallas kernels  766 us (71%)
  waiting for transfers between devices  190 us (18%)
  matrix products  67 us (6%)
  local copies, waits for them, and re-layouts  17.5 us (2%)
  other arithmetic  15.7 us (1%)
  between operations  14.6 us (1%)
    pallas_call x1, Pallas kernels, out_of_feed(): pl.pallas_call(functools.partial(out_of_feed_kernel, n), out_shape=[jax.S...  180 us
    pallas_call x1, Pallas kernels, into_feed(): pl.pallas_call(functools.partial(into_feed_kernel, n), out_shape=[mine, m...  180 us
    pallas_call x1, Pallas kernels, turn_feed(): pl.pallas_call(functools.partial(turn_feed_kernel, n), out_shape=[jax.Sha...  173 us
    pallas_call x1, Pallas kernels, last(): pl.pallas_call(functools.partial(last_kernel, n), out_shape=[jax.ShapeDty...  108 us
    reduce_scatter x5, waiting for transfers between devices, scatter_rows(): return lax.psum_scatter(grad, 'dp', scatter_dimension=0, tiled=True)  95.2 us
    all_gather x5, waiting for transfers between devices, collect(): return lax.all_gather(shard, 'dp', axis=0, tiled=True)  90.2 us
    pallas_call x1, Pallas kernels, first(): pl.pallas_call(functools.partial(first_kernel, n), out_shape=jax.ShapeDty...  84 us
    dot_general x5, matrix products, dot_tn(): lax.dot_general(a, b, (((0,), (0,)), ((), ())), preferred_element_type=F32)  67 us
  transfers between devices with their start and end apart: 11, of which 4 were waited for; matrix products, arithmetic and copies ran while one was open for 3% of the time, Pallas kernels for 55%

profile of v1, /device:TPU:0, one launch (start us, length us, event | category | flops | bytes accessed | tf_op | source)
XLA Modules:
  0.0 1071.2 jit_solution(3875534814358855192)
XLA Ops:
  8.4 1.9 pad_maximum_fusion
  13.1 6.3 gains.1
  19.6 84.0 %first.1 = bf16[4,256,2304]{2,1,0:T(8,128)(2,1)S(1)} custom-call(bf16[256,2304]{1,0:T(8,128)(2,1)S(1)} %copy-done, f32[4,2304]{1,0:T(4,128)S(1)} %reshape.73.gains), custom_call_target="tpu_custom_call" | custom-call | bytes 314572800 | tf_op jit(solution)/shard_map/first/pallas_call | solution.py:415
  103.6 2.1 copy-done.2
  105.7 1.9 multiply_sine_fusion
  107.6 13.1 %attend.1 = (bf16[2,1024,256]{2,1,0:T(8,128)(2,1)S(1)}, bf16[1,1024,256]{2,1,0:T(8,128)(2,1)S(1)}, bf16[1,1024,256]{2,1,0:T(8,128)(2,1)S(1)}, bf16[1024,512]{1,0:T(8,128)(2,1)S(1)}) custom-call(s32[1,2]{1,0:T(1,128)S(1)} %copy-done.13, bf16[1024,2304]{1,0:T(8,128)(2,1)} %bitcast.43, bf16[2304,1024]{1,0:T(8,128)(2,1)} %all-gather.7.cloned.1.call-done.w.w_hbm, ...), custom_call_target="tpu_custom_call" | custom-call | flops 21474836480 | bytes 20971520 | tf_op jit(solution)/shard_map/attend/pallas_call | solution.py:490
  124.3 24.6 %all-gather.11.cloned.1.call-done.wg_hbm = bf16[2304,2304]{1,0:T(8,128)(2,1)} async-done(((bf16[288,2304]{1,0:T(8,128)(2,1)}), bf16[2304,2304]{1,0:T(8,128)(2,1)}) %all-gather.11.cloned.1.call-update) | async-done | bytes 10616848 | tf_op jit(solution)/shard_map/all_gather | solution.py:1030
  148.8 65.6 %all-gather.13.cloned.1.call-done.wu_hbm = bf16[2304,2304]{1,0:T(8,128)(2,1)} async-done(((bf16[288,2304]{1,0:T(8,128)(2,1)}), bf16[2304,2304]{1,0:T(8,128)(2,1)}) %all-gather.13.cloned.1.call-update) | async-done | bytes 10616848 | tf_op jit(solution)/shard_map/all_gather | solution.py:1030
  214.4 180.1 %into_feed.1 = (f32[256,2304]{1,0:T(8,128)}, f32[256,2304]{1,0:T(8,128)}, bf16[4,256,2304]{2,1,0:T(8,128)(2,1)}, bf16[4,256,2304]{2,1,0:T(8,128)(2,1)}, bf16[4,2...) custom-call(bf16[256,2304]{1,0:T(8,128)(2,1)} %x.5, f32[4,2304]{1,0:T(4,128)} %copy-done.4, ...), custom_call_target="tpu_custom_call" | custom-call | bytes 629145600 | tf_op jit(solution)/shard_map/into_feed/pallas_call | solution.py:647
  394.6 173.1 %turn_feed.1 = (bf16[256,2304]{1,0:T(8,128)(2,1)}, f32[1,2304]{1,0:T(1,128)}, bf16[4,256,2304]{2,1,0:T(8,128)(2,1)}, bf16[4,256,2304]{2,1,0:T(8,128)(2,1)}, bf16[4,256,2304]{2,1,0:T(8,128)(2,1)}) custom-call(f32[256,2304]{1,0:T(8,128)} %get-tuple-element.49.y, bf16[256,2304]{1,0:T(8,128)(2,1)} %dout.3, f32[4,2304]{1,0:T(4,128)} %copy-done.4, ...), custom_call_target="tpu_custom_call" | custom-call | bytes 629145600 | tf_op jit(solution)/shard_map/turn_feed/pallas_call | solution.py:758
  567.8 16.9 %bitcast_convert_fusion.2 = bf16[2304,2304]{1,0:T(8,128)(2,1)} fusion(bf16[4,256,2304]{2,1,0:T(8,128)(2,1)} %get-tuple-element.57, bf16[4,256,2304]{2,1,0:T(8,128)(2,1)} %get-tuple-element.50.hid_hbm), kind=kOutput, calls=%fused_computation.2 | convolution fusion | flops 10876944384 | bytes 20054016 | tf_op jit(solution)/shard_map/dot_general | solution.py:37
  584.6 17.2 %bitcast_convert_fusion.1 = bf16[2304,2304]{1,0:T(8,128)(2,1)} fusion(bf16[4,256,2304]{2,1,0:T(8,128)(2,1)} %get-tuple-element.58, bf16[4,256,2304]{2,1,0:T(8,128)(2,1)} %get-tuple-element.59.dgate_hbm), kind=kOutput, calls=%fused_computation.1 | convolution fusion | flops 10876944384 | bytes 20054016 | tf_op jit(solution)/shard_map/dot_general | solution.py:37
  601.8 16.9 %bitcast_convert_fusion = bf16[2304,2304]{1,0:T(8,128)(2,1)} fusion(bf16[4,256,2304]{2,1,0:T(8,128)(2,1)} %get-tuple-element.58, bf16[4,256,2304]{2,1,0:T(8,128)(2,1)} %get-tuple-element.60.dup_hbm), kind=kOutput, calls=%fused_computation | convolution fusion | flops 10876944384 | bytes 20054016 | tf_op jit(solution)/shard_map/dot_general | solution.py:37
  620.3 180.1 %out_of_feed.1 = (f32[256,2304]{1,0:T(8,128)}, f32[2,2304]{1,0:T(2,128)}, bf16[4,256,2304]{2,1,0:T(8,128)(2,1)}, bf16[4,256,512]{2,1,0:T(8,128)(2,1)}) custom-call(f32[256,2304]{1,0:T(8,128)} %get-tuple-element.49.y, f32[256,2304]{1,0:T(8,128)} %get-tuple-element.54.attn, bf16[256,2304]{1,0:T(8,128)(2,1)} %dout.3, f32[4,2304]{1,0:T(4,128)} %copy-done.4, ...), custom_call_target="tpu_custom_call" | custom-call | bytes 629145600 | tf_op jit(solution)/shard_map/out_of_feed/pallas_call | solution.py:880
  800.5 7.5 convolution_convert_fusion.1
  812.5 10.3 attend_back.1
  822.8 8.6 convolution_convert_fusion
  831.4 38.4 %reduce-scatter.10.cloned.1.call-done = bf16[288,2304]{1,0:T(8,128)(2,1)} async-done(((bf16[2304,2304]{1,0:T(8,128)(2,1)}), bf16[288,2304]{1,0:T(8,128)(2,1)}) %reduce-scatter.10.cloned.1.call-update) | async-done | bytes 1327120 | tf_op jit(solution)/shard_map/reduce_scatter | solution.py:997
  870.5 56.7 %reduce-scatter.12.cloned.1.call-done = bf16[288,1024]{1,0:T(8,128)(2,1)} async-done(((bf16[2304,1024]{1,0:T(8,128)(2,1)}), bf16[288,1024]{1,0:T(8,128)(2,1)}) %reduce-scatter.12.cloned.1.call-update) | async-done | bytes 589840 | tf_op jit(solution)/shard_map/reduce_scatter | solution.py:997
  927.2 1.9 fusion
  929.9 108.1 %last.1 = (bf16[256,2304]{1,0:T(8,128)(2,1)S(1)}, f32[1,2304]{1,0:T(1,128)S(1)}) custom-call(bf16[256,2304]{1,0:T(8,128)(2,1)S(1)} %copy-done.1, f32[256,2304]{1,0:T(8,128)} %get-tuple-element.61.dy, f32[4,2304]{1,0:T(4,128)S(1)} %copy-done.5, bf16[4,256,1024]{2,1,0:T(8,128)(2,1)S(1)} %bitcast.47, bf16[2304,1024]{1,0:T(8,128)(2,1)} %all-gather.7.cloned.1.call-done.w.w_hbm), custom_call_target="tpu_custom_call" | custom-call | bytes 314572800 | tf_op jit(solution)/shard_map/last/pallas_call | solution.py:961
  1039.3 11.0 %sum_gains.1 = f32[4,288]{1,0:T(4,128)S(1)} custom-call(f32[8,4,288]{2,1,0:T(4,128)S(1)} %bitcast.49), custom_call_target="tpu_custom_call" | custom-call | tf_op jit(solution)/shard_map/sum_gains/pallas_call | solution.py:371
  1050.3 3.0 convert_element_type.75
  1057.2 1.9 convert_bitcast_fusion.1
  (113 shorter events, 25.4 us)
Async XLA Ops:
  7.2 12.3 %copy-start = (bf16[256,2304]{1,0:T(8,128)(2,1)S(1)}, bf16[256,2304]{1,0:T(8,128)(2,1)}, u32[]{:S(2)}) copy-start(bf16[256,2304]{1,0:T(8,128)(2,1)} %x.5) | copy-start | bytes 3538948
  7.2 100.4 %all-gather.7.cloned.1.call-start = ((), (), s32[]{:S(2)}) async-start(), calls=%async_computation.5 | async-start | bytes 5308416 | tf_op jit(solution)/shard_map/all_gather | solution.py:1030
  10.3 114.0 %all-gather.9.cloned.1.call-start = ((), (), s32[]{:S(2)}) async-start(), calls=%async_computation.6 | async-start | bytes 2654208 | tf_op jit(solution)/shard_map/all_gather | solution.py:1030
  11.0 137.8 %all-gather.11.cloned.1.call-start = ((), (), s32[]{:S(2)}) async-start(), calls=%async_computation.7 | async-start | bytes 11943936 | tf_op jit(solution)/shard_map/all_gather | solution.py:1030
  11.8 95.8 %copy-start.13 = (s32[1,2]{1,0:T(1,128)S(1)}, s32[1,2]{1,0:T(1,128)}, u32[]{:S(2)}) copy-start(s32[1,2]{1,0:T(1,128)} %starts.3) | copy-start | bytes 28
  11.8 202.7 %all-gather.13.cloned.1.call-start = ((), (), s32[]{:S(2)}) async-start(), calls=%async_computation.8 | async-start | bytes 11943936 | tf_op jit(solution)/shard_map/all_gather | solution.py:1030
  12.4 382.2 %all-gather.15.cloned.1.call-start = ((), (), s32[]{:S(2)}) async-start(), calls=%async_computation.9 | async-start | bytes 11943936 | tf_op jit(solution)/shard_map/all_gather | solution.py:1030
  12.9 787.5 %reduce-scatter.6.cloned.1.call-start = ((), (), s32[]{:S(2)}) async-start(), calls=%async_computation.10 | async-start | bytes 11943936 | tf_op jit(solution)/shard_map/reduce_scatter | solution.py:997
  19.5 101.2 %copy-start.4 = (f32[4,2304]{1,0:T(4,128)}, f32[4,2304]{1,0:T(4,128)S(1)}, u32[]{:S(2)}) copy-start(f32[4,2304]{1,0:T(4,128)S(1)} %reshape.73.gains) | copy-start | bytes 110596
  107.6 13.2 %copy-start.10 = (f32[1024,128]{1,0:T(8,128)}, f32[1024,128]{1,0:T(8,128)S(1)}, u32[]{:S(2)}) copy-start(f32[1024,128]{1,0:T(8,128)S(1)} %get-tuple-element.92.cos) | copy-start | bytes 1572868
  618.7 181.8 %reduce-scatter.8.cloned.1.call-start = ((), (), s32[]{:S(2)}) async-start(), calls=%async_computation.11 | async-start | bytes 11943936 | tf_op jit(solution)/shard_map/reduce_scatter | solution.py:997
  619.5 250.4 %reduce-scatter.10.cloned.1.call-start = ((), (), s32[]{:S(2)}) async-start(), calls=%async_computation.12 | async-start | bytes 11943936 | tf_op jit(solution)/shard_map/reduce_scatter | solution.py:997
  620.2 307.0 %reduce-scatter.12.cloned.1.call-start = ((), (), s32[]{:S(2)}) async-start(), calls=%async_computation.13 | async-start | bytes 5308416 | tf_op jit(solution)/shard_map/reduce_scatter | solution.py:997
  620.3 180.2 %copy-start.9 = (bf16[1024,512]{1,0:T(8,128)(2,1)S(1)}, bf16[1024,512]{1,0:T(8,128)(2,1)}, u32[]{:S(2)}) copy-start(bf16[1024,512]{1,0:T(8,128)(2,1)} %copy-done.8) | copy-start | bytes 3145732
  800.5 22.3 %slice-start = ((s8[4718592]{0:T(1024)(128)(4,1)}), s8[524288]{0:T(1024)(128)(4,1)S(1)}, s32[]{:S(2)}) async-start(s8[4718592]{0:T(1024)(128)(4,1)} %bitcast.44), calls=%async_computation.16 | async-start | bytes 1048576
  831.4 98.5 %copy-start.1 = (bf16[256,2304]{1,0:T(8,128)(2,1)S(1)}, bf16[256,2304]{1,0:T(8,128)(2,1)}, u32[]{:S(2)}) copy-start(bf16[256,2304]{1,0:T(8,128)(2,1)} %x.5) | copy-start | bytes 3538948
  831.4 98.5 %copy-start.3 = (bf16[1024,1024]{1,0:T(8,128)(2,1)S(1)}, bf16[1024,1024]{1,0:T(8,128)(2,1)}, u32[]{:S(2)}) copy-start(bf16[1024,1024]{1,0:T(8,128)(2,1)} %attend_back.1) | copy-start | bytes 6291460
  831.4 98.5 %copy-start.5 = (f32[4,2304]{1,0:T(4,128)S(1)}, f32[4,2304]{1,0:T(4,128)}, u32[]{:S(2)}) copy-start(f32[4,2304]{1,0:T(4,128)} %copy-done.4) | copy-start | bytes 110596
  869.9 187.4 %reduce-scatter.14.cloned.1.call-start = ((), (), s32[]{:S(2)}) async-start(), calls=%async_computation.15 | async-start | bytes 2654208 | tf_op jit(solution)/shard_map/reduce_scatter | solution.py:997
  870.4 188.7 %all-gather.17.cloned.1.call-start = ((), (), s32[]{:S(2)}) async-start(), calls=%async_computation.14 | async-start | bytes 1474560 | tf_op jit(solution)/shard_map/all_gather | solution.py:1076
  929.9 109.2 %copy-start.23 = (f32[2,2304]{1,0:T(2,128)S(1)}, f32[2,2304]{1,0:T(2,128)}, u32[]{:S(2)}) copy-start(f32[2,2304]{1,0:T(2,128)} %get-tuple-element.81) | copy-start | bytes 55300
  929.9 109.2 %copy-start.24 = (f32[1,2304]{1,0:T(1,128)S(1)}, f32[1,2304]{1,0:T(1,128)}, u32[]{:S(2)}) copy-start(f32[1,2304]{1,0:T(1,128)} %get-tuple-element.82) | copy-start | bytes 27652
  1039.1 14.2 %copy-start.21 = (bf16[288,2304]{1,0:T(8,128)(2,1)S(1)}, bf16[288,2304]{1,0:T(8,128)(2,1)}, u32[]{:S(2)}) copy-start(bf16[288,2304]{1,0:T(8,128)(2,1)} %reduce-scatter.8.cloned.1.call-done) | copy-start | bytes 3981316
  1039.1 16.4 %copy-start.20 = (bf16[288,2304]{1,0:T(8,128)(2,1)S(1)}, bf16[288,2304]{1,0:T(8,128)(2,1)}, u32[]{:S(2)}) copy-start(bf16[288,2304]{1,0:T(8,128)(2,1)} %reduce-scatter.6.cloned.1.call-done) | copy-start | bytes 3981316
  (18 other events, 61.7 us)
Sparse Core Ops, SparseCore 0:
  10.5 41.6 all-gather.6
  54.1 29.0 all-gather.8
  85.0 63.8 all-gather.10
  150.6 63.8 all-gather.12
  216.2 63.8 all-gather.14
  618.8 79.4 reduce-scatter.5
  701.8 82.2 reduce-scatter.7
  787.6 82.2 reduce-scatter.9
  873.3 53.8 reduce-scatter.11
  930.8 42.5 reduce-scatter.13
  975.6 48.2 all-gather.16

commit v2 on v1

--- a/solution.py
+++ b/solution.py
@@ -52,7 +52,7 @@
     return jnp.where(s <= 2 * m, near, far)
 
 
-def line_barrier(i, n):
+def line_barrier(i, n, peers=()):
     barrier = pltpu.get_barrier_semaphore()
 
     @pl.when(i > 0)
@@ -63,7 +63,9 @@
     def _():
         pl.semaphore_signal(barrier, 1, device_id={"tensor": i + 1}, device_id_type=MESH)
 
-    pl.semaphore_wait(barrier, jnp.minimum(i, 1) + jnp.minimum(n - 1 - i, 1))
+    for peer in peers:
+        pl.semaphore_signal(barrier, 1, device_id={"dp": peer}, device_id_type=MESH)
+    pl.semaphore_wait(barrier, len(peers) + jnp.minimum(i, 1) + jnp.minimum(n - 1 - i, 1))
 
 
 def gather_line(i, n, held, send, recv, compute):
@@ -116,7 +118,7 @@
     loop(n, finish)
 
 
-def scatter_line(i, n, part, landed, send, recv, compute, own):
+def scatter_steps(i, n, part, landed, send, recv, compute):
     rows = part.shape[1]
 
     def copy(block, way, t, to):
@@ -173,29 +175,35 @@
         def _():
             copy(below, 1, t, down).start()
 
+    def land():
+        @pl.when(i > 0)
+        def _():
+            arrived(i)
+
+        @pl.when(i < n - 1)
+        def _():
+            arrived(jnp.int32(n))
+
+    def finish(k):
+        t = k + 1
+
+        @pl.when(i + n - t < n)
+        def _():
+            copy(i + n - t, 0, t, up).wait_send()
+
+        @pl.when(i - n + t >= 0)
+        def _():
+            copy(i - n + t, 1, t, down).wait_send()
+
+    return step, land, functools.partial(loop, n - 1, finish)
+
+
+def scatter_line(i, n, part, landed, send, recv, compute, own):
+    step, land, finish = scatter_steps(i, n, part, landed, send, recv, compute)
     loop(n - 1, step)
     own(n - 1)
-
-    @pl.when(i > 0)
-    def _():
-        arrived(i)
-
-    @pl.when(i < n - 1)
-    def _():
-        arrived(jnp.int32(n))
-
-    def finish(k):
-        t = k + 1
-
-        @pl.when(i + n - t < n)
-        def _():
-            copy(i + n - t, 0, t, up).wait_send()
-
-        @pl.when(i - n + t >= 0)
-        def _():
-            copy(i - n + t, 1, t, down).wait_send()
-
-    return functools.partial(loop, n - 1, finish)
+    land()
+    return finish
 
 
 def summed_rows(i, n, mine, landed, r):
@@ -268,6 +276,97 @@
         for s in range(max(0, count - 2), count):
             for c in self.copies(jnp.int32(s)):
                 c.wait()
+
+
+class Spread:
+    sems = 8
+
+    def __init__(self, own, full, send, recv, local):
+        me = lax.axis_index("dp")
+        c, x, y = me % 2, (me // 2) % 2, me // 4
+        self.own, self.full, self.send, self.recv, self.local = own, full, send, recv, local
+        self.me = me
+        self.core = me + 1 - 2 * c
+        self.x = me + 2 - 4 * x
+        self.y = me + 4 - 8 * y
+        self.far = self.x + 4 - 8 * y
+        self.flip = 1 - 2 * c
+
+    def peers(self):
+        return (self.core, self.x, self.y)
+
+    def rows(self, part):
+        count = self.full.shape[1]
+        half = count // 2
+        return pl.ds(*{0: (0, count), 1: (0, half), 2: (half, half)}[part])
+
+    def copy(self, k, source, owner, part, to):
+        r = self.rows(part)
+        return pltpu.make_async_remote_copy(
+            self.own.at[r] if source is None else self.full.at[source, r],
+            self.full.at[owner, r],
+            self.send.at[k],
+            self.recv.at[k],
+            device_id={"dp": to},
+            device_id_type=MESH,
+        )
+
+    def sends(self):
+        return (
+            (0, None, self.me, 0, self.core),
+            (1, None, self.me, 0, self.x),
+            (2, None, self.me, 0, self.y),
+            (3, self.x, self.x, 1, self.y),
+            (4, self.y, self.y, 2, self.x),
+            (5, self.x, self.x, 0, self.core),
+            (6, self.y, self.y, 0, self.core),
+            (7, self.far, self.far, 0, self.core),
+        )
+
+    def start(self, *which):
+        for k in which:
+            self.copy(*self.sends()[k]).start()
+
+    def arrive(self, k):
+        owner, part = {
+            0: (self.core, 0),
+            1: (self.x, 0),
+            2: (self.y, 0),
+            3: (self.far, 1),
+            4: (self.far, 2),
+            5: (self.x + self.flip, 0),
+            6: (self.y + self.flip, 0),
+            7: (self.far + self.flip, 0),
+        }[k]
+        self.copy(k, owner, owner, part, self.core).wait_recv()
+
+    def keep(self):
+        return pltpu.make_async_copy(self.own, self.full.at[self.me], self.local.at[0])
+
+    def begin(self):
+        self.keep().start()
+        self.start(1, 2, 0)
+
+    def middle(self):
+        self.arrive(1)
+        self.arrive(2)
+        self.start(3, 4, 5, 6)
+
+    def turn(self):
+        self.arrive(3)
+        self.arrive(4)
+        self.start(7)
+
+    def end(self):
+        for k in (0, 5, 6, 7):
+            self.arrive(k)
+        self.keep().wait()
+        for k in range(8):
+            self.copy(*self.sends()[k]).wait_send()
+
+
+def spread_scratch():
+    return [pltpu.SemaphoreType.DMA((8,)), pltpu.SemaphoreType.DMA((8,)), pltpu.SemaphoreType.DMA((1,))]
 
 
 def line_scratch(n):
@@ -385,10 +484,17 @@
     )(mine)
 
 
-def first_kernel(n, x, gains, full, held, send, recv, out_sem):
+def first_kernel(n, spread, x, gains, *refs):
     i = lax.axis_index("tensor")
     rows = x.shape[0]
-    line_barrier(i, n)
+    if spread:
+        shard, full, gathered, held, send, recv, out_sem, *sems = refs
+        gather = Spread(shard, gathered, *sems)
+        line_barrier(i, n, gather.peers())
+        gather.begin()
+    else:
+        full, held, send, recv, out_sem = refs
+        line_barrier(i, n)
     scale = 1.0 + gains[0:1, :]
 
     def chunk(c):
@@ -400,6 +506,9 @@
 
     def keep(s, block):
         pltpu.make_async_copy(held.at[block], full.at[block], out_sem.at[s]).start()
+        if spread:
+            pl.when(s == min(1, n - 1))(gather.middle)
+            pl.when(s == min(2, n - 1))(gather.turn)
 
     gather_line(i, n, held, send, recv, keep)
 
@@ -408,22 +517,30 @@
         pltpu.make_async_copy(held.at[block], full.at[block], out_sem.at[s]).wait()
 
     loop(n, finish)
-
-
-def first(n, x, gains):
+    if spread:
+        gather.end()
+
+
+def first(n, m, x, gains, shard):
     rows, width = x.shape
-    return pl.pallas_call(
-        functools.partial(first_kernel, n),
-        out_shape=jax.ShapeDtypeStruct((n, rows, width), BF16),
-        in_specs=[VM, VM],
-        out_specs=ANY,
+    spread = shard is not None
+    outs = [jax.ShapeDtypeStruct((n, rows, width), BF16)]
+    if spread:
+        outs += [jax.ShapeDtypeStruct((m,) + shard.shape, BF16)]
+    out = pl.pallas_call(
+        functools.partial(first_kernel, n, spread),
+        out_shape=outs,
+        in_specs=[VM, VM] + [ANY] * spread,
+        out_specs=[ANY] + [ANY] * spread,
         scratch_shapes=[pltpu.VMEM((n, rows, width), BF16)]
         + line_scratch(n)
-        + [pltpu.SemaphoreType.DMA((n,))],
+        + [pltpu.SemaphoreType.DMA((n,))]
+        + (spread_scratch() if spread else []),
         compiler_params=params(1, 32),
         cost_estimate=cost(0, 300 << 20),
         name="first",
-    )(x, gains)
+    )(x, gains, *([shard] if spread else []))
+    return (out[0], out[1].reshape(-1, shard.shape[1])) if spread else (out[0], None)
 
 
 def turn(u, cos, sin):
@@ -556,23 +673,37 @@
     )(starts, q, k, v, do, cos, sin)
 
 
-def into_feed_kernel(
-    n, x, gains, o_hbm, wo_hbm, wg_hbm, wu_hbm,
-    attn_out, y_out, h3_full, hid_out, up_out, ge_out,
-    o, wo, wg, wu, part, landed, mine, held, hid_s, up_s, ge_s,
-    load, rs_send, rs_recv, ag_send, ag_recv, keep_sem, out_sem,
-):
+def into_feed_kernel(n, spread, x, gains, o_hbm, wo_hbm, wg_hbm, wu_hbm, *refs):
+    attn_out, y_out, h3_full, hid_out, up_out, ge_out, *refs = refs
+    if spread:
+        wu_full, *refs = refs
+        *refs, token, spread_send, spread_recv, spread_local = refs
+    (
+        o, wo, wg, wu, part, landed, mine, held, hid_s, up_s, ge_s,
+        load, rs_send, rs_recv, ag_send, ag_recv, keep_sem, out_sem,
+    ) = refs
     i = lax.axis_index("tensor")
     rows, width = x.shape
-    loads = [
-        pltpu.make_async_copy(src, dst, load.at[k])
-        for k, (src, dst) in enumerate(((o_hbm, o), (wo_hbm, wo), (wg_hbm, wg), (wu_hbm, wu)))
-    ]
+    pairs = [(o_hbm, o), (wo_hbm, wo), (wg_hbm, wg)] + ([] if spread else [(wu_hbm, wu)])
+    loads = [pltpu.make_async_copy(src, dst, load.at[k]) for k, (src, dst) in enumerate(pairs)]
     for c in loads:
         c.start()
-    line_barrier(i, n)
+    if spread:
+        gather = Spread(wu_hbm, wu_full, spread_send, spread_recv, spread_local)
+        core = lax.axis_index("dp") % 2
+        line_barrier(i, n, gather.peers())
+        gather.begin()
+    else:
+        line_barrier(i, n)
     loads[0].wait()
     loads[1].wait()
+    if spread:
+
+        @pl.when(core == 1)
+        def _():
+            gather.middle()
+            gather.turn()
+            pl.semaphore_wait(token, 1)
 
     def compute(t, block):
         def tile(k):
@@ -589,6 +720,13 @@
         loop(width // TILE, tile)
 
     done = scatter_line(i, n, part, landed, rs_send, rs_recv, compute, own)
+    if spread:
+
+        @pl.when(core == 0)
+        def _():
+            pl.semaphore_signal(token, 1, device_id={"dp": gather.core}, device_id_type=MESH)
+            gather.middle()
+
     scale_two, scale_three = 1.0 + gains[1:2, :], 1.0 + gains[2:3, :]
 
     def chunk(c):
@@ -601,8 +739,18 @@
 
     loop(rows // ROWS, chunk)
     done()
-    loads[2].wait()
-    loads[3].wait()
+    if spread:
+        pl.when(core == 0)(gather.turn)
+        gather.end()
+        size = wu_hbm.shape[0]
+        loads += [
+            pltpu.make_async_copy(wu_full.at[k], wu.at[pl.ds(k * size, size)], load.at[3 + k])
+            for k in range(wu_full.shape[0])
+        ]
+        for c in loads[3:]:
+            c.start()
+    for c in loads[2:]:
+        c.wait()
     drain = Drain(
         (hid_out, up_out, ge_out), (hid_s, up_s, ge_s), out_sem, lambda s: block_at(i, n, s)
     )
@@ -639,30 +787,33 @@
     loop(n, finish)
 
 
-def into_feed(n, x, gains, o, wo, wg, wu):
+def into_feed(n, m, spread, x, gains, o, wo, wg, wu):
     rows, width = x.shape
     wide = wg.shape[1]
     blocks = lambda w: jax.ShapeDtypeStruct((n, rows, w), BF16)
     mine = jax.ShapeDtypeStruct((rows, width), F32)
+    outs = [mine, mine, blocks(width), blocks(wide), blocks(wide), blocks(wide)]
+    outs += [jax.ShapeDtypeStruct((m,) + wu.shape, BF16)] * spread
     return pl.pallas_call(
-        functools.partial(into_feed_kernel, n),
-        out_shape=[mine, mine, blocks(width), blocks(wide), blocks(wide), blocks(wide)],
+        functools.partial(into_feed_kernel, n, spread),
+        out_shape=outs,
         in_specs=[VM, VM, ANY, ANY, ANY, ANY],
-        out_specs=[VM, VM, ANY, ANY, ANY, ANY],
+        out_specs=[VM, VM] + [ANY] * (len(outs) - 2),
         scratch_shapes=[
             pltpu.VMEM(o.shape, BF16),
             pltpu.VMEM(wo.shape, BF16),
             pltpu.VMEM(wg.shape, BF16),
-            pltpu.VMEM(wu.shape, BF16),
+            pltpu.VMEM(wg.shape, BF16),
             pltpu.VMEM((n, rows, width), BF16),
             pltpu.VMEM((n + 1, rows, width), BF16),
             pltpu.VMEM((rows, width), F32),
             pltpu.VMEM((n, rows, width), BF16),
         ]
         + [pltpu.VMEM((2, rows, wide), BF16)] * 3
-        + [pltpu.SemaphoreType.DMA((4,))]
+        + [pltpu.SemaphoreType.DMA((3 + m,))]
         + line_scratch(n) * 2
-        + [pltpu.SemaphoreType.DMA((n,)), pltpu.SemaphoreType.DMA((3, 2))],
+        + [pltpu.SemaphoreType.DMA((n,)), pltpu.SemaphoreType.DMA((3, 2))]
+        + ([pltpu.SemaphoreType.REGULAR] + spread_scratch() if spread else []),
         compiler_params=params(2, 62),
         cost_estimate=cost(0, 600 << 20),
         name="into_feed",
@@ -982,6 +1133,368 @@
     )(x, dy, gains, d, w)
 
 
+class Reduce:
+    def __init__(self, u, left, right, column, width, bufs, sems):
+        me = lax.axis_index("dp")
+        c, x, y = me % 2, (me // 2) % 2, me // 4
+        self.me, self.set, self.third, self.fifth, self.width = me, u % 2, u % 3, u % 5, width
+        self.left, self.right, self.column = left, right, column
+        self.dx, self.dy, self.dc = 2 - 4 * x, 4 - 8 * y, 1 - 2 * c
+        self.lefts, self.rights, self.pair, self.pair_in, self.sums, self.far_in, self.xy_in, self.own = bufs
+        (
+            self.left_sem, self.right_sem, self.pair_send, self.pair_recv,
+            self.far_send, self.far_recv, self.xy_send, self.xy_recv,
+        ) = sems
+        self.rows = self.own.shape[1]
+        self.cols = pl.ds(0, width)
+        self.top = pl.ds(0, self.rows // 2)
+        self.low = pl.ds(self.rows // 2, self.rows // 2)
+
+    def owner(self, q):
+        k = q % 4
+        x = jnp.where(k <= 1, self.dx, 0)
+        y = jnp.where(k % 2 == 0, self.dy, 0)
+        return self.me + x + jnp.where(k == 3, 0, y) + jnp.where(q < 4, self.dc, 0)
+
+    def left_copy(self, q):
+        r = pl.ds(self.owner(q) * self.rows, self.rows)
+        return pltpu.make_async_copy(self.left.at[r], self.lefts.at[q % 2], self.left_sem.at[q % 2])
+
+    def right_copy(self):
+        return pltpu.make_async_copy(
+            self.right.at[:, pl.ds(self.column, self.width)],
+            self.rights.at[self.set, :, self.cols],
+            self.right_sem.at[self.set],
+        )
+
+    def remote(self, src, dst, send, recv, shift):
+        return pltpu.make_async_remote_copy(
+            src, dst, send, recv, device_id={"dp": self.me + shift}, device_id_type=MESH
+        )
+
+    def pair_copy(self, k):
+        return self.remote(
+            self.pair.at[self.set, k, :, self.cols],
+            self.pair_in.at[self.set, k, :, self.cols],
+            self.pair_send.at[self.set, k],
+            self.pair_recv.at[self.set, k],
+            self.dc,
+        )
+
+    def far_copy(self, way):
+        return self.remote(
+            self.sums.at[self.third, 0, (self.top, self.low)[way], self.cols],
+            self.far_in.at[self.third, way, :, self.cols],
+            self.far_send.at[self.third, way],
+            self.far_recv.at[self.third, way],
+            (self.dx, self.dy)[way],
+        )
+
+    def xy_copy(self, way, half):
+        r = (self.top, self.low)[half]
+        return self.remote(
+            self.sums.at[self.third, 1 + way, r, self.cols],
+            self.xy_in.at[self.fifth, way, r, self.cols],
+            self.xy_send.at[self.third, way, half],
+            self.xy_recv.at[self.fifth, way, half],
+            (self.dx, self.dy)[way],
+        )
+
+    def product(self, q, put):
+        self.left_copy(q).wait()
+        if isinstance(q, int):
+            if q < 7:
+                self.left_copy(q + 1).start()
+        else:
+            self.left_copy(q + 1).start()
+        tile = next(t for t in (384, 256, 128) if self.width % t == 0)
+
+        def one(t):
+            at = pl.ds(pl.multiple_of(t * tile, tile), tile)
+            put(at, dot_nn(self.lefts[q % 2], self.rights[self.set, :, at]))
+
+        loop(self.width // tile, one)
+
+    def load(self):
+        self.right_copy().start()
+
+    def begin(self):
+        self.left_copy(0).start()
+        self.right_copy().wait()
+
+        def chunk(k):
+            def put(at, value):
+                self.pair[self.set, k, :, at] = value.astype(BF16)
+
+            self.product(k, put)
+            self.pair_copy(k).start()
+
+        loop(4, chunk)
+
+    def middle(self):
+        for k in range(4):
+            arrived = []
+
+            def put(at, value, k=k):
+                total = value + self.pair_in[self.set, k, :, at].astype(F32)
+                if k < 3:
+                    self.sums[self.third, k, :, at] = total.astype(BF16)
+                else:
+                    self.own[self.third, :, at] = total
+
+            self.pair_copy(k).wait_recv()
+            self.product(4 + k, put)
+            if k == 0:
+                self.far_copy(0).start()
+                self.far_copy(1).start()
+            elif k == 1:
+                self.xy_copy(0, 0).start()
+            elif k == 2:
+                self.xy_copy(1, 1).start()
+        for k in range(4):
+            self.pair_copy(k).wait_send()
+
+    def turn(self):
+        self.far_copy(0).wait_recv()
+        self.far_copy(1).wait_recv()
+        half = self.rows // 2
+
+        def chunk(c):
+            for way, first in ((0, 0), (1, half)):
+                r = pl.ds(first + c * ROWS, ROWS)
+                f = pl.ds(c * ROWS, ROWS)
+                k = 2 - way
+                total = self.sums[self.third, k, r, self.cols].astype(F32)
+                total += self.far_in[self.third, way, f, self.cols].astype(F32)
+                self.sums[self.third, k, r, self.cols] = total.astype(BF16)
+
+        loop(half // ROWS, chunk)
+        self.xy_copy(0, 1).start()
+        self.xy_copy(1, 0).start()
+
+    def end(self, put):
+        for way in range(2):
+            for half in range(2):
+                self.xy_copy(way, half).wait_recv()
+
+        def chunk(c):
+            r = pl.ds(c * ROWS, ROWS)
+            total = self.own[self.third, r, self.cols]
+            for way in range(2):
+                total += self.xy_in[self.fifth, way, r, self.cols].astype(F32)
+            put(r, total)
+
+        loop(self.rows // ROWS, chunk)
+        for way in range(2):
+            self.far_copy(way).wait_send()
+            for half in range(2):
+                self.xy_copy(way, half).wait_send()
+
+
+def reduce_scratch(rows, tokens, widest):
+    sem = pltpu.SemaphoreType.DMA
+    bufs = [
+        pltpu.VMEM((2, rows, tokens), BF16),
+        pltpu.VMEM((2, tokens, widest), BF16),
+        pltpu.VMEM((2, 4, rows, widest), BF16),
+        pltpu.VMEM((2, 4, rows, widest), BF16),
+        pltpu.VMEM((3, 3, rows, widest), BF16),
+        pltpu.VMEM((3, 2, rows // 2, widest), BF16),
+        pltpu.VMEM((5, 2, rows, widest), BF16),
+        pltpu.VMEM((3, rows, widest), F32),
+    ]
+    sems = [
+        sem((2,)), sem((2,)), sem((2, 4)), sem((2, 4)),
+        sem((3, 2)), sem((3, 2)), sem((3, 2, 2)), sem((5, 2, 2)),
+    ]
+    return bufs, sems
+
+
+def halves(width):
+    return [(0, width)] if width <= 1280 else [(0, width // 2), (width // 2, width // 2)]
+
+
+def tail_kernel(n, split, x, dy, gains, d_hbm, w_hbm, *refs):
+    lefts, rights, refs = refs[:4], refs[4:9], refs[9:]
+    in_grad, gain_out, *outs = refs[:7]
+    kv_out, refs = refs[7], refs[8:]
+    d, w, part, landed, mine, fold, stage, kv_stage = refs[:8]
+    load, rs_send, rs_recv, out_sem, kv_sem, kv_send, kv_recv = refs[8:15]
+    bufs, sems = refs[15:23], refs[23:31]
+    h1_t, df_t, h3_t, da_t = lefts
+    dqkv, hid, dgate, dup, o = rights
+    i = lax.axis_index("tensor")
+    rows, width = x.shape
+    loads = [
+        pltpu.make_async_copy(src, dst, load.at[k])
+        for k, (src, dst) in enumerate(((d_hbm, d), (w_hbm, w)))
+    ]
+    for c in loads:
+        c.start()
+
+    pairs = [(h1_t, dqkv), (df_t, hid), (h3_t, dgate), (h3_t, dup), (da_t, o)]
+    units, places = [], []
+    for k, (left, right) in enumerate(pairs):
+        for column, size in halves(right.shape[1]):
+            units.append(Reduce(len(units), left, right, column, size, bufs, sems))
+            places.append((k, column, size))
+    units[0].load()
+    me = units[0].me
+
+    barrier = pltpu.get_barrier_semaphore()
+    for shift in (units[0].dc, units[0].dx, units[0].dy):
+        pl.semaphore_signal(barrier, 1, device_id={"dp": me + shift}, device_id_type=MESH)
+    for k in range(1, n):
+        peer = lax.rem(i + k, n)
+        pl.semaphore_signal(barrier, 1, device_id={"tensor": peer}, device_id_type=MESH)
+    pl.semaphore_wait(barrier, n + 2)
+    for c in loads:
+        c.wait()
+
+    def compute(t, block):
+        def tile(k):
+            at = pl.ds(pl.multiple_of(k * TILE, TILE), TILE)
+            part[block, :, at] = dot_nt(d[block], w[at, :]).astype(BF16)
+
+        loop(width // TILE, tile)
+
+    step, land, done = scatter_steps(i, n, part, landed, rs_send, rs_recv, compute)
+
+    def input_rows():
+        def tile(k):
+            at = pl.ds(pl.multiple_of(k * TILE, TILE), TILE)
+            mine[:, at] = dot_nt(d[i], w[at, :])
+
+        loop(width // TILE, tile)
+
+    def input_grad():
+        land()
+        scale = 1.0 + gains[0:1, :]
+        fold[...] = jnp.zeros_like(fold)
+
+        def chunk(c):
+            r = pl.ds(c * ROWS, ROWS)
+            dh1 = summed_rows(i, n, mine, landed, r)
+            v = x[r, :].astype(F32)
+            inv = inverse_rms(v)
+            in_grad[r, :] = (dy[r, :] + norm_back(dh1 * scale, v, inv)).astype(BF16)
+            fold[...] += fold_rows(dh1 * (v * inv))
+
+        loop(rows // ROWS, chunk)
+        gain_out[...] = jnp.sum(fold[...], axis=0, keepdims=True)
+        done()
+
+    def out_copy(u):
+        k, column, size = places[u]
+        return pltpu.make_async_copy(
+            stage.at[u % 2, :, pl.ds(0, size)],
+            outs[k].at[:, pl.ds(column, size)],
+            out_sem.at[u % 2],
+        )
+
+    def kv_copy(k):
+        return pltpu.make_async_remote_copy(
+            kv_stage,
+            kv_out.at[i],
+            kv_send.at[k],
+            kv_recv.at[k],
+            device_id={"tensor": lax.rem(i + k, n)},
+            device_id_type=MESH,
+        )
+
+    def kv_arrival(k):
+        from_peer = lax.rem(i + n - k, n)
+        return pltpu.make_async_remote_copy(
+            kv_stage,
+            kv_out.at[from_peer],
+            kv_send.at[k],
+            kv_recv.at[k],
+            device_id={"tensor": from_peer},
+            device_id_type=MESH,
+        )
+
+    kv_own = pltpu.make_async_copy(kv_stage, kv_out.at[i], kv_sem.at[0])
+
+    def finish(u):
+        if u >= 2:
+            out_copy(u - 2).wait()
+        size = places[u][2]
+
+        def put(r, total):
+            stage[u % 2, r, pl.ds(0, size)] = total
+            if u == 0:
+                kv_stage[r, :] = total[:, split:].astype(BF16)
+
+        units[u].end(put)
+        out_copy(u).start()
+        if u == 0:
+            for k in range(1, n):
+                kv_copy(k).start()
+            kv_own.start()
+
+    count = len(units)
+    line = [functools.partial(step, jnp.int32(k)) for k in range(n - 1)] + [input_rows, input_grad]
+    for u in range(count + 2):
+        if u < count:
+            units[u].begin()
+            if u + 1 < count:
+                units[u + 1].load()
+            units[u].middle()
+        if 1 <= u <= count:
+            units[u - 1].turn()
+        if u >= 2:
+            finish(u - 2)
+        if u < len(line):
+            line[u]()
+    for u in range(count + 2, len(line)):
+        line[u]()
+    for u in range(max(0, count - 2), count):
+        out_copy(u).wait()
+    kv_own.wait()
+    for k in range(1, n):
+        kv_copy(k).wait_send()
+        kv_arrival(k).wait_recv()
+
+
+def tail(n, m, split, x, dy, gains, d, w, lefts, rights):
+    rows, width = x.shape
+    tokens = n * rows
+    own_rows = width // m
+    widest = max(size for right in rights for _, size in halves(right.shape[1]))
+    bufs, sems = reduce_scratch(own_rows, tokens, widest)
+    sem = pltpu.SemaphoreType.DMA
+    kv_width = rights[0].shape[1] - split
+    return pl.pallas_call(
+        functools.partial(tail_kernel, n, split),
+        out_shape=[
+            jax.ShapeDtypeStruct((rows, width), BF16),
+            jax.ShapeDtypeStruct((1, width), F32),
+        ]
+        + [jax.ShapeDtypeStruct((own_rows, right.shape[1]), F32) for right in rights]
+        + [jax.ShapeDtypeStruct((n, own_rows, kv_width), BF16)],
+        in_specs=[VM, VM, VM] + [ANY] * 11,
+        out_specs=[VM, VM] + [ANY] * 6,
+        scratch_shapes=[
+            pltpu.VMEM(d.shape, BF16),
+            pltpu.VMEM(w.shape, BF16),
+            pltpu.VMEM((n, rows, width), BF16),
+            pltpu.VMEM((n + 1, rows, width), BF16),
+            pltpu.VMEM((rows, width), F32),
+            pltpu.VMEM((8, width), F32),
+            pltpu.VMEM((2, own_rows, widest), F32),
+            pltpu.VMEM((own_rows, kv_width), BF16),
+            sem((2,)),
+        ]
+        + line_scratch(n)
+        + [sem((2,)), sem((1,)), sem((n,)), sem((n,))]
+        + bufs
+        + sems,
+        compiler_params=params(7, 62),
+        cost_estimate=cost(0, 600 << 20),
+        name="tail",
+    )(x, dy, gains, d, w, *lefts, *rights)
+
+
 def rope_tables():
     positions = jnp.arange(L, dtype=jnp.int32).astype(F32)
     exponent = jnp.arange(HD // 2, dtype=jnp.int32).astype(F32) * (-2.0 / HD)
@@ -1040,43 +1553,58 @@
         )
     )
     wo = collect(out_weight.T)
-    wg = collect(gate_weight)
-    wu = collect(up_weight)
     wd = collect(down_weight.T)
     cos, sin = rope_tables()
 
-    h1 = first(n, layer_in, gains)
+    spread = m == 8
+    h1, wg = first(n, m, layer_in, gains, gate_weight if spread else None)
+    if not spread:
+        wg = collect(gate_weight)
     h1_flat = h1.reshape(tokens, width)
     q, k, v, o = attend(heads, kvs, piece_starts, h1_flat, wqkv, cos, sin)
-    attn, y, h3, hid, up, ge = into_feed(
-        n, layer_in, gains, o.reshape(n, rows, heads * HD), wo, wg, wu
+    wu = up_weight if spread else collect(up_weight)
+    attn, y, h3, hid, up, ge, *wu_full = into_feed(
+        n, m, spread, layer_in, gains, o.reshape(n, rows, heads * HD), wo, wg, wu
     )
+    if spread:
+        wu = wu_full[0].reshape(wg.shape)
     layer_out, gain_four, df, dgate, dup = turn_feed(n, y, out_grad, gains, hid, wd, up, ge)
     flat = lambda a: a.reshape(tokens, a.shape[-1])
-    tie = lax.optimization_barrier
-    down_part = weight_grad(flat(df), flat(hid))
-    gate_part = weight_grad(flat(h3), flat(dgate))
-    up_part = weight_grad(flat(h3), flat(dup))
-    dgate, dup, down_part, gate_part, up_part = tie((dgate, dup, down_part, gate_part, up_part))
-    down_sum, gate_sum, up_sum = map(scatter_rows, (down_part, gate_part, up_part))
-    dy, gain_mid, dattn, do = out_of_feed(n, y, attn, out_grad, gains, dgate, dup, wg, wu, wo)
-    do, dattn, down_sum, gate_sum = tie((do, dattn, down_sum, gate_sum))
-    out_part = weight_grad(flat(dattn), o)
-    do, out_part = tie((do, out_part))
-    d = attend_back(heads, kvs, piece_starts, q, k, v, flat(do), cos, sin)
-    qkv_part = weight_grad(h1_flat, d)
-    d, qkv_part, up_sum = tie((d, qkv_part, up_sum))
-    out_sum, qkv_sum = scatter_rows(out_part), scatter_rows(qkv_part)
-    in_grad, gain_one = last(n, layer_in, dy, gains, d.reshape(n, rows, -1), wqkv)
-
-    own_rows = qkv_sum.shape[0]
     split = heads * HD
-    kv = qkv_sum[:, split:].reshape(own_rows, 2, kvs * HD).transpose(1, 0, 2)
-    if n * kvs == KV:
-        kv = lax.all_gather(kv, "tensor", axis=2, tiled=True)
+    if spread and n * kvs == KV:
+        dy, gain_mid, dattn, do = out_of_feed(n, y, attn, out_grad, gains, dgate, dup, wg, wu, wo)
+        d = attend_back(heads, kvs, piece_starts, q, k, v, flat(do), cos, sin)
+        lefts = [flat(a).T for a in (h1, df, h3, dattn)]
+        rights = [d, flat(hid), flat(dgate), flat(dup), o]
+        in_grad, gain_one, qkv_sum, down_sum, gate_sum, up_sum, out_sum, kv = tail(
+            n, m, split, layer_in, dy, gains, d.reshape(n, rows, -1), wqkv, lefts, rights
+        )
+        own_rows = qkv_sum.shape[0]
+        kv = kv.reshape(n, own_rows, 2, kvs * HD).transpose(2, 1, 0, 3).reshape(2, own_rows, KV * HD)
     else:
-        kv = lax.dynamic_update_slice_in_dim(jnp.zeros((2, own_rows, KV * HD), BF16), kv, kv_at, 2)
-        kv = lax.psum(kv, "tensor")
+        tie = lax.optimization_barrier
+        down_part = weight_grad(flat(df), flat(hid))
+        gate_part = weight_grad(flat(h3), flat(dgate))
+        up_part = weight_grad(flat(h3), flat(dup))
+        dgate, dup, down_part, gate_part, up_part = tie((dgate, dup, down_part, gate_part, up_part))
+        down_sum, gate_sum, up_sum = map(scatter_rows, (down_part, gate_part, up_part))
+        dy, gain_mid, dattn, do = out_of_feed(n, y, attn, out_grad, gains, dgate, dup, wg, wu, wo)
+        do, dattn, down_sum, gate_sum = tie((do, dattn, down_sum, gate_sum))
+        out_part = weight_grad(flat(dattn), o)
+        do, out_part = tie((do, out_part))
+        d = attend_back(heads, kvs, piece_starts, q, k, v, flat(do), cos, sin)
+        qkv_part = weight_grad(h1_flat, d)
+        d, qkv_part, up_sum = tie((d, qkv_part, up_sum))
+        out_sum, qkv_sum = scatter_rows(out_part), scatter_rows(qkv_part)
+        in_grad, gain_one = last(n, layer_in, dy, gains, d.reshape(n, rows, -1), wqkv)
+
+        own_rows = qkv_sum.shape[0]
+        kv = qkv_sum[:, split:].reshape(own_rows, 2, kvs * HD).transpose(1, 0, 2)
+        if n * kvs == KV:
+            kv = lax.all_gather(kv, "tensor", axis=2, tiled=True)
+        else:
+            kv = lax.dynamic_update_slice_in_dim(jnp.zeros((2, own_rows, KV * HD), BF16), kv, kv_at, 2)
+            kv = lax.psum(kv, "tensor")
     kv = kv.astype(F32)
 
     gain_grads = jnp.concatenate([gain_one, gain_mid, gain_four], axis=0)

time: 1080 us -> 910 us (0.84)
  waiting for transfers between devices: 190 us -> 1.42 us
  matrix products: 67 us -> 0 us
  Pallas kernels: 766 us -> 819 us
  local copies, waits for them, and re-layouts: 17.5 us -> 60.9 us
  other arithmetic: 15.7 us -> 4.5 us
    reduce_scatter x5 -> x0, waiting for transfers between devices: 95.2 us -> none  [scatter_rows(): return lax.psum_scatter(grad, 'dp', scatter_dimension=0, tiled=True)]
    pallas_call x3, Pallas kernels: 372 us -> 463 us  [the longest x1 210 us: tail(): pl.pallas_call(functools.partial(tail_kernel, n, split), out_shape=[jax.S...]
    all_gather x5 -> x3, waiting for transfers between devices: 90.2 us -> 0.02 us  [collect(): return lax.all_gather(shard, 'dp', axis=0, tiled=True)]
    dot_general x5 -> x0, matrix products: 67 us -> none  [dot_tn(): lax.dot_general(a, b, (((0,), (0,)), ((), ())), preferred_element_type=F32)]
    pallas_call x1, Pallas kernels: 173 us -> 145 us  [turn_feed(): pl.pallas_call(functools.partial(turn_feed_kernel, n), out_shape=[jax.Sha...]
    reshape x1 -> x4, local copies, waits for them, and re-layouts: 0.73 us -> 26.9 us  [the longest x3 20 us: body(): flat = lambda a: a.reshape(tokens, a.shape[-1])]
    pallas_call x1, Pallas kernels: 180 us -> 155 us  [out_of_feed(): pl.pallas_call(functools.partial(out_of_feed_kernel, n), out_shape=[jax.S...]
    pallas_call x1, Pallas kernels: 11 us -> 26.6 us  [sum_gains(): pl.pallas_call(functools.partial(sum_gains_kernel, n, m), out_shape=jax.S...]
  transfers between devices with their start and end apart: 11 -> 3, of which waited for: 4 -> 0; matrix products, arithmetic and copies ran while one was open for 3% -> 2% of each run, Pallas kernels for 55% -> 30%
where the time goes in v2:
time: 910 us; the launch traced here: 900 us
  Pallas kernels  819 us (90%)
  local copies, waits for them, and re-layouts  60.9 us (7%)
  between operations  14.6 us (2%)
    pallas_call x1, Pallas kernels, tail(): pl.pallas_call(functools.partial(tail_kernel, n, split), out_shape=[jax.S...  210 us
    pallas_call x1, Pallas kernels, into_feed(): pl.pallas_call(functools.partial(into_feed_kernel, n, spread), out_shape=...  168 us
    pallas_call x1, Pallas kernels, out_of_feed(): pl.pallas_call(functools.partial(out_of_feed_kernel, n), out_shape=[jax.S...  155 us
    pallas_call x1, Pallas kernels, turn_feed(): pl.pallas_call(functools.partial(turn_feed_kernel, n), out_shape=[jax.Sha...  145 us
    pallas_call x1, Pallas kernels, first(): pl.pallas_call(functools.partial(first_kernel, n, spread), out_shape=outs...  85.4 us
    pallas_call x1, Pallas kernels, sum_gains(): pl.pallas_call(functools.partial(sum_gains_kernel, n, m), out_shape=jax.S...  26.6 us
    unnamed x56, local copies, waits for them, and re-layouts  23.6 us
    reshape x3, local copies, waits for them, and re-layouts, body(): flat = lambda a: a.reshape(tokens, a.shape[-1])  20 us
  transfers between devices with their start and end apart: 3, of which 0 were waited for; matrix products, arithmetic and copies ran while one was open for 2% of the time, Pallas kernels for 30%

profile of v2, /device:TPU:0, one launch (start us, length us, event | category | flops | bytes accessed | tf_op | source)
XLA Modules:
  0.0 900.4 jit_solution(8844498921895565105)
XLA Ops:
  8.5 1.9 pad_maximum_fusion
  11.9 6.3 gains.1
  18.4 85.4 %first.1 = (bf16[4,256,2304]{2,1,0:T(8,128)(2,1)S(1)}, bf16[8,288,2304]{2,1,0:T(8,128)(2,1)S(1)}) custom-call(bf16[256,2304]{1,0:T(8,128)(2,1)S(1)} %copy-done.1, f32[4,2304]{1,0:T(4,128)S(1)} %reshape.101.gains, bf16[288,2304]{1,0:T(8,128)(2,1)S(1)} %copy-done.4), custom_call_target="tpu_custom_call" | custom-call | bytes 314572800 | tf_op jit(solution)/shard_map/first/pallas_call | solution.py:530
  103.8 4.1 copy-done
  107.9 2.2 copy-done.2
  110.1 6.9 copy.44
  117.0 1.9 multiply_sine_fusion
  118.9 13.0 %attend.1 = (bf16[2,1024,256]{2,1,0:T(8,128)(2,1)S(1)}, bf16[1,1024,256]{2,1,0:T(8,128)(2,1)S(1)}, bf16[1,1024,256]{2,1,0:T(8,128)(2,1)S(1)}, bf16[1024,512]{1,0:T(8,128)(2,1)S(1)}) custom-call(s32[1,2]{1,0:T(1,128)S(1)} %copy-done.7, bf16[1024,2304]{1,0:T(8,128)(2,1)} %bitcast.35, bf16[2304,1024]{1,0:T(8,128)(2,1)} %all-gather.4.cloned.1.call-done.w.w_hbm, ...), custom_call_target="tpu_custom_call" | custom-call | flops 21474836480 | bytes 20971520 | tf_op jit(solution)/shard_map/attend/pallas_call | solution.py:607
  134.7 167.5 %into_feed.1 = (f32[256,2304]{1,0:T(8,128)}, f32[256,2304]{1,0:T(8,128)}, bf16[4,256,2304]{2,1,0:T(8,128)(2,1)}, bf16[4,256,2304]{2,1,0:T(8,128)(2,1)}, bf16[4,2...) custom-call(bf16[256,2304]{1,0:T(8,128)(2,1)} %x.5, f32[4,2304]{1,0:T(4,128)} %copy-done.5, ...), custom_call_target="tpu_custom_call" | custom-call | bytes 629145600 | tf_op jit(solution)/shard_map/into_feed/pallas_call | solution.py:797
  302.2 6.6 copy.46
  308.8 145.3 %turn_feed.1 = (bf16[256,2304]{1,0:T(8,128)(2,1)}, f32[1,2304]{1,0:T(1,128)}, bf16[4,256,2304]{2,1,0:T(8,128)(2,1)}, bf16[4,256,2304]{2,1,0:T(8,128)(2,1)}, bf16[4,256,2304]{2,1,0:T(8,128)(2,1)}) custom-call(f32[256,2304]{1,0:T(8,128)} %get-tuple-element.46.y, bf16[256,2304]{1,0:T(8,128)(2,1)} %dout.3, f32[4,2304]{1,0:T(4,128)} %copy-done.5, ...), custom_call_target="tpu_custom_call" | custom-call | bytes 629145600 | tf_op jit(solution)/shard_map/turn_feed/pallas_call | solution.py:909
  454.2 6.7 copy.45
  460.9 154.5 %out_of_feed.1 = (f32[256,2304]{1,0:T(8,128)}, f32[2,2304]{1,0:T(2,128)}, bf16[4,256,2304]{2,1,0:T(8,128)(2,1)}, bf16[4,256,512]{2,1,0:T(8,128)(2,1)}) custom-call(f32[256,2304]{1,0:T(8,128)} %get-tuple-element.46.y, f32[256,2304]{1,0:T(8,128)} %get-tuple-element.51.attn, bf16[256,2304]{1,0:T(8,128)(2,1)} %dout.3, f32[4,2304]{1,0:T(4,128)} %copy-done.5, ...), custom_call_target="tpu_custom_call" | custom-call | bytes 629145600 | tf_op jit(solution)/shard_map/out_of_feed/pallas_call | solution.py:1031
  615.4 6.7 copy.47
  624.4 10.4 %attend_back.1.refs_4_ = bf16[1024,1024]{1,0:T(8,128)(2,1)} custom-call(s32[1,2]{1,0:T(1,128)S(1)} %copy-done.7, bf16[2,1024,256]{2,1,0:T(8,128)(2,1)S(1)} %copy-done.9, bf16[1,1024,256]{2,1,0:T(8,128)(2,1)S(1)} %get-tuple-element.57.k_in, bf16[1,1024,256]{2,1,0:T(8,128)(2,1)S(1)} %copy-done.11, bf16[1024,512]{1,0:T(8,128)(2,1)S(1)} %bitcast.38, ...), custom_call_target="tpu_custom_call" | custom-call | flops 32212254720 | bytes 20971520 | tf_op jit(solution)/shard_map/attend_back/pallas_call | solution.py:664
  634.9 209.7 %tail.1 = (bf16[256,2304]{1,0:T(8,128)(2,1)}, f32[1,2304]{1,0:T(1,128)}, f32[288,1024]{1,0:T(8,128)}, f32[288,2304]{1,0:T(8,128)}, f32[288,2304]{1,0:T(8,128)}, ...) custom-call(bf16[256,2304]{1,0:T(8,128)(2,1)} %x.5, f32[256,2304]{1,0:T(8,128)} %get-tuple-element.55.dy, ...), custom_call_target="tpu_custom_call" | custom-call | bytes 629145600 | tf_op jit(solution)/shard_map/tail/pallas_call | solution.py:1467
  845.4 26.6 %sum_gains.1 = f32[4,288]{1,0:T(4,128)S(1)} custom-call(f32[8,4,288]{2,1,0:T(4,128)S(1)} %bitcast.37), custom_call_target="tpu_custom_call" | custom-call | tf_op jit(solution)/shard_map/sum_gains/pallas_call | solution.py:470
  872.6 1.9 slice.23
  874.6 3.2 reshape.102
  877.7 1.8 fusion
  880.3 1.2 copy.49
  886.5 1.5 copy.61
  889.2 1.5 copy.62
  891.9 1.5 copy.63
  (76 shorter events, 17.4 us)
Async XLA Ops:
  7.2 4.7 copy-start.20
  7.2 4.7 copy-start.21
  7.2 4.7 copy-start.22
  7.2 4.7 copy-start.23
  7.2 11.2 %copy-start.1 = (bf16[256,2304]{1,0:T(8,128)(2,1)S(1)}, bf16[256,2304]{1,0:T(8,128)(2,1)}, u32[]{:S(2)}) copy-start(bf16[256,2304]{1,0:T(8,128)(2,1)} %x.5) | copy-start | bytes 3538948
  7.2 11.2 %copy-start.4 = (bf16[288,2304]{1,0:T(8,128)(2,1)S(1)}, bf16[288,2304]{1,0:T(8,128)(2,1)}, u32[]{:S(2)}) copy-start(bf16[288,2304]{1,0:T(8,128)(2,1)} %refs_0_.1) | copy-start | bytes 3981316
  7.2 111.7 %all-gather.4.cloned.1.call-start = ((), (), s32[]{:S(2)}) async-start(), calls=%async_computation | async-start | bytes 5308416 | tf_op jit(solution)/shard_map/all_gather | solution.py:1543
  10.3 124.3 %all-gather.6.cloned.1.call-start = ((), (), s32[]{:S(2)}) async-start(), calls=%async_computation.1 | async-start | bytes 2654208 | tf_op jit(solution)/shard_map/all_gather | solution.py:1543
  11.1 297.7 %all-gather.8.cloned.1.call-start = ((), (), s32[]{:S(2)}) async-start(), calls=%async_computation.2 | async-start | bytes 11943936 | tf_op jit(solution)/shard_map/all_gather | solution.py:1543
  18.4 98.6 %copy-start.5 = (f32[4,2304]{1,0:T(4,128)}, f32[4,2304]{1,0:T(4,128)S(1)}, u32[]{:S(2)}) copy-start(f32[4,2304]{1,0:T(4,128)S(1)} %reshape.101.gains) | copy-start | bytes 110596
  103.8 4.1 copy-start
  107.9 2.2 copy-start.2
  110.1 8.8 copy-start.7
  615.4 6.7 copy-start.6
  622.1 1.2 copy-start.9
  623.4 1.0 copy-start.11
  634.9 209.7 %copy-start.18 = (f32[2,2304]{1,0:T(2,128)S(1)}, f32[2,2304]{1,0:T(2,128)}, u32[]{:S(2)}) copy-start(f32[2,2304]{1,0:T(2,128)} %get-tuple-element.71) | copy-start | bytes 55300
  634.9 209.7 %copy-start.19 = (f32[1,2304]{1,0:T(1,128)S(1)}, f32[1,2304]{1,0:T(1,128)}, u32[]{:S(2)}) copy-start(f32[1,2304]{1,0:T(1,128)} %get-tuple-element.72) | copy-start | bytes 27652
  881.6 2.0 copy-start.15
  882.3 2.3 copy-start.16
  883.6 2.0 copy-start.17
  883.6 2.9 copy-start.14
  886.5 2.7 copy-start.13
  889.2 2.7 copy-start.12
  (3 other events, 2.7 us)
Sparse Core Ops, SparseCore 0:
  10.5 61.1 all-gather.3
  73.6 29.9 all-gather.5
  105.5 94.1 all-gather.7

commit v3 on v2

--- a/solution.py
+++ b/solution.py
@@ -41,6 +41,14 @@
     return next(t for t in (256, 384, 128) if width % t == 0)
 
 
+def strip_of(count):
+    return next(t for t in (64, 48, 32, 16) if count % t == 0)
+
+
+def wide_tile(width):
+    return next(t for t in (1152, 1024, 768, 512, 384, 256, 128) if width % t == 0)
+
+
 def loop(count, body):
     lax.fori_loop(0, count, lambda t, c: (body(t), c)[1], 0)
 
@@ -68,7 +76,7 @@
     pl.semaphore_wait(barrier, len(peers) + jnp.minimum(i, 1) + jnp.minimum(n - 1 - i, 1))
 
 
-def gather_line(i, n, held, send, recv, compute):
+def gather_steps(i, n, held, send, recv):
     def copy(block, way, s, to):
         return pltpu.make_async_remote_copy(
             held.at[block],
@@ -81,7 +89,7 @@
 
     up, down = jnp.minimum(i + 1, n - 1), jnp.maximum(i - 1, 0)
 
-    def step(s):
+    def pass_on(s):
         low, high = i - s, i + s
 
         @pl.when((s > 0) & (low >= 0))
@@ -100,10 +108,6 @@
         def _():
             copy(high, 1, s, down).start()
 
-        compute(s, block_at(i, n, s))
-
-    loop(n, step)
-
     def finish(s):
         low, high = i - s, i + s
 
@@ -115,7 +119,18 @@
         def _():
             copy(high, 1, s, down).wait_send()
 
-    loop(n, finish)
+    return pass_on, functools.partial(loop, n, finish)
+
+
+def gather_line(i, n, held, send, recv, compute):
+    pass_on, finish = gather_steps(i, n, held, send, recv)
+
+    def step(s):
+        pass_on(s)
+        compute(s, block_at(i, n, s))
+
+    loop(n, step)
+    finish()
 
 
 def scatter_steps(i, n, part, landed, send, recv, compute):
@@ -143,12 +158,14 @@
         ).wait_recv()
 
     def add(block):
+        strip = strip_of(rows)
+
         def chunk(c):
-            r = pl.ds(c * ROWS, ROWS)
+            r = pl.ds(c * strip, strip)
             total = part[block, r, :].astype(F32) + landed[block, r, :].astype(F32)
             part[block, r, :] = total.astype(BF16)
 
-        loop(rows // ROWS, chunk)
+        loop(rows // strip, chunk)
 
     up, down = jnp.minimum(i + 1, n - 1), jnp.maximum(i - 1, 0)
 
@@ -279,8 +296,6 @@
 
 
 class Spread:
-    sems = 8
-
     def __init__(self, own, full, send, recv, local):
         me = lax.axis_index("dp")
         c, x, y = me % 2, (me // 2) % 2, me // 4
@@ -295,16 +310,15 @@
     def peers(self):
         return (self.core, self.x, self.y)
 
-    def rows(self, part):
-        count = self.full.shape[1]
-        half = count // 2
-        return pl.ds(*{0: (0, count), 1: (0, half), 2: (half, half)}[part])
+    def view(self, owner, part):
+        count = self.own.shape[0]
+        first, size = ((0, count), (0, count // 2), (count // 2, count // 2))[part]
+        return self.full.at[pl.ds(pl.multiple_of(owner * count + first, ROWS), size)]
 
     def copy(self, k, source, owner, part, to):
-        r = self.rows(part)
         return pltpu.make_async_remote_copy(
-            self.own.at[r] if source is None else self.full.at[source, r],
-            self.full.at[owner, r],
+            self.own if source is None else self.view(source, part),
+            self.view(owner, part),
             self.send.at[k],
             self.recv.at[k],
             device_id={"dp": to},
@@ -341,7 +355,7 @@
         self.copy(k, owner, owner, part, self.core).wait_recv()
 
     def keep(self):
-        return pltpu.make_async_copy(self.own, self.full.at[self.me], self.local.at[0])
+        return pltpu.make_async_copy(self.own, self.view(self.me, 0), self.local.at[0])
 
     def begin(self):
         self.keep().start()
@@ -488,7 +502,7 @@
     i = lax.axis_index("tensor")
     rows = x.shape[0]
     if spread:
-        shard, full, gathered, held, send, recv, out_sem, *sems = refs
+        shard, full, gathered, turned, held, send, recv, out_sem, turn, turn_sem, *sems = refs
         gather = Spread(shard, gathered, *sems)
         line_barrier(i, n, gather.peers())
         gather.begin()
@@ -497,16 +511,19 @@
         line_barrier(i, n)
     scale = 1.0 + gains[0:1, :]
 
+    strip = strip_of(rows)
+
     def chunk(c):
-        r = pl.ds(c * ROWS, ROWS)
+        r = pl.ds(c * strip, strip)
         v = x[r, :].astype(F32)
         held[i, r, :] = (v * inverse_rms(v) * scale).astype(BF16)
 
-    loop(rows // ROWS, chunk)
+    loop(rows // strip, chunk)
 
     def keep(s, block):
         pltpu.make_async_copy(held.at[block], full.at[block], out_sem.at[s]).start()
         if spread:
+            flip_rows(held.at[block], turned, block * rows, turn, turn_sem)
             pl.when(s == min(1, n - 1))(gather.middle)
             pl.when(s == min(2, n - 1))(gather.turn)
 
@@ -519,6 +536,29 @@
     loop(n, finish)
     if spread:
         gather.end()
+
+
+def flip_rows(block, target, column, stage, sem):
+    rows, width = block.shape
+    size = stage.shape[1]
+    pieces = width // size
+
+    def copy(k):
+        return pltpu.make_async_copy(
+            stage.at[k % 2],
+            target.at[pl.ds(k * size, size), pl.ds(pl.multiple_of(column, 128), rows)],
+            sem.at[k % 2],
+        )
+
+    for k in range(pieces):
+        if k >= 2:
+            copy(k - 2).wait()
+        for j in range(size // 256):
+            at = pl.ds(k * size + j * 256, 256)
+            stage[k % 2, pl.ds(j * 256, 256), :] = block[:, at].T
+        copy(k).start()
+    for k in range(max(0, pieces - 2), pieces):
+        copy(k).wait()
 
 
 def first(n, m, x, gains, shard):
@@ -526,21 +566,23 @@
     spread = shard is not None
     outs = [jax.ShapeDtypeStruct((n, rows, width), BF16)]
     if spread:
-        outs += [jax.ShapeDtypeStruct((m,) + shard.shape, BF16)]
+        outs += [jax.ShapeDtypeStruct((m * shard.shape[0], shard.shape[1]), BF16)]
+        outs += [jax.ShapeDtypeStruct((width, n * rows), BF16)]
+        turn = [pltpu.VMEM((2, 768, rows), BF16), pltpu.SemaphoreType.DMA((2,))]
     out = pl.pallas_call(
         functools.partial(first_kernel, n, spread),
         out_shape=outs,
         in_specs=[VM, VM] + [ANY] * spread,
-        out_specs=[ANY] + [ANY] * spread,
+        out_specs=[ANY] * len(outs),
         scratch_shapes=[pltpu.VMEM((n, rows, width), BF16)]
         + line_scratch(n)
         + [pltpu.SemaphoreType.DMA((n,))]
-        + (spread_scratch() if spread else []),
+        + (turn + spread_scratch() if spread else []),
         compiler_params=params(1, 32),
         cost_estimate=cost(0, 300 << 20),
         name="first",
     )(x, gains, *([shard] if spread else []))
-    return (out[0], out[1].reshape(-1, shard.shape[1])) if spread else (out[0], None)
+    return out if spread else (out[0], None, None)
 
 
 def turn(u, cos, sin):
@@ -673,37 +715,23 @@
     )(starts, q, k, v, do, cos, sin)
 
 
-def into_feed_kernel(n, spread, x, gains, o_hbm, wo_hbm, wg_hbm, wu_hbm, *refs):
-    attn_out, y_out, h3_full, hid_out, up_out, ge_out, *refs = refs
-    if spread:
-        wu_full, *refs = refs
-        *refs, token, spread_send, spread_recv, spread_local = refs
-    (
-        o, wo, wg, wu, part, landed, mine, held, hid_s, up_s, ge_s,
-        load, rs_send, rs_recv, ag_send, ag_recv, keep_sem, out_sem,
-    ) = refs
+def into_feed_kernel(
+    n, x, gains, o_hbm, wo_hbm, wg_hbm, wu_hbm,
+    attn_out, y_out, h3_full, hid_out, up_out, ge_out,
+    o, wo, wg, wu, part, landed, mine, held, hid_s, up_s, ge_s,
+    load, rs_send, rs_recv, ag_send, ag_recv, keep_sem, out_sem,
+):
     i = lax.axis_index("tensor")
     rows, width = x.shape
-    pairs = [(o_hbm, o), (wo_hbm, wo), (wg_hbm, wg)] + ([] if spread else [(wu_hbm, wu)])
-    loads = [pltpu.make_async_copy(src, dst, load.at[k]) for k, (src, dst) in enumerate(pairs)]
+    loads = [
+        pltpu.make_async_copy(src, dst, load.at[k])
+        for k, (src, dst) in enumerate(((o_hbm, o), (wo_hbm, wo), (wg_hbm, wg), (wu_hbm, wu)))
+    ]
     for c in loads:
         c.start()
-    if spread:
-        gather = Spread(wu_hbm, wu_full, spread_send, spread_recv, spread_local)
-        core = lax.axis_index("dp") % 2
-        line_barrier(i, n, gather.peers())
-        gather.begin()
-    else:
-        line_barrier(i, n)
+    line_barrier(i, n)
     loads[0].wait()
     loads[1].wait()
-    if spread:
-
-        @pl.when(core == 1)
-        def _():
-            gather.middle()
-            gather.turn()
-            pl.semaphore_wait(token, 1)
 
     def compute(t, block):
         def tile(k):
@@ -720,13 +748,6 @@
         loop(width // TILE, tile)
 
     done = scatter_line(i, n, part, landed, rs_send, rs_recv, compute, own)
-    if spread:
-
-        @pl.when(core == 0)
-        def _():
-            pl.semaphore_signal(token, 1, device_id={"dp": gather.core}, device_id_type=MESH)
-            gather.middle()
-
     scale_two, scale_three = 1.0 + gains[1:2, :], 1.0 + gains[2:3, :]
 
     def chunk(c):
@@ -739,18 +760,8 @@
 
     loop(rows // ROWS, chunk)
     done()
-    if spread:
-        pl.when(core == 0)(gather.turn)
-        gather.end()
-        size = wu_hbm.shape[0]
-        loads += [
-            pltpu.make_async_copy(wu_full.at[k], wu.at[pl.ds(k * size, size)], load.at[3 + k])
-            for k in range(wu_full.shape[0])
-        ]
-        for c in loads[3:]:
-            c.start()
-    for c in loads[2:]:
-        c.wait()
+    loads[2].wait()
+    loads[3].wait()
     drain = Drain(
         (hid_out, up_out, ge_out), (hid_s, up_s, ge_s), out_sem, lambda s: block_at(i, n, s)
     )
@@ -787,33 +798,30 @@
     loop(n, finish)
 
 
-def into_feed(n, m, spread, x, gains, o, wo, wg, wu):
+def into_feed(n, x, gains, o, wo, wg, wu):
     rows, width = x.shape
     wide = wg.shape[1]
     blocks = lambda w: jax.ShapeDtypeStruct((n, rows, w), BF16)
     mine = jax.ShapeDtypeStruct((rows, width), F32)
-    outs = [mine, mine, blocks(width), blocks(wide), blocks(wide), blocks(wide)]
-    outs += [jax.ShapeDtypeStruct((m,) + wu.shape, BF16)] * spread
     return pl.pallas_call(
-        functools.partial(into_feed_kernel, n, spread),
-        out_shape=outs,
+        functools.partial(into_feed_kernel, n),
+        out_shape=[mine, mine, blocks(width), blocks(wide), blocks(wide), blocks(wide)],
         in_specs=[VM, VM, ANY, ANY, ANY, ANY],
-        out_specs=[VM, VM] + [ANY] * (len(outs) - 2),
+        out_specs=[VM, VM, ANY, ANY, ANY, ANY],
         scratch_shapes=[
             pltpu.VMEM(o.shape, BF16),
             pltpu.VMEM(wo.shape, BF16),
             pltpu.VMEM(wg.shape, BF16),
-            pltpu.VMEM(wg.shape, BF16),
+            pltpu.VMEM(wu.shape, BF16),
             pltpu.VMEM((n, rows, width), BF16),
             pltpu.VMEM((n + 1, rows, width), BF16),
             pltpu.VMEM((rows, width), F32),
             pltpu.VMEM((n, rows, width), BF16),
         ]
         + [pltpu.VMEM((2, rows, wide), BF16)] * 3
-        + [pltpu.SemaphoreType.DMA((3 + m,))]
+        + [pltpu.SemaphoreType.DMA((4,))]
         + line_scratch(n) * 2
-        + [pltpu.SemaphoreType.DMA((n,)), pltpu.SemaphoreType.DMA((3, 2))]
-        + ([pltpu.SemaphoreType.REGULAR] + spread_scratch() if spread else []),
+        + [pltpu.SemaphoreType.DMA((n,)), pltpu.SemaphoreType.DMA((3, 2))],
         compiler_params=params(2, 62),
         cost_estimate=cost(0, 600 << 20),
         name="into_feed",
@@ -1060,6 +1068,350 @@
     )(y, attn, dout, gains, dgate, dup, wg, wu, wo)
 
 
+class Slots:
+    def __init__(self, arrays, pool, firsts, sems, view, width=None):
+        self.arrays, self.pool, self.firsts, self.sems, self.view = arrays, pool, firsts, sems, view
+        self.width = width or pool.shape[2]
+
+    def copies(self, s, inward):
+        for k, (array, first) in enumerate(zip(self.arrays, self.firsts)):
+            slot = self.pool.at[first + s % 2, :, pl.ds(0, self.width)]
+            block = self.view(array, s)
+            pair = (block, slot) if inward else (slot, block)
+            yield pltpu.make_async_copy(*pair, self.sems.at[k, s % 2])
+
+    def fetch(self, s):
+        for c in self.copies(s, True):
+            c.start()
+
+    def advance(self, s, count):
+        for c in self.copies(s, True):
+            c.wait()
+        if s + 1 < count:
+            self.fetch(s + 1)
+
+    def free(self, s):
+        if s >= 2:
+            self.settle(s - 2)
+
+    def settle(self, s):
+        for c in self.copies(s, False):
+            c.wait()
+
+    def leave(self, s):
+        for c in self.copies(s, False):
+            c.start()
+
+    def finish(self, count):
+        for s in range(max(0, count - 2), count):
+            self.settle(s)
+
+
+def middle_kernel(
+    n, x_hbm, dout_hbm, gains, o_hbm, wo_hbm, wg_hbm, wu_hbm, wd_hbm,
+    layer_out, dy_out, gain_out, h3_t, hid_out, up_out, ge_out, df_t, dgate_out, dup_out,
+    dattn_t, do_out,
+    xs, dout, wo, wg, wu, wd, part, landed, held, y, attn, pool, fold, flip,
+    load, rs_send, rs_recv, ag_send, ag_recv, flip_sem, in_sem, out_sem, last_sem,
+    wu_send, wu_recv, wu_local, wd_send, wd_recv, wd_local,
+):
+    i = lax.axis_index("tensor")
+    rows, width = xs.shape
+    piece = rows // 2
+    narrow = wo_hbm.shape[1]
+    pairs = ((wo_hbm, wo), (x_hbm, xs), (wg_hbm, wg), (dout_hbm, dout))
+    loads = [pltpu.make_async_copy(a, b, load.at[k]) for k, (a, b) in enumerate(pairs)]
+    for c in loads:
+        c.start()
+    up_spread = Spread(wu_hbm, wu, wu_send, wu_recv, wu_local)
+    down_spread = Spread(wd_hbm, wd, wd_send, wd_recv, wd_local)
+    line_barrier(i, n, up_spread.peers())
+    up_spread.begin()
+    loads[0].wait()
+    wide = wd.shape[1]
+    over, across = min(768, wide_tile(width)), min(768, wide_tile(wide))
+    scale_two, scale_three, scale_four = (1.0 + gains[k : k + 1, :] for k in (1, 2, 3))
+    fold[...] = jnp.zeros_like(fold)
+
+    def tiles(total, size, body):
+        loop(total // size, lambda k: body(pl.ds(pl.multiple_of(k * size, size), size)))
+
+    def place(c):
+        return pl.ds(c * piece, piece)
+
+    def forward_view(c):
+        return lambda array, s: array.at[block_at(i, n, s), place(c)]
+
+    def backward_view(c):
+        return lambda array, s: array.at[block_at(i, n, n - 1 - s), place(c)]
+
+    class Sum:
+        def __init__(self, which, c, product, feed=None):
+            at = 2 * which + c
+            self.c, self.feed = c, feed
+            self.part, self.landed = part.at[c], landed.at[c]
+
+            def compute(t, block):
+                if feed:
+                    feed.advance(t, n)
+
+                def tile(at):
+                    self.part[block, :, at] = product(t, block, at).astype(BF16)
+
+                tiles(width, over, tile)
+
+            self.compute = compute
+            self.step, self.land, self.done = scatter_steps(
+                i, n, self.part, self.landed, rs_send.at[at], rs_recv.at[at], compute
+            )
+
+        def start(self):
+            if self.feed:
+                self.feed.fetch(0)
+            self.step(0)
+
+        def own(self):
+            self.compute(n - 1, i)
+
+        def rows(self, r):
+            return summed_rows(i, n, self.part.at[i], self.landed, r)
+
+    class Gather:
+        def __init__(self, which, c, full, compute, drained):
+            at = 2 * which + c
+            self.c, self.full, self.compute, self.drained = c, full, compute, drained
+            self.pass_on, self.sent = gather_steps(i, n, held.at[c], ag_send.at[at], ag_recv.at[at])
+
+        def use(self, s):
+            block = block_at(i, n, s)
+            self.compute(s, block)
+            column = block * rows + self.c * piece
+            flip_rows(held.at[self.c, block], self.full, column, flip, flip_sem)
+
+        def finish(self):
+            self.use(n - 1)
+            self.sent()
+            self.drained(n)
+
+    def chunks(c, body):
+        strip = strip_of(piece)
+
+        def one(k):
+            body(pl.ds(k * strip, strip), pl.ds(c * piece + k * strip, strip))
+
+        loop(piece // strip, one)
+
+
+    def out_product(t, block, at):
+        return dot_nt(pool[8 + t % 2, :, pl.ds(0, narrow)], wo[at, :])
+
+    def down_product(t, block, at):
+        return dot_nt(pool[6 + t % 2], wd[at, :])
+
+    def in_product(t, block, at):
+        return dot_nt(pool[6 + t % 2], wg[at, :]) + dot_nt(pool[10 + t % 2], wu[at, :])
+
+    def sums(c):
+        heads = Slots((o_hbm,), pool, (8,), in_sem.at[3, c], backward_view(c), narrow)
+        hid = Slots((hid_out,), pool, (6,), in_sem.at[0, c], backward_view(c))
+        both = Slots((dgate_out, dup_out), pool, (6, 10), in_sem.at[1, c], backward_view(c))
+        return (
+            Sum(0, c, out_product, heads),
+            Sum(1, c, down_product, hid),
+            Sum(2, c, in_product, both),
+        )
+
+
+    def after_attention(c, total):
+        def body(r, g):
+            a = total.rows(r)
+            attn[g, :] = a.astype(BF16)
+            v = xs[g, :].astype(F32) + a * inverse_rms(a) * scale_two
+            y[g, :] = v
+            held[c, i, r, :] = (v * inverse_rms(v) * scale_three).astype(BF16)
+
+        chunks(c, body)
+
+    def after_down(c, total):
+        def body(r, g):
+            f = total.rows(r)
+            d = dout[g, :].astype(F32)
+            inv = inverse_rms(f)
+            xs[g, :] = (y[g, :] + f * inv * scale_four).astype(BF16)
+            held[c, i, r, :] = norm_back(d * scale_four, f, inv).astype(BF16)
+            fold[2] += fold_rows(d * (f * inv))
+
+        chunks(c, body)
+
+    def after_in(c, total):
+        def body(r, g):
+            dh3 = total.rows(r)
+            v = y[g, :]
+            inv = inverse_rms(v)
+            dy = dout[g, :].astype(F32) + norm_back(dh3 * scale_three, v, inv)
+            y[g, :] = dy
+            fold[1] += fold_rows(dh3 * (v * inv))
+            a = attn[g, :].astype(F32)
+            inv = inverse_rms(a)
+            held[c, i, r, :] = norm_back(dy * scale_two, a, inv).astype(BF16)
+            fold[0] += fold_rows(dy * (a * inv))
+
+        chunks(c, body)
+
+
+    def gathers(c):
+        ahead = Slots((hid_out, up_out, ge_out), pool, (0, 2, 4), out_sem.at[0, c], forward_view(c))
+        sides = Slots((up_out, ge_out), pool, (0, 2), in_sem.at[2, c], forward_view(c))
+        back = Slots((dgate_out, dup_out), pool, (4, 8), out_sem.at[1, c], forward_view(c))
+
+        def into(s, block):
+            if s == 0 and c == 0:
+                up_spread.end()
+                loads[2].wait()
+            ahead.free(s)
+            k = s % 2
+
+            def tile(at):
+                u = dot_nn(held[c, block], wg[:, at])
+                up = dot_nn(held[c, block], wu[:, at])
+                b = 0.7978845608028654
+                th = jnp.tanh(b * (u + 0.044715 * (u * u * u)))
+                half = 0.5 * (1.0 + th)
+                gelu = u * half
+                slope = half + 0.5 * u * (1.0 - th * th) * (b * (1.0 + 0.134145 * (u * u)))
+                pool[0 + k, :, at] = (gelu * up).astype(BF16)
+                pool[2 + k, :, at] = (up * slope).astype(BF16)
+                pool[4 + k, :, at] = gelu.astype(BF16)
+
+            tiles(wide, across, tile)
+            ahead.leave(s)
+
+        def turned(s, block):
+            if s == 0:
+                sides.fetch(0)
+            sides.advance(s, n)
+            back.free(s)
+            k = s % 2
+
+            def tile(at):
+                dhid = dot_nn(held[c, block], wd[:, at])
+                pool[4 + k, :, at] = (dhid * pool[0 + k, :, at].astype(F32)).astype(BF16)
+                pool[8 + k, :, at] = (dhid * pool[2 + k, :, at].astype(F32)).astype(BF16)
+
+            tiles(wide, across, tile)
+            back.leave(s)
+
+        heads = Slots((do_out,), pool, (0,), out_sem.at[2, c], forward_view(c), narrow)
+
+        def out(s, block):
+            heads.free(s)
+            pool[s % 2, :, pl.ds(0, narrow)] = dot_nn(held[c, block], wo[...]).astype(BF16)
+            heads.leave(s)
+
+        return (
+            Gather(0, c, h3_t, into, ahead.finish),
+            Gather(1, c, df_t, turned, back.finish),
+            Gather(2, c, dattn_t, out, heads.finish),
+        )
+
+    sum_of = (sums(0), sums(1))
+    gather_of = (gathers(0), gathers(1))
+    own_rows = (after_attention, after_down, after_in)
+
+    first_sum = sum_of[0][0]
+    first_sum.start()
+    for k in range(1, n - 1):
+        first_sum.step(k)
+    first_sum.own()
+    up_spread.middle()
+    loads[1].wait()
+    loads[3].wait()
+    before = None
+    for turn in range(6):
+        which, c = turn // 2, turn % 2
+        total = sum_of[c][which]
+        later = (turn + 1) // 2
+        following = sum_of[1 - c][later] if later < 3 else None
+        gather = gather_of[c][which]
+        total.land()
+        own_rows[which](c, total)
+        gather.pass_on(0)
+        total.done()
+        if turn == 0:
+            up_spread.turn()
+            down_spread.begin()
+        if before:
+            before.finish()
+        if turn == 1:
+            down_spread.end()
+        if turn == 4:
+            pltpu.make_async_copy(xs, layer_out, last_sem.at[0]).start()
+        if following:
+            following.start()
+        for k in range(1, n):
+            gather.pass_on(k)
+            gather.use(k - 1)
+            if following and k < n - 1:
+                following.step(k)
+            elif following:
+                following.own()
+        if turn == 0:
+            down_spread.middle()
+            down_spread.turn()
+        before = gather
+    before.finish()
+    pltpu.make_async_copy(y, dy_out, last_sem.at[1]).start()
+    for k in range(3):
+        gain_out[k : k + 1, :] = jnp.sum(fold[k], axis=0, keepdims=True)
+    pltpu.make_async_copy(xs, layer_out, last_sem.at[0]).wait()
+    pltpu.make_async_copy(y, dy_out, last_sem.at[1]).wait()
+
+
+def middle(n, x, dout, gains, o, wo, wg, wu, wd):
+    rows, width = x.shape
+    wide = wg.shape[1]
+    piece = rows // 2
+    sem = pltpu.SemaphoreType.DMA
+    blocks = lambda w: jax.ShapeDtypeStruct((n, rows, w), BF16)
+    turned = jax.ShapeDtypeStruct((width, n * rows), BF16)
+    return pl.pallas_call(
+        functools.partial(middle_kernel, n),
+        out_shape=[
+            jax.ShapeDtypeStruct((rows, width), BF16),
+            jax.ShapeDtypeStruct((rows, width), F32),
+            jax.ShapeDtypeStruct((3, width), F32),
+            turned, blocks(wide), blocks(wide), blocks(wide),
+            turned, blocks(wide), blocks(wide), turned, blocks(wo.shape[1]),
+        ],
+        in_specs=[ANY, ANY, VM] + [ANY] * 5,
+        out_specs=[ANY, ANY, VM] + [ANY] * 9,
+        scratch_shapes=[
+            pltpu.VMEM(x.shape, BF16),
+            pltpu.VMEM(x.shape, BF16),
+            pltpu.VMEM(wo.shape, BF16),
+            pltpu.VMEM(wg.shape, BF16),
+            pltpu.VMEM(wg.shape, BF16),
+            pltpu.VMEM((width, wide), BF16),
+            pltpu.VMEM((2, n, piece, width), BF16),
+            pltpu.VMEM((2, n + 1, piece, width), BF16),
+            pltpu.VMEM((2, n, piece, width), BF16),
+            pltpu.VMEM(x.shape, F32),
+            pltpu.VMEM(x.shape, BF16),
+            pltpu.VMEM((12, piece, wide), BF16),
+            pltpu.VMEM((3, 8, width), F32),
+            pltpu.VMEM((2, 768, piece), BF16),
+            sem((4,)), sem((6, 2, n)), sem((6, n + 1)), sem((6, 2, n)), sem((6, n)),
+            sem((2,)), sem((4, 2, 2, 2)), sem((3, 2, 3, 2)), sem((2,)),
+        ]
+        + spread_scratch() * 2,
+        compiler_params=pltpu.CompilerParams(
+            collective_id=8, has_side_effects=True, vmem_limit_bytes=(127 << 20) // 2
+        ),
+        cost_estimate=cost(0, 1200 << 20),
+        name="middle",
+    )(x, dout, gains, o, wo, wg, wu, wd)
+
+
 def last_kernel(
     n, x, dy, gains, d_hbm, w_hbm, in_grad, gain_out,
     d, w, part, landed, mine, fold, load, rs_send, rs_recv,
@@ -1207,7 +1559,7 @@
                 self.left_copy(q + 1).start()
         else:
             self.left_copy(q + 1).start()
-        tile = next(t for t in (384, 256, 128) if self.width % t == 0)
+        tile = wide_tile(self.width)
 
         def one(t):
             at = pl.ds(pl.multiple_of(t * tile, tile), tile)
@@ -1259,16 +1611,18 @@
         self.far_copy(1).wait_recv()
         half = self.rows // 2
 
+        strip = strip_of(half)
+
         def chunk(c):
             for way, first in ((0, 0), (1, half)):
-                r = pl.ds(first + c * ROWS, ROWS)
-                f = pl.ds(c * ROWS, ROWS)
+                r = pl.ds(first + c * strip, strip)
+                f = pl.ds(c * strip, strip)
                 k = 2 - way
                 total = self.sums[self.third, k, r, self.cols].astype(F32)
                 total += self.far_in[self.third, way, f, self.cols].astype(F32)
                 self.sums[self.third, k, r, self.cols] = total.astype(BF16)
 
-        loop(half // ROWS, chunk)
+        loop(half // strip, chunk)
         self.xy_copy(0, 1).start()
         self.xy_copy(1, 0).start()
 
@@ -1277,14 +1631,16 @@
             for half in range(2):
                 self.xy_copy(way, half).wait_recv()
 
+        strip = strip_of(self.rows)
+
         def chunk(c):
-            r = pl.ds(c * ROWS, ROWS)
+            r = pl.ds(c * strip, strip)
             total = self.own[self.third, r, self.cols]
             for way in range(2):
                 total += self.xy_in[self.fifth, way, r, self.cols].astype(F32)
             put(r, total)
 
-        loop(self.rows // ROWS, chunk)
+        loop(self.rows // strip, chunk)
         for way in range(2):
             self.far_copy(way).wait_send()
             for half in range(2):
@@ -1325,6 +1681,7 @@
     dqkv, hid, dgate, dup, o = rights
     i = lax.axis_index("tensor")
     rows, width = x.shape
+    over = min(768, wide_tile(width))
     loads = [
         pltpu.make_async_copy(src, dst, load.at[k])
         for k, (src, dst) in enumerate(((d_hbm, d), (w_hbm, w)))
@@ -1353,34 +1710,36 @@
 
     def compute(t, block):
         def tile(k):
-            at = pl.ds(pl.multiple_of(k * TILE, TILE), TILE)
+            at = pl.ds(pl.multiple_of(k * over, over), over)
             part[block, :, at] = dot_nt(d[block], w[at, :]).astype(BF16)
 
-        loop(width // TILE, tile)
+        loop(width // over, tile)
 
     step, land, done = scatter_steps(i, n, part, landed, rs_send, rs_recv, compute)
 
     def input_rows():
         def tile(k):
-            at = pl.ds(pl.multiple_of(k * TILE, TILE), TILE)
+            at = pl.ds(pl.multiple_of(k * over, over), over)
             mine[:, at] = dot_nt(d[i], w[at, :])
 
-        loop(width // TILE, tile)
+        loop(width // over, tile)
 
     def input_grad():
         land()
         scale = 1.0 + gains[0:1, :]
         fold[...] = jnp.zeros_like(fold)
 
+        strip = strip_of(rows)
+
         def chunk(c):
-            r = pl.ds(c * ROWS, ROWS)
+            r = pl.ds(c * strip, strip)
             dh1 = summed_rows(i, n, mine, landed, r)
             v = x[r, :].astype(F32)
             inv = inverse_rms(v)
             in_grad[r, :] = (dy[r, :] + norm_back(dh1 * scale, v, inv)).astype(BF16)
             fold[...] += fold_rows(dh1 * (v * inv))
 
-        loop(rows // ROWS, chunk)
+        loop(rows // strip, chunk)
         gain_out[...] = jnp.sum(fold[...], axis=0, keepdims=True)
         done()
 
@@ -1553,28 +1912,28 @@
         )
     )
     wo = collect(out_weight.T)
-    wd = collect(down_weight.T)
     cos, sin = rope_tables()
 
-    spread = m == 8
-    h1, wg = first(n, m, layer_in, gains, gate_weight if spread else None)
+    spread = m == 8 and n * kvs == KV
+    h1, wg, h1_t = first(n, m, layer_in, gains, gate_weight if spread else None)
     if not spread:
         wg = collect(gate_weight)
     h1_flat = h1.reshape(tokens, width)
     q, k, v, o = attend(heads, kvs, piece_starts, h1_flat, wqkv, cos, sin)
-    wu = up_weight if spread else collect(up_weight)
-    attn, y, h3, hid, up, ge, *wu_full = into_feed(
-        n, m, spread, layer_in, gains, o.reshape(n, rows, heads * HD), wo, wg, wu
-    )
+    o_blocks = o.reshape(n, rows, heads * HD)
     if spread:
-        wu = wu_full[0].reshape(wg.shape)
-    layer_out, gain_four, df, dgate, dup = turn_feed(n, y, out_grad, gains, hid, wd, up, ge)
+        layer_out, dy, gain_later, h3_t, hid, _, _, df_t, dgate, dup, dattn_t, do = middle(
+            n, layer_in, out_grad, gains, o_blocks, wo, wg, up_weight, down_weight.T
+        )
+    else:
+        wu, wd = collect(up_weight), collect(down_weight.T)
+        attn, y, h3, hid, up, ge = into_feed(n, layer_in, gains, o_blocks, wo, wg, wu)
+        layer_out, gain_four, df, dgate, dup = turn_feed(n, y, out_grad, gains, hid, wd, up, ge)
     flat = lambda a: a.reshape(tokens, a.shape[-1])
     split = heads * HD
-    if spread and n * kvs == KV:
-        dy, gain_mid, dattn, do = out_of_feed(n, y, attn, out_grad, gains, dgate, dup, wg, wu, wo)
+    if spread:
         d = attend_back(heads, kvs, piece_starts, q, k, v, flat(do), cos, sin)
-        lefts = [flat(a).T for a in (h1, df, h3, dattn)]
+        lefts = [h1_t, df_t, h3_t, dattn_t]
         rights = [d, flat(hid), flat(dgate), flat(dup), o]
         in_grad, gain_one, qkv_sum, down_sum, gate_sum, up_sum, out_sum, kv = tail(
             n, m, split, layer_in, dy, gains, d.reshape(n, rows, -1), wqkv, lefts, rights
@@ -1597,6 +1956,7 @@
         d, qkv_part, up_sum = tie((d, qkv_part, up_sum))
         out_sum, qkv_sum = scatter_rows(out_part), scatter_rows(qkv_part)
         in_grad, gain_one = last(n, layer_in, dy, gains, d.reshape(n, rows, -1), wqkv)
+        gain_later = jnp.concatenate([gain_mid, gain_four], axis=0)
 
         own_rows = qkv_sum.shape[0]
         kv = qkv_sum[:, split:].reshape(own_rows, 2, kvs * HD).transpose(1, 0, 2)
@@ -1607,7 +1967,7 @@
             kv = lax.psum(kv, "tensor")
     kv = kv.astype(F32)
 
-    gain_grads = jnp.concatenate([gain_one, gain_mid, gain_four], axis=0)
+    gain_grads = jnp.concatenate([gain_one, gain_later], axis=0)
     gain_grads = sum_gains(n, m, gain_grads.reshape(4, m, width // m).transpose(1, 0, 2))
     return (
         layer_out,

time: 910 us -> 751 us (0.83)
  Pallas kernels: 819 us -> 678 us
  local copies, waits for them, and re-layouts: 60.9 us -> 40.8 us
    pallas_call x3 -> x1, Pallas kernels: 467 us -> 359 us  [middle(): pl.pallas_call(functools.partial(middle_kernel, n), out_shape=[jax.ShapeD...]
    pallas_call x1, Pallas kernels: 210 us -> 178 us  [tail(): pl.pallas_call(functools.partial(tail_kernel, n, split), out_shape=[jax.S...]
    reshape x4 -> x0, local copies, waits for them, and re-layouts: 26.9 us -> none  [the longest x3 20 us: body(): flat = lambda a: a.reshape(tokens, a.shape[-1])]
    unnamed x56 -> x70, local copies, waits for them, and re-layouts: 23.6 us -> 31.8 us
  transfers between devices with their start and end apart: 3 -> 2, of which waited for: 0 -> 0; matrix products, arithmetic and copies ran while one was open for 2% -> 0% of each run, Pallas kernels for 30% -> 14%
where the time goes in v3:
time: 751 us; the launch traced here: 739 us
  Pallas kernels  678 us (90%)
  local copies, waits for them, and re-layouts  40.8 us (5%)
  between operations  15 us (2%)
    pallas_call x1, Pallas kernels, middle(): pl.pallas_call(functools.partial(middle_kernel, n), out_shape=[jax.ShapeD...  359 us
    pallas_call x1, Pallas kernels, tail(): pl.pallas_call(functools.partial(tail_kernel, n, split), out_shape=[jax.S...  178 us
    pallas_call x1, Pallas kernels, first(): pl.pallas_call(functools.partial(first_kernel, n, spread), out_shape=outs...  84.8 us
    unnamed x70, local copies, waits for them, and re-layouts  31.8 us
    pallas_call x1, Pallas kernels, sum_gains(): pl.pallas_call(functools.partial(sum_gains_kernel, n, m), out_shape=jax.S...  26.7 us
  transfers between devices with their start and end apart: 2, of which 0 were waited for; matrix products, arithmetic and copies ran while one was open for 0% of the time, Pallas kernels for 14%

profile of v3, /device:TPU:0, one launch (start us, length us, event | category | flops | bytes accessed | tf_op | source)
XLA Modules:
  0.0 739.4 jit_solution(11895309816519392018)
XLA Ops:
  8.4 2.0 pad_maximum_fusion
  11.3 6.3 gains.1
  17.8 84.8 %first.1 = (bf16[4,256,2304]{2,1,0:T(8,128)(2,1)S(1)}, bf16[2304,2304]{1,0:T(8,128)(2,1)S(1)}, bf16[2304,1024]{1,0:T(8,128)(2,1)S(1)}) custom-call(bf16[256,2304]{1,0:T(8,128)(2,1)S(1)} %copy-done.1, f32[4,2304]{1,0:T(4,128)S(1)} %reshape.80.gains, bf16[288,2304]{1,0:T(8,128)(2,1)S(1)} %copy-done.4), custom_call_target="tpu_custom_call" | custom-call | bytes 314572800 | tf_op jit(solution)/shard_map/first/pallas_call | solution.py:572
  102.6 4.1 copy-done
  106.6 2.1 copy-done.2
  108.7 2.1 copy-done.10
  110.9 1.9 multiply_sine_fusion
  112.8 13.3 %attend.1 = (bf16[2,1024,256]{2,1,0:T(8,128)(2,1)S(1)}, bf16[1,1024,256]{2,1,0:T(8,128)(2,1)S(1)}, bf16[1,1024,256]{2,1,0:T(8,128)(2,1)S(1)}, bf16[1024,512]{1,0:T(8,128)(2,1)S(1)}) custom-call(s32[1,2]{1,0:T(1,128)S(1)} %copy-done.12, bf16[1024,2304]{1,0:T(8,128)(2,1)} %bitcast.25, bf16[2304,1024]{1,0:T(8,128)(2,1)} %all-gather.3.cloned.1.call-done.w.w_hbm, ...), custom_call_target="tpu_custom_call" | custom-call | flops 21474836480 | bytes 20971520 | tf_op jit(solution)/shard_map/attend/pallas_call | solution.py:649
  129.7 358.9 %middle.1 = (bf16[256,2304]{1,0:T(8,128)(2,1)}, f32[256,2304]{1,0:T(8,128)}, f32[3,2304]{1,0:T(4,128)}, bf16[2304,1024]{1,0:T(8,128)(2,1)}, bf16[4,256,2304]{2,1...) custom-call(bf16[256,2304]{1,0:T(8,128)(2,1)} %x.3, ...), custom_call_target="tpu_custom_call" | custom-call | bytes 1258291200 | tf_op jit(solution)/shard_map/middle/pallas_call | solution.py:1377
  490.7 1.2 copy-done.11
  491.9 1.2 copy-done.14
  495.2 10.2 %attend_back.1.refs_4_ = bf16[1024,1024]{1,0:T(8,128)(2,1)} custom-call(s32[1,2]{1,0:T(1,128)S(1)} %copy-done.12, bf16[2,1024,256]{2,1,0:T(8,128)(2,1)S(1)} %copy-done.14, bf16[1,1024,256]{2,1,0:T(8,128)(2,1)S(1)} %copy-done.16, bf16[1,1024,256]{2,1,0:T(8,128)(2,1)S(1)} %copy-done.18, bf16[1024,512]{1,0:T(8,128)(2,1)S(1)} %bitcast.26, ...), custom_call_target="tpu_custom_call" | custom-call | flops 32212254720 | bytes 20971520 | tf_op jit(solution)/shard_map/attend_back/pallas_call | solution.py:706
  505.5 178.0 %tail.1 = (bf16[256,2304]{1,0:T(8,128)(2,1)}, f32[1,2304]{1,0:T(1,128)}, f32[288,1024]{1,0:T(8,128)}, f32[288,2304]{1,0:T(8,128)}, f32[288,2304]{1,0:T(8,128)}, ...) custom-call(bf16[256,2304]{1,0:T(8,128)(2,1)} %x.3, f32[256,2304]{1,0:T(8,128)} %get-tuple-element.42.dy, ...), custom_call_target="tpu_custom_call" | custom-call | bytes 629145600 | tf_op jit(solution)/shard_map/tail/pallas_call | solution.py:1826
  684.4 26.7 %sum_gains.1 = f32[4,288]{1,0:T(4,128)S(1)} custom-call(f32[8,4,288]{2,1,0:T(4,128)S(1)} %bitcast.24), custom_call_target="tpu_custom_call" | custom-call | tf_op jit(solution)/shard_map/sum_gains/pallas_call | solution.py:484
  711.7 1.9 slice.23
  713.6 1.8 reshape.81
  715.4 1.8 fusion
  718.0 1.2 copy.35
  720.0 1.2 copy.34
  725.2 1.5 copy.47
  726.7 1.2 copy-done.20
  727.9 1.5 copy.48
  729.4 1.2 copy-done.19
  730.6 1.5 copy.49
  (81 shorter events, 16.8 us)
Async XLA Ops:
  7.2 105.6 %all-gather.3.cloned.1.call-start = ((), (), s32[]{:S(2)}) async-start(), calls=%async_computation | async-start | bytes 5308416 | tf_op jit(solution)/shard_map/all_gather | solution.py:1902
  7.2 3.9 copy-start.27
  7.3 3.9 copy-start.28
  7.3 3.9 copy-start.29
  7.3 3.9 copy-start.30
  7.3 10.4 %copy-start.4 = (bf16[288,2304]{1,0:T(8,128)(2,1)S(1)}, bf16[288,2304]{1,0:T(8,128)(2,1)}, u32[]{:S(2)}) copy-start(bf16[288,2304]{1,0:T(8,128)(2,1)} %refs_0_.1) | copy-start | bytes 3981316
  8.4 9.3 %copy-start.1 = (bf16[256,2304]{1,0:T(8,128)(2,1)S(1)}, bf16[256,2304]{1,0:T(8,128)(2,1)}, u32[]{:S(2)}) copy-start(bf16[256,2304]{1,0:T(8,128)(2,1)} %x.3) | copy-start | bytes 3538948
  10.4 119.3 %all-gather.5.cloned.1.call-start = ((), (), s32[]{:S(2)}) async-start(), calls=%async_computation.1 | async-start | bytes 2654208 | tf_op jit(solution)/shard_map/all_gather | solution.py:1902
  17.7 95.0 %copy-start.5 = (f32[4,2304]{1,0:T(4,128)}, f32[4,2304]{1,0:T(4,128)S(1)}, u32[]{:S(2)}) copy-start(f32[4,2304]{1,0:T(4,128)S(1)} %reshape.80.gains) | copy-start | bytes 110596
  17.7 95.1 %copy-start.12 = (s32[1,2]{1,0:T(1,128)S(1)}, s32[1,2]{1,0:T(1,128)}, u32[]{:S(2)}) copy-start(s32[1,2]{1,0:T(1,128)} %starts.3) | copy-start | bytes 28
  102.5 4.1 copy-start
  106.6 2.1 copy-start.2
  108.7 2.1 copy-start.10
  112.8 13.3 %copy-start.6 = (f32[1024,128]{1,0:T(8,128)}, f32[1024,128]{1,0:T(8,128)S(1)}, u32[]{:S(2)}) copy-start(f32[1024,128]{1,0:T(8,128)S(1)} %get-tuple-element.69.sin) | copy-start | bytes 1572868
  112.8 13.3 %copy-start.8 = (f32[1024,128]{1,0:T(8,128)}, f32[1024,128]{1,0:T(8,128)S(1)}, u32[]{:S(2)}) copy-start(f32[1024,128]{1,0:T(8,128)S(1)} %get-tuple-element.70.cos) | copy-start | bytes 1572868
  490.7 1.2 copy-start.11
  505.5 178.0 %copy-start.26 = (f32[3,2304]{1,0:T(4,128)S(1)}, f32[3,2304]{1,0:T(4,128)}, u32[]{:S(2)}) copy-start(f32[3,2304]{1,0:T(4,128)} %get-tuple-element.62) | copy-start | bytes 82948
  683.5 30.2 %copy-start.22 = (bf16[4,288,512]{2,1,0:T(8,128)(2,1)S(1)}, bf16[4,288,512]{2,1,0:T(8,128)(2,1)}, u32[]{:S(2)}) copy-start(bf16[4,288,512]{2,1,0:T(8,128)(2,1)} %get-tuple-element.56) | copy-start | bytes 3538948
  720.0 1.5 copy-start.23
  721.2 1.5 copy-start.24
  721.5 2.2 copy-start.25
  722.7 2.4 copy-start.21
  725.2 2.7 copy-start.20
  727.9 2.7 copy-start.19
  (9 other events, 8.9 us)
Sparse Core Ops, SparseCore 0:
  10.5 62.0 all-gather.2
  74.5 28.6 all-gather.4

commit v4 on v3

--- a/solution.py
+++ b/solution.py
@@ -578,7 +578,7 @@
         + line_scratch(n)
         + [pltpu.SemaphoreType.DMA((n,))]
         + (turn + spread_scratch() if spread else []),
-        compiler_params=params(1, 32),
+        compiler_params=params(1, 62),
         cost_estimate=cost(0, 300 << 20),
         name="first",
     )(x, gains, *([shard] if spread else []))
@@ -662,10 +662,9 @@
     )(starts, h1, w, cos, sin)
 
 
-def attend_back_kernel(heads, kvs, starts, q_in, k_in, v_in, do_in, cos, sin, out, dk, dv):
+def attend_back_kernel(heads, kvs, block, starts, q_in, k_in, v_in, do_in, cos, sin, out, dk, dv):
     tokens = q_in.shape[1]
     fan = heads // kvs
-    block = 256
     for seq in range(tokens // L):
         base = seq * L
         for g in range(kvs):
@@ -704,7 +703,7 @@
 def attend_back(heads, kvs, starts, q, k, v, do, cos, sin):
     tokens = q.shape[1]
     return pl.pallas_call(
-        functools.partial(attend_back_kernel, heads, kvs),
+        functools.partial(attend_back_kernel, heads, kvs, 256),
         out_shape=jax.ShapeDtypeStruct((tokens, (heads + 2 * kvs) * HD), BF16),
         in_specs=[SM, VM, VM, VM, VM, VM, VM],
         out_specs=VM,
@@ -1110,7 +1109,7 @@
 def middle_kernel(
     n, x_hbm, dout_hbm, gains, o_hbm, wo_hbm, wg_hbm, wu_hbm, wd_hbm,
     layer_out, dy_out, gain_out, h3_t, hid_out, up_out, ge_out, df_t, dgate_out, dup_out,
-    dattn_t, do_out,
+    dattn_t, do_out, dattn_own,
     xs, dout, wo, wg, wu, wd, part, landed, held, y, attn, pool, fold, flip,
     load, rs_send, rs_recv, ag_send, ag_recv, flip_sem, in_sem, out_sem, last_sem,
     wu_send, wu_recv, wu_local, wd_send, wd_recv, wd_local,
@@ -1327,7 +1326,7 @@
     loads[1].wait()
     loads[3].wait()
     before = None
-    for turn in range(6):
+    for turn in range(5):
         which, c = turn // 2, turn % 2
         total = sum_of[c][which]
         later = (turn + 1) // 2
@@ -1359,12 +1358,19 @@
             down_spread.middle()
             down_spread.turn()
         before = gather
+    total = sum_of[1][2]
+    total.land()
+    own_rows[2](1, total)
+    own_out = pltpu.make_async_copy(held.at[1, i], dattn_own, last_sem.at[2])
+    own_out.start()
+    total.done()
     before.finish()
     pltpu.make_async_copy(y, dy_out, last_sem.at[1]).start()
     for k in range(3):
         gain_out[k : k + 1, :] = jnp.sum(fold[k], axis=0, keepdims=True)
     pltpu.make_async_copy(xs, layer_out, last_sem.at[0]).wait()
     pltpu.make_async_copy(y, dy_out, last_sem.at[1]).wait()
+    own_out.wait()
 
 
 def middle(n, x, dout, gains, o, wo, wg, wu, wd):
@@ -1382,9 +1388,10 @@
             jax.ShapeDtypeStruct((3, width), F32),
             turned, blocks(wide), blocks(wide), blocks(wide),
             turned, blocks(wide), blocks(wide), turned, blocks(wo.shape[1]),
+            jax.ShapeDtypeStruct((piece, width), BF16),
         ],
         in_specs=[ANY, ANY, VM] + [ANY] * 5,
-        out_specs=[ANY, ANY, VM] + [ANY] * 9,
+        out_specs=[ANY, ANY, VM] + [ANY] * 10,
         scratch_shapes=[
             pltpu.VMEM(x.shape, BF16),
             pltpu.VMEM(x.shape, BF16),
@@ -1401,7 +1408,7 @@
             pltpu.VMEM((3, 8, width), F32),
             pltpu.VMEM((2, 768, piece), BF16),
             sem((4,)), sem((6, 2, n)), sem((6, n + 1)), sem((6, 2, n)), sem((6, n)),
-            sem((2,)), sem((4, 2, 2, 2)), sem((3, 2, 3, 2)), sem((2,)),
+            sem((2,)), sem((4, 2, 2, 2)), sem((3, 2, 3, 2)), sem((3,)),
         ]
         + spread_scratch() * 2,
         compiler_params=pltpu.CompilerParams(
@@ -1666,110 +1673,119 @@
     return bufs, sems
 
 
-def halves(width):
-    return [(0, width)] if width <= 1280 else [(0, width // 2), (width // 2, width // 2)]
-
-
-def tail_kernel(n, split, x, dy, gains, d_hbm, w_hbm, *refs):
-    lefts, rights, refs = refs[:4], refs[4:9], refs[9:]
-    in_grad, gain_out, *outs = refs[:7]
-    kv_out, refs = refs[7], refs[8:]
-    d, w, part, landed, mine, fold, stage, kv_stage = refs[:8]
-    load, rs_send, rs_recv, out_sem, kv_sem, kv_send, kv_recv = refs[8:15]
-    bufs, sems = refs[15:23], refs[23:31]
-    h1_t, df_t, h3_t, da_t = lefts
-    dqkv, hid, dgate, dup, o = rights
+def finish_kernel(
+    n, heads, kvs, units_of, starts, x_hbm, dy_hbm, gains, own_hbm, do_hbm, q_hbm, k_hbm, v_hbm,
+    cos_hbm, sin_hbm, wo_hbm, w_hbm, dattn_in, h1_t, df_t, h3_t, hid, dgate, dup, o_hbm,
+    in_grad, gain_out, out_qkv, out_down, out_gate, out_up, out_out, kv_out, dattn_t,
+    x, dy, held, do, q, k, v, cos, sin, wo, w, d, dk, dv, part, landed, fold, flip, stage, kv_stage,
+    load, do_load, ag_send, ag_recv, rs_send, rs_recv, flip_sem, out_sem, last_sem, kv_sem, kv_send,
+    kv_recv, *reduce_refs,
+):
     i = lax.axis_index("tensor")
     rows, width = x.shape
+    piece = rows // 2
     over = min(768, wide_tile(width))
-    loads = [
-        pltpu.make_async_copy(src, dst, load.at[k])
-        for k, (src, dst) in enumerate(((d_hbm, d), (w_hbm, w)))
-    ]
+    split = heads * HD
+    pairs = (
+        (own_hbm, held.at[i]), (wo_hbm, wo), (q_hbm, q), (k_hbm, k), (v_hbm, v), (cos_hbm, cos),
+        (sin_hbm, sin), (w_hbm, w), (x_hbm, x), (dy_hbm, dy),
+    )
+    loads = [pltpu.make_async_copy(a, b, load.at[j]) for j, (a, b) in enumerate(pairs)]
     for c in loads:
         c.start()
-
-    pairs = [(h1_t, dqkv), (df_t, hid), (h3_t, dgate), (h3_t, dup), (da_t, o)]
-    units, places = [], []
-    for k, (left, right) in enumerate(pairs):
-        for column, size in halves(right.shape[1]):
-            units.append(Reduce(len(units), left, right, column, size, bufs, sems))
-            places.append((k, column, size))
+    half_loads = [
+        pltpu.make_async_copy(
+            do_hbm.at[j, pl.ds(0, piece)], do.at[pl.ds(j * rows, piece)], do_load.at[j]
+        )
+        for j in range(n)
+    ]
+    for c in half_loads:
+        c.start()
+
+    lefts = dict(qkv=h1_t, down=df_t, gate=h3_t, up=h3_t, out=dattn_t)
+    rights = dict(qkv=d, down=hid, gate=dgate, up=dup, out=o_hbm)
+    outs = dict(qkv=out_qkv, down=out_down, gate=out_gate, up=out_up, out=out_out)
+    units = [
+        Reduce(u, lefts[name], rights[name], column, size, reduce_refs[:8], reduce_refs[8:])
+        for u, (name, column, size) in enumerate(units_of)
+    ]
+    count = len(units)
     units[0].load()
     me = units[0].me
 
     barrier = pltpu.get_barrier_semaphore()
     for shift in (units[0].dc, units[0].dx, units[0].dy):
         pl.semaphore_signal(barrier, 1, device_id={"dp": me + shift}, device_id_type=MESH)
-    for k in range(1, n):
-        peer = lax.rem(i + k, n)
+    for j in range(1, n):
+        peer = lax.rem(i + j, n)
         pl.semaphore_signal(barrier, 1, device_id={"tensor": peer}, device_id_type=MESH)
     pl.semaphore_wait(barrier, n + 2)
-    for c in loads:
-        c.wait()
+
+
+    pass_on, sent = gather_steps(i, n, held, ag_send, ag_recv)
+
+    def use(s):
+        block = block_at(i, n, s)
+        at = pl.ds(pl.multiple_of(block * rows + piece, piece), piece)
+        do[at, :] = dot_nn(held[block], wo[...]).astype(BF16)
+        flip_rows(held.at[block], dattn_t, block * rows + piece, flip, flip_sem)
+
+    def attention():
+        use(n - 1)
+        sent()
+        for c in half_loads + loads[2:7]:
+            c.wait()
+        attend_back_kernel(heads, kvs, 128, starts, q, k, v, do, cos, sin, d, dk, dv)
+
 
     def compute(t, block):
-        def tile(k):
-            at = pl.ds(pl.multiple_of(k * over, over), over)
-            part[block, :, at] = dot_nt(d[block], w[at, :]).astype(BF16)
+        mine = d[pl.ds(pl.multiple_of(block * rows, rows), rows), :]
+
+        def tile(j):
+            at = pl.ds(pl.multiple_of(j * over, over), over)
+            part[block, :, at] = dot_nt(mine, w[at, :]).astype(BF16)
 
         loop(width // over, tile)
 
     step, land, done = scatter_steps(i, n, part, landed, rs_send, rs_recv, compute)
 
-    def input_rows():
-        def tile(k):
-            at = pl.ds(pl.multiple_of(k * over, over), over)
-            mine[:, at] = dot_nt(d[i], w[at, :])
-
-        loop(width // over, tile)
+    def begin_line():
+        for c in loads[7:]:
+            c.wait()
+        step(0)
 
     def input_grad():
         land()
         scale = 1.0 + gains[0:1, :]
         fold[...] = jnp.zeros_like(fold)
-
         strip = strip_of(rows)
 
         def chunk(c):
             r = pl.ds(c * strip, strip)
-            dh1 = summed_rows(i, n, mine, landed, r)
-            v = x[r, :].astype(F32)
-            inv = inverse_rms(v)
-            in_grad[r, :] = (dy[r, :] + norm_back(dh1 * scale, v, inv)).astype(BF16)
-            fold[...] += fold_rows(dh1 * (v * inv))
+            dh1 = summed_rows(i, n, part.at[i], landed, r)
+            a = x[r, :].astype(F32)
+            inv = inverse_rms(a)
+            x[r, :] = (dy[r, :] + norm_back(dh1 * scale, a, inv)).astype(BF16)
+            fold[...] += fold_rows(dh1 * (a * inv))
 
         loop(rows // strip, chunk)
         gain_out[...] = jnp.sum(fold[...], axis=0, keepdims=True)
+        pltpu.make_async_copy(x, in_grad, last_sem.at[0]).start()
         done()
 
+
     def out_copy(u):
-        k, column, size = places[u]
+        name, column, size = units_of[u]
         return pltpu.make_async_copy(
             stage.at[u % 2, :, pl.ds(0, size)],
-            outs[k].at[:, pl.ds(column, size)],
+            outs[name].at[:, pl.ds(column, size)],
             out_sem.at[u % 2],
         )
 
-    def kv_copy(k):
+    def kv_copy(j, owner, peer):
         return pltpu.make_async_remote_copy(
-            kv_stage,
-            kv_out.at[i],
-            kv_send.at[k],
-            kv_recv.at[k],
-            device_id={"tensor": lax.rem(i + k, n)},
-            device_id_type=MESH,
-        )
-
-    def kv_arrival(k):
-        from_peer = lax.rem(i + n - k, n)
-        return pltpu.make_async_remote_copy(
-            kv_stage,
-            kv_out.at[from_peer],
-            kv_send.at[k],
-            kv_recv.at[k],
-            device_id={"tensor": from_peer},
-            device_id_type=MESH,
+            kv_stage, kv_out.at[owner], kv_send.at[j], kv_recv.at[j],
+            device_id={"tensor": peer}, device_id_type=MESH,
         )
 
     kv_own = pltpu.make_async_copy(kv_stage, kv_out.at[i], kv_sem.at[0])
@@ -1777,23 +1793,35 @@
     def finish(u):
         if u >= 2:
             out_copy(u - 2).wait()
-        size = places[u][2]
+        name, column, size = units_of[u]
+        keys = name == "qkv" and column == split
 
         def put(r, total):
             stage[u % 2, r, pl.ds(0, size)] = total
-            if u == 0:
-                kv_stage[r, :] = total[:, split:].astype(BF16)
+            if keys:
+                kv_stage[r, :] = total.astype(BF16)
 
         units[u].end(put)
         out_copy(u).start()
-        if u == 0:
-            for k in range(1, n):
-                kv_copy(k).start()
+        if keys:
+            for j in range(1, n):
+                kv_copy(j, i, lax.rem(i + j, n)).start()
             kv_own.start()
 
-    count = len(units)
-    line = [functools.partial(step, jnp.int32(k)) for k in range(n - 1)] + [input_rows, input_grad]
-    for u in range(count + 2):
+    def passing(s):
+        pass_on(s)
+        use(s - 1)
+
+    line = [[functools.partial(passing, s)] for s in range(1, n)]
+    line[-1] += [attention, begin_line]
+    for t in range(1, n - 1):
+        line += [[], [functools.partial(step, t)]]
+    line += [[lambda: compute(n - 1, i)], [input_grad]]
+
+    loads[0].wait()
+    loads[1].wait()
+    pass_on(0)
+    for u in range(max(count + 2, len(line))):
         if u < count:
             units[u].begin()
             if u + 1 < count:
@@ -1801,57 +1829,135 @@
             units[u].middle()
         if 1 <= u <= count:
             units[u - 1].turn()
-        if u >= 2:
+        if 2 <= u < count + 2:
             finish(u - 2)
-        if u < len(line):
-            line[u]()
-    for u in range(count + 2, len(line)):
-        line[u]()
+        for action in line[u] if u < len(line) else ():
+            action()
     for u in range(max(0, count - 2), count):
         out_copy(u).wait()
+    pltpu.make_async_copy(x, in_grad, last_sem.at[0]).wait()
     kv_own.wait()
-    for k in range(1, n):
-        kv_copy(k).wait_send()
-        kv_arrival(k).wait_recv()
-
-
-def tail(n, m, split, x, dy, gains, d, w, lefts, rights):
+    for j in range(1, n):
+        kv_copy(j, i, lax.rem(i + j, n)).wait_send()
+        peer = lax.rem(i + n - j, n)
+        kv_copy(j, peer, peer).wait_recv()
+
+
+def pieces(name, width, most=768):
+    count = next(c for c in range(1, width) if width % (c * 128) == 0 and width // c <= most)
+    return [(name, k * (width // count), width // count) for k in range(count)]
+
+
+def finish(n, m, heads, kvs, starts, x, dy, gains, own, do, q, k, v, cos, sin, wo, w, turned, rights, o):
     rows, width = x.shape
     tokens = n * rows
     own_rows = width // m
-    widest = max(size for right in rights for _, size in halves(right.shape[1]))
+    split, across = heads * HD, w.shape[1]
+    down, gate, up = (pieces(s, r.shape[1]) for s, r in zip(("down", "gate", "up"), rights))
+    early = (down + gate)[: n + 1]
+    late = (down + gate)[n + 1 :] + up + pieces("out", o.shape[1])
+    units = early + [("qkv", split, across - split), ("qkv", 0, split)] + late
+    widest = max(size for _, _, size in units)
     bufs, sems = reduce_scratch(own_rows, tokens, widest)
     sem = pltpu.SemaphoreType.DMA
-    kv_width = rights[0].shape[1] - split
+    shape = lambda a, b, t=F32: jax.ShapeDtypeStruct((a, b), t)
     return pl.pallas_call(
-        functools.partial(tail_kernel, n, split),
-        out_shape=[
-            jax.ShapeDtypeStruct((rows, width), BF16),
-            jax.ShapeDtypeStruct((1, width), F32),
-        ]
-        + [jax.ShapeDtypeStruct((own_rows, right.shape[1]), F32) for right in rights]
-        + [jax.ShapeDtypeStruct((n, own_rows, kv_width), BF16)],
-        in_specs=[VM, VM, VM] + [ANY] * 11,
-        out_specs=[VM, VM] + [ANY] * 6,
+        functools.partial(finish_kernel, n, heads, kvs, units),
+        out_shape=[shape(rows, width, BF16), shape(1, width), shape(own_rows, across)]
+        + [shape(own_rows, r.shape[1]) for r in (*rights, o)]
+        + [jax.ShapeDtypeStruct((n, own_rows, across - split), BF16), shape(width, tokens, BF16)],
+        in_specs=[SM, ANY, ANY, VM] + [ANY] * 17,
+        out_specs=[ANY, VM] + [ANY] * 7,
         scratch_shapes=[
-            pltpu.VMEM(d.shape, BF16),
+            pltpu.VMEM(x.shape, BF16),
+            pltpu.VMEM(x.shape, F32),
+            pltpu.VMEM((n, rows // 2, width), BF16),
+            pltpu.VMEM((tokens, split), BF16),
+            pltpu.VMEM(q.shape, BF16),
+            pltpu.VMEM(k.shape, BF16),
+            pltpu.VMEM(v.shape, BF16),
+            pltpu.VMEM(cos.shape, F32),
+            pltpu.VMEM(sin.shape, F32),
+            pltpu.VMEM(wo.shape, BF16),
             pltpu.VMEM(w.shape, BF16),
+            pltpu.VMEM((tokens, across), BF16),
+            pltpu.VMEM((L, HD), F32),
+            pltpu.VMEM((L, HD), F32),
             pltpu.VMEM((n, rows, width), BF16),
             pltpu.VMEM((n + 1, rows, width), BF16),
-            pltpu.VMEM((rows, width), F32),
             pltpu.VMEM((8, width), F32),
+            pltpu.VMEM((2, 768, rows // 2), BF16),
             pltpu.VMEM((2, own_rows, widest), F32),
-            pltpu.VMEM((own_rows, kv_width), BF16),
-            sem((2,)),
+            pltpu.VMEM((own_rows, across - split), BF16),
+            sem((10,)), sem((n,)),
         ]
-        + line_scratch(n)
-        + [sem((2,)), sem((1,)), sem((n,)), sem((n,))]
+        + line_scratch(n) * 2
+        + [sem((2,)), sem((2,)), sem((1,)), sem((1,)), sem((n,)), sem((n,))]
         + bufs
         + sems,
-        compiler_params=params(7, 62),
+        input_output_aliases={13: 8},
+        compiler_params=pltpu.CompilerParams(
+            collective_id=7, has_side_effects=True, vmem_limit_bytes=(127 << 20) // 2
+        ),
         cost_estimate=cost(0, 600 << 20),
-        name="tail",
-    )(x, dy, gains, d, w, *lefts, *rights)
+        name="finish",
+    )(starts, x, dy, gains, own, do, q, k, v, cos, sin, wo, w, turned[3], *turned[:3], *rights, o)
+
+
+def deliver_kernel(count, *refs):
+    sources, qkv, kv_hbm = refs[:count], refs[count], refs[count + 1]
+    targets, k_out, v_out = refs[count + 2 : 2 * count + 3], *refs[2 * count + 3 : 2 * count + 5]
+    stages = refs[2 * count + 5 : 3 * count + 6]
+    kv, k_s, v_s, load, store = refs[3 * count + 6 :]
+    n, rows, across = kv.shape
+    split = targets[-1].shape[1]
+    sources = (*sources, qkv.at[:, pl.ds(0, split)])
+    first = pltpu.make_async_copy(kv_hbm, kv, load.at[count + 1])
+    first.start()
+    loads = [pltpu.make_async_copy(a, b, load.at[j]) for j, (a, b) in enumerate(zip(sources, stages))]
+    for c in loads:
+        c.start()
+    stores = [
+        pltpu.make_async_copy(a, b, store.at[j])
+        for j, (a, b) in enumerate(zip((*stages, k_s, v_s), (*targets, k_out, v_out)))
+    ]
+    first.wait()
+    half = across // 2
+    for j in range(n):
+        k_s[:, j * half : (j + 1) * half] = kv[j, :, :half].astype(F32)
+        v_s[:, j * half : (j + 1) * half] = kv[j, :, half:].astype(F32)
+    stores[-2].start()
+    stores[-1].start()
+    for a, b in zip(loads, stores):
+        a.wait()
+        b.start()
+    for c in stores:
+        c.wait()
+
+
+def deliver(split, sources, qkv, kv):
+    n, rows, across = kv.shape
+    shape = lambda a: jax.ShapeDtypeStruct(a.shape, a.dtype)
+    wide = jax.ShapeDtypeStruct((rows, n * across // 2), F32)
+    count = len(sources)
+    return pl.pallas_call(
+        functools.partial(deliver_kernel, count),
+        out_shape=[shape(a) for a in sources] + [jax.ShapeDtypeStruct((rows, split), F32), wide, wide],
+        in_specs=[ANY] * (count + 2),
+        out_specs=[ANY] * (count + 3),
+        scratch_shapes=[pltpu.VMEM(a.shape, a.dtype) for a in sources]
+        + [
+            pltpu.VMEM((rows, split), F32),
+            pltpu.VMEM(kv.shape, BF16),
+            pltpu.VMEM(wide.shape, F32),
+            pltpu.VMEM(wide.shape, F32),
+            pltpu.SemaphoreType.DMA((count + 2,)),
+            pltpu.SemaphoreType.DMA((count + 3,)),
+        ],
+        compiler_params=pltpu.CompilerParams(vmem_limit_bytes=62 << 20),
+        cost_estimate=cost(0, 40 << 20),
+        name="deliver",
+    )(*sources, qkv, kv)
 
 
 def rope_tables():
@@ -1922,7 +2028,7 @@
     q, k, v, o = attend(heads, kvs, piece_starts, h1_flat, wqkv, cos, sin)
     o_blocks = o.reshape(n, rows, heads * HD)
     if spread:
-        layer_out, dy, gain_later, h3_t, hid, _, _, df_t, dgate, dup, dattn_t, do = middle(
+        layer_out, dy, gain_later, h3_t, hid, _, _, df_t, dgate, dup, dattn_t, do, own = middle(
             n, layer_in, out_grad, gains, o_blocks, wo, wg, up_weight, down_weight.T
         )
     else:
@@ -1932,14 +2038,10 @@
     flat = lambda a: a.reshape(tokens, a.shape[-1])
     split = heads * HD
     if spread:
-        d = attend_back(heads, kvs, piece_starts, q, k, v, flat(do), cos, sin)
-        lefts = [h1_t, df_t, h3_t, dattn_t]
-        rights = [d, flat(hid), flat(dgate), flat(dup), o]
-        in_grad, gain_one, qkv_sum, down_sum, gate_sum, up_sum, out_sum, kv = tail(
-            n, m, split, layer_in, dy, gains, d.reshape(n, rows, -1), wqkv, lefts, rights
-        )
-        own_rows = qkv_sum.shape[0]
-        kv = kv.reshape(n, own_rows, 2, kvs * HD).transpose(2, 1, 0, 3).reshape(2, own_rows, KV * HD)
+        in_grad, gain_one, qkv_sum, down_sum, gate_sum, up_sum, out_sum, kv, _ = finish(
+            n, m, heads, kvs, piece_starts, layer_in, dy, gains, own, do, q, k, v, cos, sin, wo, wqkv,
+            (h1_t, df_t, h3_t, dattn_t), (flat(hid), flat(dgate), flat(dup)), o,
+        )
     else:
         tie = lax.optimization_barrier
         down_part = weight_grad(flat(df), flat(hid))
@@ -1965,16 +2067,20 @@
         else:
             kv = lax.dynamic_update_slice_in_dim(jnp.zeros((2, own_rows, KV * HD), BF16), kv, kv_at, 2)
             kv = lax.psum(kv, "tensor")
-    kv = kv.astype(F32)
-
     gain_grads = jnp.concatenate([gain_one, gain_later], axis=0)
     gain_grads = sum_gains(n, m, gain_grads.reshape(4, m, width // m).transpose(1, 0, 2))
+    if spread:
+        layer_out, in_grad, down_sum, gate_sum, up_sum, out_sum, q_sum, k_sum, v_sum = deliver(
+            split, (layer_out, in_grad, down_sum, gate_sum, up_sum, out_sum), qkv_sum, kv
+        )
+    else:
+        q_sum, k_sum, v_sum = qkv_sum[:, :split].astype(F32), kv[0].astype(F32), kv[1].astype(F32)
     return (
         layer_out,
         in_grad,
-        qkv_sum[:, :split].astype(F32),
-        kv[0],
-        kv[1],
+        q_sum,
+        k_sum,
+        v_sum,
         out_sum.astype(F32).T,
         gate_sum.astype(F32),
         up_sum.astype(F32),

time: 751 us -> 688 us (0.916)
  local copies, waits for them, and re-layouts: 40.8 us -> 6.01 us
  Pallas kernels: 678 us -> 650 us
    pallas_call x1, Pallas kernels: 359 us -> 319 us  [middle(): pl.pallas_call(functools.partial(middle_kernel, n), out_shape=[jax.ShapeD...]
    unnamed x70 -> x24, local copies, waits for them, and re-layouts: 31.8 us -> 3.56 us
    pallas_call x2, Pallas kernels: 188 us -> 209 us  [the longest x1 200 us: finish(): pl.pallas_call(functools.partial(finish_kernel, n, heads, kvs, units), ou...]
    pallas_call x1, Pallas kernels: 26.7 us -> 15 us  [sum_gains(): pl.pallas_call(functools.partial(sum_gains_kernel, n, m), out_shape=jax.S...]
  transfers between devices with their start and end apart: 2 -> 2, of which waited for: 0 -> 0; matrix products, arithmetic and copies ran while one was open for 0% -> 0% of each run, Pallas kernels for 14% -> 16%
where the time goes in v4:
time: 688 us; the launch traced here: 676 us
  Pallas kernels  650 us (94%)
  between operations  14.6 us (2%)
    pallas_call x1, Pallas kernels, middle(): pl.pallas_call(functools.partial(middle_kernel, n), out_shape=[jax.ShapeD...  319 us
    pallas_call x1, Pallas kernels, finish(): pl.pallas_call(functools.partial(finish_kernel, n, heads, kvs, units), ou...  200 us
    pallas_call x1, Pallas kernels, first(): pl.pallas_call(functools.partial(first_kernel, n, spread), out_shape=outs...  87.2 us
    pallas_call x1, Pallas kernels, sum_gains(): pl.pallas_call(functools.partial(sum_gains_kernel, n, m), out_shape=jax.S...  15 us
  transfers between devices with their start and end apart: 2, of which 0 were waited for; matrix products, arithmetic and copies ran while one was open for 0% of the time, Pallas kernels for 16%

profile of v4, /device:TPU:0, one launch (start us, length us, event | category | flops | bytes accessed | tf_op | source)
XLA Modules:
  0.0 675.6 jit_solution(4052105092533413091)
XLA Ops:
  7.2 0.0 all-gather.3.cloned.1.call-start
  7.3 1.0 constant_dynamic-slice_fusion
  8.3 1.9 pad_maximum_fusion
  10.2 0.0 all-gather.3.cloned.1.call-update
  10.2 0.0 all-gather.5.cloned.1.call-start
  10.2 0.7 all-gather.5.cloned.1.call-update
  11.0 6.3 gains.1
  17.4 0.7 reshape.63.gains
  18.1 87.2 %first.1 = (bf16[4,256,2304]{2,1,0:T(8,128)(2,1)}, bf16[2304,2304]{1,0:T(8,128)(2,1)}, bf16[2304,1024]{1,0:T(8,128)(2,1)}) custom-call(bf16[256,2304]{1,0:T(8,128)(2,1)} %x_hbm.3, f32[4,2304]{1,0:T(4,128)} %reshape.63.gains, bf16[288,2304]{1,0:T(8,128)(2,1)} %refs_0_.1), custom_call_target="tpu_custom_call" | custom-call | bytes 314572800 | tf_op jit(solution)/shard_map/first/pallas_call | solution.py:572
  105.3 1.9 multiply_sine_fusion
  107.2 0.0 copy-start.1
  107.2 0.0 all-gather.3.cloned.1.call-done.w.w_hbm
  107.3 13.5 %attend.1 = (bf16[2,1024,256]{2,1,0:T(8,128)(2,1)S(1)}, bf16[1,1024,256]{2,1,0:T(8,128)(2,1)S(1)}, bf16[1,1024,256]{2,1,0:T(8,128)(2,1)S(1)}, bf16[1024,512]{1,0:T(8,128)(2,1)S(1)}) custom-call(s32[1,2]{1,0:T(1,128)S(1)} %copy-done.6, bf16[1024,2304]{1,0:T(8,128)(2,1)} %bitcast.21, bf16[2304,1024]{1,0:T(8,128)(2,1)} %all-gather.3.cloned.1.call-done.w.w_hbm, ...), custom_call_target="tpu_custom_call" | custom-call | flops 21474836480 | bytes 20971520 | tf_op jit(solution)/shard_map/attend/pallas_call | solution.py:649
  120.8 1.0 copy-done
  121.7 1.0 copy-done.3
  122.7 0.8 copy-done.4
  123.5 0.8 copy-done.5
  124.3 318.6 %middle.1 = (bf16[256,2304]{1,0:T(8,128)(2,1)}, f32[256,2304]{1,0:T(8,128)}, f32[3,2304]{1,0:T(4,128)}, bf16[2304,1024]{1,0:T(8,128)(2,1)}, bf16[4,256,2304]{2,1...) custom-call(bf16[256,2304]{1,0:T(8,128)(2,1)} %x_hbm.3, ...), custom_call_target="tpu_custom_call" | custom-call | bytes 1258291200 | tf_op jit(solution)/shard_map/middle/pallas_call | solution.py:1383
  442.9 200.2 %finish.1 = (bf16[256,2304]{1,0:T(8,128)(2,1)}, f32[1,2304]{1,0:T(1,128)}, f32[288,1024]{1,0:T(8,128)}, f32[288,2304]{1,0:T(8,128)}, f32[288,2304]{1,0:T(8,128)}...) custom-call(s32[1,2]{1,0:T(1,128)} %starts.3, ...), custom_call_target="tpu_custom_call", output_to_operand_aliasing={{8}: (13, {})} | custom-call | bytes 629145600 | tf_op jit(solution)/shard_map/finish/pallas_call | solution.py:1864
  643.1 0.7 pad_maximum_fusion.1
  643.8 0.1 reshape.62
  643.9 15.0 %sum_gains.1 = f32[4,288]{1,0:T(4,128)S(1)} custom-call(f32[8,4,288]{2,1,0:T(4,128)S(1)} %bitcast.15), custom_call_target="tpu_custom_call" | custom-call | tf_op jit(solution)/shard_map/sum_gains/pallas_call | solution.py:484
  658.9 0.6 slice_reduce_fusion
  659.5 9.0 %deliver.1 = (bf16[256,2304]{1,0:T(8,128)(2,1)}, bf16[256,2304]{1,0:T(8,128)(2,1)}, f32[288,2304]{1,0:T(8,128)}, f32[288,2304]{1,0:T(8,128)}, f32[288,2304]{1,0:...) custom-call(bf16[256,2304]{1,0:T(8,128)(2,1)} %get-tuple-element.51.refs_0_, ...), custom_call_target="tpu_custom_call" | custom-call | bytes 41943040 | tf_op jit(solution)/shard_map/deliver/pallas_call | solution.py:1943
  (30 shorter events, 0.1 us)
Async XLA Ops:
  7.2 3.8 copy-start.8
  7.2 3.8 copy-start.9
  7.2 3.8 copy-start.10
  7.2 3.8 copy-start.11
  7.2 100.0 %all-gather.3.cloned.1.call-start = ((), (), s32[]{:S(2)}) async-start(), calls=%async_computation | async-start | bytes 5308416 | tf_op jit(solution)/shard_map/all_gather | solution.py:2008
  10.2 97.1 %copy-start.6 = (s32[1,2]{1,0:T(1,128)S(1)}, s32[1,2]{1,0:T(1,128)}, u32[]{:S(2)}) copy-start(s32[1,2]{1,0:T(1,128)} %starts.3) | copy-start | bytes 28
  10.2 114.1 %all-gather.5.cloned.1.call-start = ((), (), s32[]{:S(2)}) async-start(), calls=%async_computation.1 | async-start | bytes 2654208 | tf_op jit(solution)/shard_map/all_gather | solution.py:2008
  107.2 13.5 %copy-start.1 = (f32[1024,128]{1,0:T(8,128)}, f32[1024,128]{1,0:T(8,128)S(1)}, u32[]{:S(2)}) copy-start(f32[1024,128]{1,0:T(8,128)S(1)} %get-tuple-element.87.sin.sin_hbm) | copy-start | bytes 1572868
  107.2 13.5 %copy-start.2 = (f32[1024,128]{1,0:T(8,128)}, f32[1024,128]{1,0:T(8,128)S(1)}, u32[]{:S(2)}) copy-start(f32[1024,128]{1,0:T(8,128)S(1)} %get-tuple-element.88.cos.cos_hbm) | copy-start | bytes 1572868
  120.7 1.0 copy-start
  121.7 1.0 copy-start.3
  122.7 0.8 copy-start.4
  123.5 0.8 copy-start.5
  442.8 200.2 %copy-start.7 = (f32[3,2304]{1,0:T(4,128)S(1)}, f32[3,2304]{1,0:T(4,128)}, u32[]{:S(2)}) copy-start(f32[3,2304]{1,0:T(4,128)} %get-tuple-element.82) | copy-start | bytes 82948
Sparse Core Ops, SparseCore 0:
  10.5 60.6 all-gather.2
  73.1 31.9 all-gather.4

commit v5 on v4

--- a/solution.py
+++ b/solution.py
@@ -2,6 +2,7 @@
 
 import jax
 import jax.numpy as jnp
+import numpy as np
 from jax import lax
 from jax.experimental import pallas as pl
 from jax.experimental.pallas import tpu as pltpu
@@ -23,6 +24,7 @@
 SM = pl.BlockSpec(memory_space=pltpu.SMEM)
 ROWS = 16
 TILE = 256
+AHEAD = 4
 
 
 def dot_nn(a, b):
@@ -523,7 +525,7 @@
     def keep(s, block):
         pltpu.make_async_copy(held.at[block], full.at[block], out_sem.at[s]).start()
         if spread:
-            flip_rows(held.at[block], turned, block * rows, turn, turn_sem)
+            flip_rows(held.at[block], turned, block * rows, turn, turn_sem, s == 0)
             pl.when(s == min(1, n - 1))(gather.middle)
             pl.when(s == min(2, n - 1))(gather.turn)
 
@@ -535,13 +537,13 @@
 
     loop(n, finish)
     if spread:
+        flip_end(turned, turn, turn_sem)
         gather.end()
 
 
-def flip_rows(block, target, column, stage, sem):
+def flip_rows(block, target, column, stage, sem, fresh):
     rows, width = block.shape
     size = stage.shape[1]
-    pieces = width // size
 
     def copy(k):
         return pltpu.make_async_copy(
@@ -550,15 +552,25 @@
             sem.at[k % 2],
         )
 
-    for k in range(pieces):
+    for k in range(width // size):
         if k >= 2:
             copy(k - 2).wait()
+        elif fresh is False:
+            copy(k).wait()
+        elif fresh is not True:
+            pl.when(jnp.logical_not(fresh))(lambda k=k: copy(k).wait())
         for j in range(size // 256):
             at = pl.ds(k * size + j * 256, 256)
             stage[k % 2, pl.ds(j * 256, 256), :] = block[:, at].T
         copy(k).start()
-    for k in range(max(0, pieces - 2), pieces):
-        copy(k).wait()
+
+
+def flip_end(target, stage, sem):
+    size, rows = stage.shape[1:]
+    for k in range(2):
+        pltpu.make_async_copy(
+            stage.at[k], target.at[pl.ds(k * size, size), pl.ds(0, rows)], sem.at[k]
+        ).wait()
 
 
 def first(n, m, x, gains, shard):
@@ -612,13 +624,37 @@
     return w * pl.reciprocal(jnp.sum(w, axis=-1, keepdims=True)), bent
 
 
-def attend_kernel(heads, kvs, starts, h1, w, cos, sin, q_out, k_out, v_out, o_out):
+def attend_kernel(
+    heads, kvs, starts, h1_hbm, w_hbm, cos_hbm, sin_hbm, q_hbm, k_hbm, v_hbm, o_hbm,
+    h1, w, cos, sin, q_out, k_out, v_out, o_out, load, h1_load, store, o_store,
+):
     tokens = h1.shape[0]
     fan = heads // kvs
     block = 256
+    pairs = ((w_hbm, w), (cos_hbm, cos), (sin_hbm, sin))
+    loads = [pltpu.make_async_copy(a, b, load.at[j]) for j, (a, b) in enumerate(pairs)]
+    outs = ((q_out, q_hbm), (k_out, k_hbm), (v_out, v_hbm))
+    stores = [pltpu.make_async_copy(a, b, store.at[j]) for j, (a, b) in enumerate(outs)]
+
+    def rows_of(b):
+        return pl.ds(pl.multiple_of(b * block, block), block)
+
+    def h1_copy(b):
+        return pltpu.make_async_copy(h1_hbm.at[rows_of(b)], h1.at[rows_of(b)], h1_load.at[b])
+
+    def o_copy(b):
+        return pltpu.make_async_copy(o_out.at[rows_of(b)], o_hbm.at[rows_of(b)], o_store.at[b])
+
+    for c in loads:
+        c.start()
+    for b in range(tokens // block):
+        h1_copy(b).start()
+    for c in loads:
+        c.wait()
 
     def project(b):
-        r = pl.ds(pl.multiple_of(b * block, block), block)
+        h1_copy(b).wait()
+        r = rows_of(b)
         at = pl.ds(pl.multiple_of(lax.rem(b * block, L), block), block)
         c, s = cos[at, :], sin[at, :]
         x = h1[r, :]
@@ -632,6 +668,8 @@
             v_out[g, r, :] = u.astype(BF16)
 
     loop(tokens // block, project)
+    for c in stores:
+        c.start()
     for seq in range(tokens // L):
         base = seq * L
         for row in range(0, L, block):
@@ -642,21 +680,26 @@
                 p, _ = weights_of(q, k_out[h // fan, base : base + span, :], limit)
                 o = dot_nn(p.astype(BF16), v_out[h // fan, base : base + span, :])
                 o_out[base + row : base + row + block, h * HD : (h + 1) * HD] = o.astype(BF16)
+            o_copy((base + row) // block).start()
+    for c in stores:
+        c.wait()
+    for b in range(tokens // block):
+        o_copy(b).wait()
 
 
 def attend(heads, kvs, starts, h1, w, cos, sin):
     tokens = h1.shape[0]
+    outs = [(heads, tokens, HD), (kvs, tokens, HD), (kvs, tokens, HD), (tokens, heads * HD)]
+    sem = pltpu.SemaphoreType.DMA
     return pl.pallas_call(
         functools.partial(attend_kernel, heads, kvs),
-        out_shape=[
-            jax.ShapeDtypeStruct((heads, tokens, HD), BF16),
-            jax.ShapeDtypeStruct((kvs, tokens, HD), BF16),
-            jax.ShapeDtypeStruct((kvs, tokens, HD), BF16),
-            jax.ShapeDtypeStruct((tokens, heads * HD), BF16),
-        ],
-        in_specs=[SM, VM, VM, VM, VM],
-        out_specs=[VM, VM, VM, VM],
-        compiler_params=pltpu.CompilerParams(vmem_limit_bytes=48 << 20),
+        out_shape=[jax.ShapeDtypeStruct(o, BF16) for o in outs],
+        in_specs=[SM, ANY, ANY, ANY, ANY],
+        out_specs=[ANY] * 4,
+        scratch_shapes=[pltpu.VMEM(a.shape, a.dtype) for a in (h1, w, cos, sin)]
+        + [pltpu.VMEM(o, BF16) for o in outs]
+        + [sem((3,)), sem((tokens // 256,)), sem((3,)), sem((tokens // 256,))],
+        compiler_params=pltpu.CompilerParams(vmem_limit_bytes=62 << 20),
         cost_estimate=cost(20 << 30, 20 << 20),
         name="attend",
     )(starts, h1, w, cos, sin)
@@ -1185,7 +1228,8 @@
             block = block_at(i, n, s)
             self.compute(s, block)
             column = block * rows + self.c * piece
-            flip_rows(held.at[self.c, block], self.full, column, flip, flip_sem)
+            flip_rows(held.at[self.c, block], self.full, column, flip, flip_sem, True)
+            flip_end(self.full, flip, flip_sem)
 
         def finish(self):
             self.use(n - 1)
@@ -1497,7 +1541,7 @@
         me = lax.axis_index("dp")
         c, x, y = me % 2, (me // 2) % 2, me // 4
         self.me, self.set, self.third, self.fifth, self.width = me, u % 2, u % 3, u % 5, width
-        self.left, self.right, self.column = left, right, column
+        self.left, self.right, self.column, self.next = left, right, column, None
         self.dx, self.dy, self.dc = 2 - 4 * x, 4 - 8 * y, 1 - 2 * c
         self.lefts, self.rights, self.pair, self.pair_in, self.sums, self.far_in, self.xy_in, self.own = bufs
         (
@@ -1517,7 +1561,7 @@
 
     def left_copy(self, q):
         r = pl.ds(self.owner(q) * self.rows, self.rows)
-        return pltpu.make_async_copy(self.left.at[r], self.lefts.at[q % 2], self.left_sem.at[q % 2])
+        return pltpu.make_async_copy(self.left.at[r], self.lefts.at[q % AHEAD], self.left_sem.at[q % AHEAD])
 
     def right_copy(self):
         return pltpu.make_async_copy(
@@ -1561,24 +1605,26 @@
 
     def product(self, q, put):
         self.left_copy(q).wait()
-        if isinstance(q, int):
-            if q < 7:
-                self.left_copy(q + 1).start()
-        else:
-            self.left_copy(q + 1).start()
+        later = q + AHEAD - 1
+        if not isinstance(q, int) or later < 8:
+            self.left_copy(later).start()
+        elif self.next:
+            self.next.left_copy(later - 8).start()
         tile = wide_tile(self.width)
 
         def one(t):
             at = pl.ds(pl.multiple_of(t * tile, tile), tile)
-            put(at, dot_nn(self.lefts[q % 2], self.rights[self.set, :, at]))
+            put(at, dot_nn(self.lefts[q % AHEAD], self.rights[self.set, :, at]))
 
         loop(self.width // tile, one)
 
-    def load(self):
+    def load(self, first=False):
         self.right_copy().start()
+        if first:
+            for q in range(AHEAD - 1):
+                self.left_copy(q).start()
 
     def begin(self):
-        self.left_copy(0).start()
         self.right_copy().wait()
 
         def chunk(k):
@@ -1657,7 +1703,7 @@
 def reduce_scratch(rows, tokens, widest):
     sem = pltpu.SemaphoreType.DMA
     bufs = [
-        pltpu.VMEM((2, rows, tokens), BF16),
+        pltpu.VMEM((AHEAD, rows, tokens), BF16),
         pltpu.VMEM((2, tokens, widest), BF16),
         pltpu.VMEM((2, 4, rows, widest), BF16),
         pltpu.VMEM((2, 4, rows, widest), BF16),
@@ -1667,19 +1713,20 @@
         pltpu.VMEM((3, rows, widest), F32),
     ]
     sems = [
-        sem((2,)), sem((2,)), sem((2, 4)), sem((2, 4)),
+        sem((AHEAD,)), sem((2,)), sem((2, 4)), sem((2, 4)),
         sem((3, 2)), sem((3, 2)), sem((3, 2, 2)), sem((5, 2, 2)),
     ]
     return bufs, sems
 
 
 def finish_kernel(
-    n, heads, kvs, units_of, starts, x_hbm, dy_hbm, gains, own_hbm, do_hbm, q_hbm, k_hbm, v_hbm,
+    n, m, heads, kvs, units_of, starts, x_hbm, dy_hbm, gains, own_hbm, do_hbm, q_hbm, k_hbm, v_hbm,
     cos_hbm, sin_hbm, wo_hbm, w_hbm, dattn_in, h1_t, df_t, h3_t, hid, dgate, dup, o_hbm,
+    later_gains,
     in_grad, gain_out, out_qkv, out_down, out_gate, out_up, out_out, kv_out, dattn_t,
-    x, dy, held, do, q, k, v, cos, sin, wo, w, d, dk, dv, part, landed, fold, flip, stage, kv_stage,
+    x, dy, total_gains, line_gains, dp_gains, held, do, q, k, v, cos, sin, wo, w, d, dk, dv, part, landed, fold, flip, stage, kv_stage,
     load, do_load, ag_send, ag_recv, rs_send, rs_recv, flip_sem, out_sem, last_sem, kv_sem, kv_send,
-    kv_recv, *reduce_refs,
+    kv_recv, gain_send, gain_recv, *reduce_refs,
 ):
     i = lax.axis_index("tensor")
     rows, width = x.shape
@@ -1710,16 +1757,19 @@
         for u, (name, column, size) in enumerate(units_of)
     ]
     count = len(units)
-    units[0].load()
+    for a, b in zip(units, units[1:]):
+        a.next = b
+    units[0].load(True)
     me = units[0].me
 
     barrier = pltpu.get_barrier_semaphore()
-    for shift in (units[0].dc, units[0].dx, units[0].dy):
-        pl.semaphore_signal(barrier, 1, device_id={"dp": me + shift}, device_id_type=MESH)
+    for j in range(1, m):
+        peer = lax.rem(me + j, m)
+        pl.semaphore_signal(barrier, 1, device_id={"dp": peer}, device_id_type=MESH)
     for j in range(1, n):
         peer = lax.rem(i + j, n)
         pl.semaphore_signal(barrier, 1, device_id={"tensor": peer}, device_id_type=MESH)
-    pl.semaphore_wait(barrier, n + 2)
+    pl.semaphore_wait(barrier, m + n - 2)
 
 
     pass_on, sent = gather_steps(i, n, held, ag_send, ag_recv)
@@ -1728,10 +1778,11 @@
         block = block_at(i, n, s)
         at = pl.ds(pl.multiple_of(block * rows + piece, piece), piece)
         do[at, :] = dot_nn(held[block], wo[...]).astype(BF16)
-        flip_rows(held.at[block], dattn_t, block * rows + piece, flip, flip_sem)
+        flip_rows(held.at[block], dattn_t, block * rows + piece, flip, flip_sem, s == 0)
 
     def attention():
         use(n - 1)
+        flip_end(dattn_t, flip, flip_sem)
         sent()
         for c in half_loads + loads[2:7]:
             c.wait()
@@ -1769,9 +1820,44 @@
             fold[...] += fold_rows(dh1 * (a * inv))
 
         loop(rows // strip, chunk)
-        gain_out[...] = jnp.sum(fold[...], axis=0, keepdims=True)
+        total_gains[0:1, :] = jnp.sum(fold[...], axis=0, keepdims=True)
+        total_gains[1:4, :] = later_gains[...]
+        for j in range(1, n):
+            gain_copy(0, j).start()
         pltpu.make_async_copy(x, in_grad, last_sem.at[0]).start()
         done()
+
+
+    def gain_copy(way, j):
+        peer = {"dp": lax.rem(me + j, m)} if way else {"tensor": lax.rem(i + j, n)}
+        return pltpu.make_async_remote_copy(
+            gain_out if way else total_gains,
+            (dp_gains if way else line_gains).at[j - 1],
+            gain_send.at[way, j],
+            gain_recv.at[way, j],
+            device_id=peer,
+            device_id_type=MESH,
+        )
+
+    def gains_over_line():
+        total = total_gains[...]
+        for j in range(1, n):
+            gain_copy(0, j).wait_recv()
+            total += line_gains[j - 1]
+        gain_out[...] = total
+        for j in range(1, m):
+            gain_copy(1, j).start()
+
+    def gains_over_dp():
+        total = gain_out[...]
+        for j in range(1, m):
+            gain_copy(1, j).wait_recv()
+            total += dp_gains[j - 1]
+        for j in range(1, n):
+            gain_copy(0, j).wait_send()
+        for j in range(1, m):
+            gain_copy(1, j).wait_send()
+        gain_out[...] = total
 
 
     def out_copy(u):
@@ -1813,10 +1899,11 @@
         use(s - 1)
 
     line = [[functools.partial(passing, s)] for s in range(1, n)]
-    line[-1] += [attention, begin_line]
+    line[-1] += [attention]
+    line += [[begin_line]]
     for t in range(1, n - 1):
-        line += [[], [functools.partial(step, t)]]
-    line += [[lambda: compute(n - 1, i)], [input_grad]]
+        line += [[], [], [functools.partial(step, t)]]
+    line += [[lambda: compute(n - 1, i), input_grad], [gains_over_line], [], [gains_over_dp]]
 
     loads[0].wait()
     loads[1].wait()
@@ -1829,10 +1916,10 @@
             units[u].middle()
         if 1 <= u <= count:
             units[u - 1].turn()
+        for action in line[u] if u < len(line) else ():
+            action()
         if 2 <= u < count + 2:
             finish(u - 2)
-        for action in line[u] if u < len(line) else ():
-            action()
     for u in range(max(0, count - 2), count):
         out_copy(u).wait()
     pltpu.make_async_copy(x, in_grad, last_sem.at[0]).wait()
@@ -1848,7 +1935,9 @@
     return [(name, k * (width // count), width // count) for k in range(count)]
 
 
-def finish(n, m, heads, kvs, starts, x, dy, gains, own, do, q, k, v, cos, sin, wo, w, turned, rights, o):
+def finish(
+    n, m, heads, kvs, starts, x, dy, gains, own, do, q, k, v, cos, sin, wo, w, turned, rights, o, later
+):
     rows, width = x.shape
     tokens = n * rows
     own_rows = width // m
@@ -1862,15 +1951,18 @@
     sem = pltpu.SemaphoreType.DMA
     shape = lambda a, b, t=F32: jax.ShapeDtypeStruct((a, b), t)
     return pl.pallas_call(
-        functools.partial(finish_kernel, n, heads, kvs, units),
-        out_shape=[shape(rows, width, BF16), shape(1, width), shape(own_rows, across)]
+        functools.partial(finish_kernel, n, m, heads, kvs, units),
+        out_shape=[shape(rows, width, BF16), shape(4, width), shape(own_rows, across)]
         + [shape(own_rows, r.shape[1]) for r in (*rights, o)]
         + [jax.ShapeDtypeStruct((n, own_rows, across - split), BF16), shape(width, tokens, BF16)],
-        in_specs=[SM, ANY, ANY, VM] + [ANY] * 17,
+        in_specs=[SM, ANY, ANY, VM] + [ANY] * 17 + [VM],
         out_specs=[ANY, VM] + [ANY] * 7,
         scratch_shapes=[
             pltpu.VMEM(x.shape, BF16),
             pltpu.VMEM(x.shape, F32),
+            pltpu.VMEM((4, width), F32),
+            pltpu.VMEM((n - 1, 4, width), F32),
+            pltpu.VMEM((m - 1, 4, width), F32),
             pltpu.VMEM((n, rows // 2, width), BF16),
             pltpu.VMEM((tokens, split), BF16),
             pltpu.VMEM(q.shape, BF16),
@@ -1892,7 +1984,7 @@
             sem((10,)), sem((n,)),
         ]
         + line_scratch(n) * 2
-        + [sem((2,)), sem((2,)), sem((1,)), sem((1,)), sem((n,)), sem((n,))]
+        + [sem((2,)), sem((2,)), sem((1,)), sem((1,)), sem((n,)), sem((n,)), sem((2, m)), sem((2, m))]
         + bufs
         + sems,
         input_output_aliases={13: 8},
@@ -1901,7 +1993,7 @@
         ),
         cost_estimate=cost(0, 600 << 20),
         name="finish",
-    )(starts, x, dy, gains, own, do, q, k, v, cos, sin, wo, w, turned[3], *turned[:3], *rights, o)
+    )(starts, x, dy, gains, own, do, q, k, v, cos, sin, wo, w, turned[3], *turned[:3], *rights, o, later)
 
 
 def deliver_kernel(count, *refs):
@@ -1961,10 +2053,11 @@
 
 
 def rope_tables():
-    positions = jnp.arange(L, dtype=jnp.int32).astype(F32)
-    exponent = jnp.arange(HD // 2, dtype=jnp.int32).astype(F32) * (-2.0 / HD)
-    angles = positions[:, None] * jnp.exp(exponent * jnp.log(F32(10000.0)))[None, :]
-    return jnp.cos(angles), jnp.sin(angles)
+    positions = np.arange(L, dtype=np.float32)
+    exponent = np.arange(HD // 2, dtype=np.float32) * np.float32(-2.0 / HD)
+    angles = positions[:, None] * np.exp(exponent * np.log(np.float32(10000.0)))[None, :]
+    angles = angles.astype(np.float64)
+    return jnp.asarray(np.cos(angles), F32), jnp.asarray(np.sin(angles), F32)
 
 
 def weight_grad(left, right):
@@ -2038,9 +2131,9 @@
     flat = lambda a: a.reshape(tokens, a.shape[-1])
     split = heads * HD
     if spread:
-        in_grad, gain_one, qkv_sum, down_sum, gate_sum, up_sum, out_sum, kv, _ = finish(
+        in_grad, gain_grads, qkv_sum, down_sum, gate_sum, up_sum, out_sum, kv, _ = finish(
             n, m, heads, kvs, piece_starts, layer_in, dy, gains, own, do, q, k, v, cos, sin, wo, wqkv,
-            (h1_t, df_t, h3_t, dattn_t), (flat(hid), flat(dgate), flat(dup)), o,
+            (h1_t, df_t, h3_t, dattn_t), (flat(hid), flat(dgate), flat(dup)), o, gain_later,
         )
     else:
         tie = lax.optimization_barrier
@@ -2067,8 +2160,12 @@
         else:
             kv = lax.dynamic_update_slice_in_dim(jnp.zeros((2, own_rows, KV * HD), BF16), kv, kv_at, 2)
             kv = lax.psum(kv, "tensor")
-    gain_grads = jnp.concatenate([gain_one, gain_later], axis=0)
-    gain_grads = sum_gains(n, m, gain_grads.reshape(4, m, width // m).transpose(1, 0, 2))
+    if spread:
+        own_at = lax.axis_index("dp") * (width // m)
+        gain_grads = lax.dynamic_slice_in_dim(gain_grads, own_at, width // m, 1)
+    else:
+        gain_grads = jnp.concatenate([gain_one, gain_later], axis=0)
+        gain_grads = sum_gains(n, m, gain_grads.reshape(4, m, width // m).transpose(1, 0, 2))
     if spread:
         layer_out, in_grad, down_sum, gate_sum, up_sum, out_sum, q_sum, k_sum, v_sum = deliver(
             split, (layer_out, in_grad, down_sum, gate_sum, up_sum, out_sum), qkv_sum, kv

time: 688 us -> 667 us (0.969)
  Pallas kernels: 650 us -> 635 us
    pallas_call x2 -> x1, Pallas kernels: 215 us -> 197 us  [finish(): pl.pallas_call(functools.partial(finish_kernel, n, m, heads, kvs, units),...]
where the time goes in v5:
time: 667 us; the launch traced here: 655 us
  Pallas kernels  635 us (95%)
  between operations  14.4 us (2%)
    pallas_call x1, Pallas kernels, middle(): pl.pallas_call(functools.partial(middle_kernel, n), out_shape=[jax.ShapeD...  321 us
    pallas_call x1, Pallas kernels, finish(): pl.pallas_call(functools.partial(finish_kernel, n, m, heads, kvs, units),...  197 us
    pallas_call x1, Pallas kernels, first(): pl.pallas_call(functools.partial(first_kernel, n, spread), out_shape=outs...  87.2 us
    pallas_call x1, Pallas kernels, attend(): pl.pallas_call(functools.partial(attend_kernel, heads, kvs), out_shape=[j...  14.2 us
  transfers between devices with their start and end apart: 2, of which 0 were waited for; matrix products, arithmetic and copies ran while one was open for 0% of the time, Pallas kernels for 16%

profile of v5, /device:TPU:0, one launch (start us, length us, event | category | flops | bytes accessed | tf_op | source)
XLA Modules:
  0.0 655.5 jit_solution(14419527173349789890)
XLA Ops:
  7.2 0.0 copy-start
  7.2 0.0 copy-start.1
  7.2 0.0 copy-start.2
  7.2 0.0 copy-start.3
  7.2 0.0 all-gather.3.cloned.1.call-start
  7.3 1.0 constant_dynamic-slice_fusion
  8.3 1.9 pad_maximum_fusion
  10.2 0.0 all-gather.3.cloned.1.call-update
  10.2 0.0 all-gather.5.cloned.1.call-start
  10.2 0.7 all-gather.5.cloned.1.call-update
  10.9 0.0 copy-done
  11.0 0.0 copy-done.1
  11.0 0.0 copy-done.2
  11.0 0.0 copy-done.3
  11.0 6.3 gains.1
  17.4 0.7 reshape.49.gains
  18.1 87.2 %first.1 = (bf16[4,256,2304]{2,1,0:T(8,128)(2,1)}, bf16[2304,2304]{1,0:T(8,128)(2,1)}, bf16[2304,1024]{1,0:T(8,128)(2,1)}) custom-call(bf16[256,2304]{1,0:T(8,128)(2,1)} %x_hbm.3, f32[4,2304]{1,0:T(4,128)} %reshape.49.gains, bf16[288,2304]{1,0:T(8,128)(2,1)} %refs_0_.1), custom_call_target="tpu_custom_call" | custom-call | bytes 314572800 | tf_op jit(solution)/shard_map/first/pallas_call | solution.py:584
  105.3 0.0 all-gather.3.cloned.1.call-done.w_hbm
  105.3 14.2 %attend.1 = (bf16[2,1024,256]{2,1,0:T(8,128)(2,1)}, bf16[1,1024,256]{2,1,0:T(8,128)(2,1)}, bf16[1,1024,256]{2,1,0:T(8,128)(2,1)}, bf16[1024,512]{1,0:T(8,128)(2,1)}) custom-call(s32[1,2]{1,0:T(1,128)} %starts.3, bf16[1024,2304]{1,0:T(8,128)(2,1)} %bitcast.17, bf16[2304,1024]{1,0:T(8,128)(2,1)} %all-gather.3.cloned.1.call-done.w_hbm, ...), custom_call_target="tpu_custom_call" | custom-call | flops 21474836480 | bytes 20971520 | tf_op jit(solution)/shard_map/attend/pallas_call | solution.py:694
  119.6 0.0 all-gather.5.cloned.1.call-done.wo_hbm
  119.6 321.2 %middle.1 = (bf16[256,2304]{1,0:T(8,128)(2,1)}, f32[256,2304]{1,0:T(8,128)}, f32[3,2304]{1,0:T(4,128)}, bf16[2304,1024]{1,0:T(8,128)(2,1)}, bf16[4,256,2304]{2,1...) custom-call(bf16[256,2304]{1,0:T(8,128)(2,1)} %x_hbm.3, ...), custom_call_target="tpu_custom_call" | custom-call | bytes 1258291200 | tf_op jit(solution)/shard_map/middle/pallas_call | solution.py:1427
  440.8 197.1 %finish.1 = (bf16[256,2304]{1,0:T(8,128)(2,1)}, f32[4,2304]{1,0:T(4,128)}, f32[288,1024]{1,0:T(8,128)}, f32[288,2304]{1,0:T(8,128)}, f32[288,2304]{1,0:T(8,128)}...) custom-call(s32[1,2]{1,0:T(1,128)} %starts.3, ...), custom_call_target="tpu_custom_call", output_to_operand_aliasing={{8}: (13, {})} | custom-call | bytes 629145600 | tf_op jit(solution)/shard_map/finish/pallas_call | solution.py:1953
  637.9 1.5 dynamic-slice_reduce_fusion
  639.4 9.0 %deliver.1 = (bf16[256,2304]{1,0:T(8,128)(2,1)}, bf16[256,2304]{1,0:T(8,128)(2,1)}, f32[288,2304]{1,0:T(8,128)}, f32[288,2304]{1,0:T(8,128)}, f32[288,2304]{1,0:...) custom-call(bf16[256,2304]{1,0:T(8,128)(2,1)} %get-tuple-element.51.refs_0_, ...), custom_call_target="tpu_custom_call" | custom-call | bytes 41943040 | tf_op jit(solution)/shard_map/deliver/pallas_call | solution.py:2035
  (7 shorter events, 0.0 us)
Async XLA Ops:
  7.2 3.8 copy-start
  7.2 3.8 copy-start.1
  7.2 3.8 copy-start.2
  7.2 3.8 copy-start.3
  7.2 98.1 %all-gather.3.cloned.1.call-start = ((), (), s32[]{:S(2)}) async-start(), calls=%async_computation | async-start | bytes 5308416 | tf_op jit(solution)/shard_map/all_gather | solution.py:2101
  10.2 109.4 %all-gather.5.cloned.1.call-start = ((), (), s32[]{:S(2)}) async-start(), calls=%async_computation.1 | async-start | bytes 2654208 | tf_op jit(solution)/shard_map/all_gather | solution.py:2101
Sparse Core Ops, SparseCore 0:
  10.5 60.6 all-gather.2
  73.1 31.9 all-gather.4

commit v6 on v5

--- a/solution.py
+++ b/solution.py
@@ -1786,7 +1786,7 @@
         sent()
         for c in half_loads + loads[2:7]:
             c.wait()
-        attend_back_kernel(heads, kvs, 128, starts, q, k, v, do, cos, sin, d, dk, dv)
+        attend_back_kernel(heads, kvs, 256, starts, q, k, v, do, cos, sin, d, dk, dv)
 
 
     def compute(t, block):

time: 667 us -> 663 us (level)
  transfers between devices with their start and end apart: 2 -> 2, of which waited for: 0 -> 0; matrix products, arithmetic and copies ran while one was open for 0% -> 0% of each run, Pallas kernels for 16% -> 17%
where the time goes in v6:
time: 663 us; the launch traced here: 652 us
  Pallas kernels  631 us (95%)
  between operations  14.8 us (2%)
    pallas_call x1, Pallas kernels, middle(): pl.pallas_call(functools.partial(middle_kernel, n), out_shape=[jax.ShapeD...  321 us
    pallas_call x1, Pallas kernels, finish(): pl.pallas_call(functools.partial(finish_kernel, n, m, heads, kvs, units),...  193 us
    pallas_call x1, Pallas kernels, first(): pl.pallas_call(functools.partial(first_kernel, n, spread), out_shape=outs...  87.2 us
    pallas_call x1, Pallas kernels, attend(): pl.pallas_call(functools.partial(attend_kernel, heads, kvs), out_shape=[j...  14.2 us
  transfers between devices with their start and end apart: 2, of which 0 were waited for; matrix products, arithmetic and copies ran while one was open for 0% of the time, Pallas kernels for 17%

profile of v6, /device:TPU:0, one launch (start us, length us, event | category | flops | bytes accessed | tf_op | source)
XLA Modules:
  0.0 651.6 jit_solution(16831343684148142738)
XLA Ops:
  7.2 0.0 copy-start
  7.2 0.0 copy-start.1
  7.2 0.0 copy-start.2
  7.2 0.0 copy-start.3
  7.2 0.0 all-gather.3.cloned.1.call-start
  7.3 1.0 constant_dynamic-slice_fusion
  8.3 1.9 pad_maximum_fusion
  10.2 0.0 all-gather.3.cloned.1.call-update
  10.2 0.0 all-gather.5.cloned.1.call-start
  10.2 0.7 all-gather.5.cloned.1.call-update
  10.9 0.0 copy-done
  11.0 0.0 copy-done.1
  11.0 0.0 copy-done.2
  11.0 0.0 copy-done.3
  11.0 6.3 gains.1
  17.4 0.7 reshape.49.gains
  18.1 87.2 %first.1 = (bf16[4,256,2304]{2,1,0:T(8,128)(2,1)}, bf16[2304,2304]{1,0:T(8,128)(2,1)}, bf16[2304,1024]{1,0:T(8,128)(2,1)}) custom-call(bf16[256,2304]{1,0:T(8,128)(2,1)} %x_hbm.3, f32[4,2304]{1,0:T(4,128)} %reshape.49.gains, bf16[288,2304]{1,0:T(8,128)(2,1)} %refs_0_.1), custom_call_target="tpu_custom_call" | custom-call | bytes 314572800 | tf_op jit(solution)/shard_map/first/pallas_call | solution.py:584
  105.3 0.0 all-gather.3.cloned.1.call-done.w_hbm
  105.3 14.2 %attend.1 = (bf16[2,1024,256]{2,1,0:T(8,128)(2,1)}, bf16[1,1024,256]{2,1,0:T(8,128)(2,1)}, bf16[1,1024,256]{2,1,0:T(8,128)(2,1)}, bf16[1024,512]{1,0:T(8,128)(2,1)}) custom-call(s32[1,2]{1,0:T(1,128)} %starts.3, bf16[1024,2304]{1,0:T(8,128)(2,1)} %bitcast.17, bf16[2304,1024]{1,0:T(8,128)(2,1)} %all-gather.3.cloned.1.call-done.w_hbm, ...), custom_call_target="tpu_custom_call" | custom-call | flops 21474836480 | bytes 20971520 | tf_op jit(solution)/shard_map/attend/pallas_call | solution.py:694
  119.6 0.0 all-gather.5.cloned.1.call-done.wo_hbm
  119.6 320.9 %middle.1 = (bf16[256,2304]{1,0:T(8,128)(2,1)}, f32[256,2304]{1,0:T(8,128)}, f32[3,2304]{1,0:T(4,128)}, bf16[2304,1024]{1,0:T(8,128)(2,1)}, bf16[4,256,2304]{2,1...) custom-call(bf16[256,2304]{1,0:T(8,128)(2,1)} %x_hbm.3, ...), custom_call_target="tpu_custom_call" | custom-call | bytes 1258291200 | tf_op jit(solution)/shard_map/middle/pallas_call | solution.py:1427
  440.5 193.1 %finish.1 = (bf16[256,2304]{1,0:T(8,128)(2,1)}, f32[4,2304]{1,0:T(4,128)}, f32[288,1024]{1,0:T(8,128)}, f32[288,2304]{1,0:T(8,128)}, f32[288,2304]{1,0:T(8,128)}...) custom-call(s32[1,2]{1,0:T(1,128)} %starts.3, ...), custom_call_target="tpu_custom_call", output_to_operand_aliasing={{8}: (13, {})} | custom-call | bytes 629145600 | tf_op jit(solution)/shard_map/finish/pallas_call | solution.py:1953
  633.6 1.5 dynamic-slice_reduce_fusion
  635.2 9.0 %deliver.1 = (bf16[256,2304]{1,0:T(8,128)(2,1)}, bf16[256,2304]{1,0:T(8,128)(2,1)}, f32[288,2304]{1,0:T(8,128)}, f32[288,2304]{1,0:T(8,128)}, f32[288,2304]{1,0:...) custom-call(bf16[256,2304]{1,0:T(8,128)(2,1)} %get-tuple-element.51.refs_0_, ...), custom_call_target="tpu_custom_call" | custom-call | bytes 41943040 | tf_op jit(solution)/shard_map/deliver/pallas_call | solution.py:2035
  (7 shorter events, 0.0 us)
Async XLA Ops:
  7.2 3.8 copy-start
  7.2 3.8 copy-start.1
  7.2 3.8 copy-start.2
  7.2 3.8 copy-start.3
  7.2 98.1 %all-gather.3.cloned.1.call-start = ((), (), s32[]{:S(2)}) async-start(), calls=%async_computation | async-start | bytes 5308416 | tf_op jit(solution)/shard_map/all_gather | solution.py:2101
  10.2 109.4 %all-gather.5.cloned.1.call-start = ((), (), s32[]{:S(2)}) async-start(), calls=%async_computation.1 | async-start | bytes 2654208 | tf_op jit(solution)/shard_map/all_gather | solution.py:2101
Sparse Core Ops, SparseCore 0:
  10.5 60.6 all-gather.2
  73.1 31.9 all-gather.4
